TPU v7x, 32 devices: a whole 2x2x4 slice. The times are simulated.
32 devices in a mesh: dp: 2 (over x), head: 4 (over z), frame: 4 (over y, core).
Axes of the slice: x: 2, y: 2, z: 4, core: 2. Of those that a mesh axis runs over, the one named last changes fastest.
Arguments:
- queries: bfloat16 [2048, 5120], P(('dp', 'frame', 'head')), parts along dimension 0, may hold values from -5 to 5
- keys: bfloat16 [2048, 5120], P(('dp', 'frame', 'head')), parts along dimension 0, may hold values from -5 to 5
- values: bfloat16 [2048, 5120], P(('dp', 'frame', 'head')), parts along dimension 0, may hold values from -6 to 6
- out_grad: bfloat16 [2048, 5120], P(('dp', 'frame', 'head')), parts along dimension 0, may hold values from -6 to 6
- tile_mask: int32 [40, 8, 8], P('head'), may hold values from 0 to 1, as said below
Outputs:
- attended: bfloat16 [2048, 5120], P(('dp', 'frame'), 'head'), parts along dimension 0
- query_grad: bfloat16 [2048, 5120], P(('dp', 'frame'), 'head'), parts along dimension 0
- key_grad: bfloat16 [2048, 5120], P(('dp', 'frame'), 'head'), parts along dimension 0
- value_grad: bfloat16 [2048, 5120], P(('dp', 'frame'), 'head'), parts along dimension 0
There are 2 independent parts, one for each index of `dp`. A program takes and returns all parts, laid end to end along the dimension named above; an argument that names none is the same for every part. Nothing has to cross between parts.
Inputs may be any that keep to these rules, and one draw needn't show every extreme that they name: tile_mask[h, i, i] = 1 for every head h and tile i.
All inputs are finite; a program needn't handle non-finite values.
Results may differ from a plain program's by a relative error of at most 0.022.
Values may be sent and summed in bfloat16 or wider, within the bound.
No kernel may reach another device: no remote copies, remote signals or barrier semaphores. Data moves between devices by JAX's collectives and lax.ppermute only.
A program may use at most 128 MiB of HBM per device.

v0:
```python
import math

import jax
import jax.numpy as jnp
from jax import lax
from jax.sharding import PartitionSpec as P

HD = 128
TILE = 128


EXCLUDED = -1e30


def expand_tiles(live_block, tile_size):
    head_count, query_tiles, key_tiles = live_block.shape
    spread = jnp.broadcast_to(
        live_block[:, :, None, :, None] == 1,
        (head_count, query_tiles, tile_size, key_tiles, tile_size),
    )
    return spread.reshape(head_count, query_tiles * tile_size, key_tiles * tile_size)


def local(queries, keys, values, out_grad, tile_mask):
    frame_index = lax.axis_index("frame")
    frame_count = lax.axis_size("frame")
    query_rows, key_rows, value_rows, grad_rows = (
        lax.all_to_all(queries, "head", split_axis=1, concat_axis=0, tiled=True),
        lax.all_to_all(keys, "head", split_axis=1, concat_axis=0, tiled=True),
        lax.all_to_all(values, "head", split_axis=1, concat_axis=0, tiled=True),
        lax.all_to_all(out_grad, "head", split_axis=1, concat_axis=0, tiled=True),
    )
    slab_rows = query_rows.shape[0]
    groups = query_rows.shape[1] // HD
    token_count = slab_rows * frame_count
    scaling = 1.0 / math.sqrt(HD)
    query_heads = query_rows.reshape(slab_rows, groups, HD)
    grad_heads = grad_rows.reshape(slab_rows, groups, HD)
    query_tiles = slab_rows // TILE
    mask_rows = lax.dynamic_slice_in_dim(tile_mask, frame_index * query_tiles, query_tiles, 1)

    def blocked(step, initial, piece):
        piece_rows = piece[0].shape[0]
        block_width = slab_rows * math.gcd(piece_rows // slab_rows, 4)

        def one_block(block_index, running_state):
            offset = block_index * block_width
            key_block = lax.dynamic_slice_in_dim(piece[0], offset, block_width, 0).reshape(
                block_width, groups, HD
            )
            value_block = lax.dynamic_slice_in_dim(piece[1], offset, block_width, 0).reshape(
                block_width, groups, HD
            )
            live_block = lax.dynamic_slice_in_dim(mask_rows, offset // TILE, block_width // TILE, 2)
            return step(running_state, key_block, value_block, live_block, offset, 0, groups)

        return lax.fori_loop(0, piece_rows // block_width, one_block, initial)

    def forward_step(
        running_state, key_block, value_block, live_block, block_start, head_lo, head_hi
    ):
        running, totals, summed = running_state
        allowed = expand_tiles(live_block, TILE)
        scores = (
            jnp.einsum("qhd,khd->hqk", query_heads, key_block, preferred_element_type=jnp.float32)
            * scaling
        )
        masked = jnp.where(allowed, scores, EXCLUDED)
        new_running = jnp.maximum(running, jnp.max(masked, axis=2))
        weights = jnp.where(allowed, jnp.exp(masked - new_running[:, :, None]), 0.0)
        factor = jnp.exp(running - new_running)
        new_totals = totals * factor + jnp.sum(weights, axis=2)
        update = jnp.einsum(
            "hqk,khd->qhd",
            weights.astype(jnp.bfloat16),
            value_block,
            preferred_element_type=jnp.float32,
        )
        new_summed = summed * factor.T[:, :, None] + update
        return (
            running.at[head_lo:head_hi].set(new_running),
            totals.at[head_lo:head_hi].set(new_totals),
            summed.at[:, head_lo:head_hi].set(new_summed),
        )

    initial_forward = (
        jnp.full((groups, slab_rows), EXCLUDED, jnp.float32),
        jnp.zeros((groups, slab_rows), jnp.float32),
        jnp.zeros((slab_rows, groups, HD), jnp.float32),
    )
    running, totals, summed = blocked(
        forward_step,
        initial_forward,
        (
            lax.all_gather(key_rows, "frame", axis=0, tiled=True),
            lax.all_gather(value_rows, "frame", axis=0, tiled=True),
        ),
    )
    attended = (summed / totals.T[:, :, None]).astype(jnp.bfloat16)
    logsum = running + jnp.log(totals)
    out_delta = jnp.sum(grad_heads.astype(jnp.float32) * attended.astype(jnp.float32), axis=2).T

    def backward_step(
        running_state, key_block, value_block, live_block, block_start, head_lo, head_hi
    ):
        query_acc, key_acc, value_acc = running_state
        block_width = key_block.shape[0]
        head_count = head_hi - head_lo
        allowed = expand_tiles(live_block, TILE)
        scores = (
            jnp.einsum("qhd,khd->hqk", query_heads, key_block, preferred_element_type=jnp.float32)
            * scaling
        )
        masked = jnp.where(allowed, scores, EXCLUDED)
        probabilities = jnp.where(allowed, jnp.exp(masked - logsum[head_lo:head_hi, :, None]), 0.0)
        prob_grad = jnp.einsum(
            "qhd,khd->hqk", grad_heads, value_block, preferred_element_type=jnp.float32
        )
        score_grad = probabilities * (prob_grad - out_delta[head_lo:head_hi, :, None])
        probs_half = probabilities.astype(jnp.bfloat16)
        score_half = score_grad.astype(jnp.bfloat16)
        value_part = jnp.einsum(
            "hqk,qhd->khd", probs_half, grad_heads, preferred_element_type=jnp.float32
        )
        key_part = (
            jnp.einsum("hqk,qhd->khd", score_half, query_heads, preferred_element_type=jnp.float32)
            * scaling
        )
        query_new = query_acc + jnp.einsum(
            "hqk,khd->qhd", score_half, key_block, preferred_element_type=jnp.float32
        )
        query_acc = query_acc.at[:, head_lo:head_hi].set(query_new)
        key_acc = lax.dynamic_update_slice(
            key_acc, key_part.reshape(block_width, head_count * HD), (block_start, head_lo * HD)
        )
        value_acc = lax.dynamic_update_slice(
            value_acc, value_part.reshape(block_width, head_count * HD), (block_start, head_lo * HD)
        )
        return (query_acc, key_acc, value_acc)

    initial_backward = (
        jnp.zeros((slab_rows, groups, HD), jnp.float32),
        jnp.zeros((token_count, groups * HD), jnp.float32),
        jnp.zeros((token_count, groups * HD), jnp.float32),
    )
    query_acc, key_acc, value_acc = blocked(
        backward_step,
        initial_backward,
        (
            lax.all_gather(key_rows, "frame", axis=0, tiled=True),
            lax.all_gather(value_rows, "frame", axis=0, tiled=True),
        ),
    )
    key_sum, value_sum = (
        lax.psum_scatter(
            key_acc.astype(jnp.bfloat16), "frame", scatter_dimension=0, tiled=True
        ).astype(jnp.float32),
        lax.psum_scatter(
            value_acc.astype(jnp.bfloat16), "frame", scatter_dimension=0, tiled=True
        ).astype(jnp.float32),
    )
    attended_out = attended.reshape(slab_rows, groups * HD)
    query_out = (query_acc * scaling).astype(jnp.bfloat16).reshape(slab_rows, groups * HD)
    return (attended_out, query_out, key_sum.astype(jnp.bfloat16), value_sum.astype(jnp.bfloat16))


def solution(mesh):
    return jax.shard_map(
        local,
        mesh=mesh,
        in_specs=(
            P(("dp", "frame", "head"), None),
            P(("dp", "frame", "head"), None),
            P(("dp", "frame", "head"), None),
            P(("dp", "frame", "head"), None),
            P("head", None, None),
        ),
        out_specs=(
            P(("dp", "frame"), "head"),
            P(("dp", "frame"), "head"),
            P(("dp", "frame"), "head"),
            P(("dp", "frame"), "head"),
        ),
        check_vma=False,
    )
```

profile of v0, /device:TPU:0, one launch (start us, length us, event | category | flops | bytes accessed | tf_op | source)
XLA Modules:
  0.0 200.4 jit_solution(17691626571015534409)
XLA Ops:
  8.5 23.5 %all_to_all.70 = bf16[64,4,1280]{2,0,1:T(8,128)(2,1)} all-to-all(bf16[64,4,1280]{2,0,1:T(8,128)(2,1)S(1)} %bitcast.72), channel_id=1, replica_groups=mesh['dp'=2,'head'=4,'frame'=4] {'head'}, dimensions={1} | all-to-all | bytes 1310720 | tf_op jit(solution)/shard_map/all_to_all | solution.py:29
  32.0 2.0 copy.83
  34.0 3.5 %all-to-all-start.2 = ((bf16[64,4,1280]{2,0,1:T(8,128)(2,1)}), bf16[64,4,1280]{2,0,1:T(8,128)(2,1)S(1)}, u32[]{:S(2)}, u32[]{:S(2)}) async-start(bf16[64,4,1280]{2,0,1:T(8,128)(2,1)} %bitcast.58), calls=%async_computation.2 | async-start | bytes 1310720 | tf_op jit(solution)/shard_map/all_to_all | solution.py:30
  38.4 15.5 %all-to-all-done.2 = bf16[64,4,1280]{2,0,1:T(8,128)(2,1)S(1)} async-done(((bf16[64,4,1280]{2,0,1:T(8,128)(2,1)}), bf16[64,4,1280]{2,0,1:T(8,128)(2,1)S(1)}, u32[]{:S(2)}, u32[]{:S(2)}) %all-to-all-start.2) | async-done | bytes 655392 | tf_op jit(solution)/shard_map/all_to_all | solution.py:30
  53.9 3.5 %all-to-all-start = ((bf16[64,4,1280]{2,0,1:T(8,128)(2,1)}), bf16[64,4,1280]{2,0,1:T(8,128)(2,1)S(1)}, u32[]{:S(2)}, u32[]{:S(2)}) async-start(bf16[64,4,1280]{2,0,1:T(8,128)(2,1)} %bitcast.60), calls=%async_computation | async-start | bytes 1310720 | tf_op jit(solution)/shard_map/all_to_all | solution.py:28
  59.0 15.1 %all-to-all-done = bf16[64,4,1280]{2,0,1:T(8,128)(2,1)S(1)} async-done(((bf16[64,4,1280]{2,0,1:T(8,128)(2,1)}), bf16[64,4,1280]{2,0,1:T(8,128)(2,1)S(1)}, u32[]{:S(2)}, u32[]{:S(2)}) %all-to-all-start) | async-done | bytes 655392 | tf_op jit(solution)/shard_map/all_to_all | solution.py:28
  74.1 4.2 %all-to-all-start.3 = ((bf16[64,4,1280]{2,0,1:T(8,128)(2,1)}), bf16[64,4,1280]{2,0,1:T(8,128)(2,1)}, u32[]{:S(2)}, u32[]{:S(2)}) async-start(bf16[64,4,1280]{2,0,1:T(8,128)(2,1)} %bitcast.57), calls=%async_computation.3 | async-start | bytes 1310720 | tf_op jit(solution)/shard_map/all_to_all | solution.py:31
  79.2 2.3 %broadcast_in_dim.45 = pred[10,2,128,8,128]{4,3,2,1,0:T(8,128)(4,1)} broadcast(pred[10,2,8]{2,1,0:T(4,128)(4,1)S(1)} %copy.54), dimensions={0,1,3} | broadcast | bytes 2621600 | tf_op jit(solution)/shard_map/while/body/eval_jaxpr/broadcast_in_dim | solution.py:17
  81.5 6.5 %reshape.198 = pred[10,256,1024]{2,1,0:T(32,128)(4,1)S(1)} reshape(pred[10,2,128,8,128]{4,3,2,1,0:T(8,128)(4,1)} %broadcast_in_dim.45) | data formatting | bytes 5242880 | tf_op jit(solution)/shard_map/while/body/eval_jaxpr/reshape | solution.py:21
  91.4 3.8 %all-to-all-done.3 = bf16[64,4,1280]{2,0,1:T(8,128)(2,1)} async-done(((bf16[64,4,1280]{2,0,1:T(8,128)(2,1)}), bf16[64,4,1280]{2,0,1:T(8,128)(2,1)}, u32[]{:S(2)}, u32[]{:S(2)}) %all-to-all-start.3) | async-done | bytes 655392 | tf_op jit(solution)/shard_map/all_to_all | solution.py:31
  95.1 2.2 %reshape.202 = bf16[256,10,128]{2,1,0:T(8,128)(2,1)} reshape(bf16[4,64,1280]{2,1,0:T(8,128)(2,1)} %bitcast.11) | data formatting | bytes 1310720 | tf_op jit(solution)/shard_map/reshape | solution.py:38
  97.4 2.4 %copy.65 = bf16[256,10,128]{0,2,1:T(8,128)(2,1)} copy(bf16[256,10,128]{2,1,0:T(8,128)(2,1)} %reshape.202) | data formatting | bytes 1310720 | tf_op jit(solution)/shard_map/reshape | solution.py:38
  99.8 4.5 %copy.57 = bf16[1024,1280]{0,1:T(8,128)(2,1)} copy(bf16[1024,1280]{1,0:T(8,128)(2,1)} %all-gather.3.cloned.1.call-done) | data formatting | bytes 5242880 | tf_op jit(solution)/shard_map/all_gather | solution.py:95
  104.2 4.4 %fusion = (f32[10,256]{1,0:T(8,128)S(1)}, f32[10,256,1024]{2,1,0:T(8,128)S(1)}) fusion(pred[10,256,1024]{2,1,0:T(32,128)(4,1)S(1)} %reshape.198, bf16[256,10,128]{0,2,1:T(8,128)(2,1)S(1)} %copy.66, bf16[1024,10,128]{0,2,1:T(8,128)(2,1)} %bitcast.63), kind=kOutput, calls=%fused_computation.4 | convolution fusion | flops 678950400 | bytes 16394240 | tf_op jit(solution)/shard_map/while/body/eval_jaxpr/qhd,khd->hqk/dot_general | solution.py:65
  108.7 3.8 %fusion.1 = f32[10,256]{1,0:T(8,128)S(1)} fusion(pred[10,256,1024]{2,1,0:T(32,128)(4,1)S(1)} %reshape.198, f32[10,256,1024]{2,1,0:T(8,128)S(1)} %get-tuple-element.186, f32[10,256]{1,0:T(8,128)S(1)} %broadcast_maximum_fusion), kind=kLoop, calls=%fused_computation.5 | loop fusion | flops 13104640 | bytes 13127680 | tf_op jit(solution)/shard_map/while/body/eval_jaxpr/reduce_sum | solution.py:72
  112.6 5.0 %fusion.12 = bf16[10,1024,128]{1,2,0:T(8,128)(2,1)} fusion(bf16[256,10,128]{0,2,1:T(8,128)(2,1)S(1)} %copy-done.9, pred[10,256,1024]{2,1,0:T(32,128)(4,1)S(1)} %reshape.198, f32[10,256,1024]{2,1,0:T(8,128)S(1)} %get-tuple-element.186, f32[10,256]{1,0:T(8,128)S(1)} %get-tuple-element.183), kind=kOutput, calls=%fused_computation.15 | convolution fusion | flops 685506560 | bytes 16394240 | tf_op jit(solution)/shard_map/while/body/eval_jaxpr/hqk,qhd->khd/dot_general | solution.py:122
  117.7 4.4 %copy.69 = bf16[1024,1280]{1,0:T(8,128)(2,1)} copy(bf16[1024,1280]{0,1:T(8,128)(2,1)} %bitcast.68) | data formatting | bytes 5242880 | tf_op jit(solution)/shard_map/convert_element_type | solution.py:159
  122.3 4.7 %copy.61 = bf16[1024,1280]{0,1:T(8,128)(2,1)} copy(bf16[1024,1280]{1,0:T(8,128)(2,1)} %all-gather.5.cloned.1.call-done) | data formatting | bytes 5242880 | tf_op jit(solution)/shard_map/all_gather | solution.py:96
  127.1 10.3 %multiply_reduce_fusion = (f32[256,10]{0,1:T(8,128)S(1)}, bf16[256,10,128]{0,2,1:T(8,128)(2,1)}) fusion(bf16[256,10,128]{0,2,1:T(8,128)(2,1)} %copy.65, f32[256,10]{0,1:T(8,128)S(1)} %bitcast_add_fusion, bf16[1024,10,128]{0,2,1:T(8,128)(2,1)} %bitcast.66, pred[10,256,1024]{2,1,0:T(32,128)(4,1)} %copy-done.1, f32[10,256,1024]{2,1,0:T(8,128)} %copy-done, ...), kind=kOutput, calls=%fused_computation.20 | convolution fusion | flops 686487040 | bytes 17080320 | tf_op jit(solution)/shard_map/while/body/eval_jaxpr/hqk,khd->qhd/dot_general | solution.py:73
  138.7 5.2 %multiply_convert_fusion = bf16[10,256,1024]{2,1,0:T(8,128)(2,1)S(1)} fusion(pred[10,256,1024]{2,1,0:T(32,128)(4,1)S(1)} %copy-done.2, f32[10,256,1024]{2,1,0:T(8,128)S(1)} %bitcast.62, f32[10,256]{1,0:T(8,128)S(1)} %bitcast.79, f32[10,256]{1,0:T(8,128)S(1)} %get-tuple-element.183, bf16[256,10,128]{0,2,1:T(8,128)(2,1)S(1)} %copy-done.10, ...), kind=kOutput, calls=%fused_computation | convolution fusion | flops 689438720 | bytes 21647360 | tf_op jit(solution)/shard_map/while/body/eval_jaxpr/qhd,khd->hqk/dot_general | solution.py:116
  143.9 3.2 %multiply_convert_fusion.1 = bf16[10,1024,128]{1,2,0:T(8,128)(2,1)} fusion(bf16[256,10,128]{0,2,1:T(8,128)(2,1)S(1)} %copy.66, bf16[10,256,1024]{2,1,0:T(8,128)(2,1)S(1)} %multiply_convert_fusion), kind=kOutput, calls=%fused_computation.9 | convolution fusion | flops 673710080 | bytes 8519680 | tf_op jit(solution)/shard_map/while/body/eval_jaxpr/hqk,qhd->khd/dot_general | solution.py:126
  147.2 4.5 %copy.67 = bf16[1024,1280]{1,0:T(8,128)(2,1)} copy(bf16[1024,1280]{0,1:T(8,128)(2,1)} %bitcast.65) | data formatting | bytes 5242880 | tf_op jit(solution)/shard_map/convert_element_type | solution.py:156
  152.9 4.4 %fusion.21 = bf16[10,256,128]{1,2,0:T(8,128)(2,1)S(1)} fusion(bf16[10,256,1024]{2,1,0:T(8,128)(2,1)} %copy-done.4, bf16[1024,10,128]{0,2,1:T(8,128)(2,1)S(1)} %bitcast.64), kind=kOutput, calls=%fused_computation.19 | convolution fusion | flops 671744000 | bytes 8519680 | tf_op jit(solution)/shard_map/while/body/eval_jaxpr/hqk,khd->qhd/dot_general | solution.py:129
  158.3 35.5 %reduce-scatter.3.cloned.1.call-done = bf16[256,1280]{1,0:T(8,128)(2,1)} async-done(((bf16[1024,1280]{1,0:T(8,128)(2,1)}), bf16[256,1280]{1,0:T(8,128)(2,1)}) %reduce-scatter.3.cloned.1.call-update) | async-done | bytes 655376 | tf_op jit(solution)/shard_map/reduce_scatter | solution.py:155
  (54 shorter events, 12.1 us)
Async XLA Ops:
  7.2 30.3 %copy-start.7 = (bf16[64,5120]{1,0:T(8,128)(2,1)S(1)}, bf16[64,5120]{1,0:T(8,128)(2,1)}, u32[]{:S(2)}) copy-start(bf16[64,5120]{1,0:T(8,128)(2,1)} %param.21) | copy-start | bytes 1966084
  7.2 50.9 %copy-start.8 = (bf16[64,5120]{1,0:T(8,128)(2,1)S(1)}, bf16[64,5120]{1,0:T(8,128)(2,1)}, u32[]{:S(2)}) copy-start(bf16[64,5120]{1,0:T(8,128)(2,1)} %param.24) | copy-start | bytes 1966084
  7.2 92.6 %all-gather.3.cloned.1.call-start = ((), (), s32[]{:S(2)}) async-start(), calls=%async_computation.6 | async-start | bytes 3276800 | tf_op jit(solution)/shard_map/all_gather | solution.py:95
  34.0 19.9 %all-to-all-start.2 = ((bf16[64,4,1280]{2,0,1:T(8,128)(2,1)}), bf16[64,4,1280]{2,0,1:T(8,128)(2,1)S(1)}, u32[]{:S(2)}, u32[]{:S(2)}) async-start(bf16[64,4,1280]{2,0,1:T(8,128)(2,1)} %bitcast.58), calls=%async_computation.2 | async-start | bytes 1310720 | tf_op jit(solution)/shard_map/all_to_all | solution.py:30
  53.9 3.5 %copy-start.6 = (bf16[64,4,1280]{2,0,1:T(8,128)(2,1)}, bf16[64,4,1280]{2,0,1:T(8,128)(2,1)S(1)}, u32[]{:S(2)}) copy-start(bf16[64,4,1280]{2,0,1:T(8,128)(2,1)S(1)} %all-to-all-done.2) | copy-start | bytes 1966084
  53.9 20.2 %all-to-all-start = ((bf16[64,4,1280]{2,0,1:T(8,128)(2,1)}), bf16[64,4,1280]{2,0,1:T(8,128)(2,1)S(1)}, u32[]{:S(2)}, u32[]{:S(2)}) async-start(bf16[64,4,1280]{2,0,1:T(8,128)(2,1)} %bitcast.60), calls=%async_computation | async-start | bytes 1310720 | tf_op jit(solution)/shard_map/all_to_all | solution.py:28
  57.4 65.0 %all-gather.5.cloned.1.call-start = ((), (), s32[]{:S(2)}) async-start(), calls=%async_computation.7 | async-start | bytes 3276800 | tf_op jit(solution)/shard_map/all_gather | solution.py:96
  74.1 21.0 %all-to-all-start.3 = ((bf16[64,4,1280]{2,0,1:T(8,128)(2,1)}), bf16[64,4,1280]{2,0,1:T(8,128)(2,1)}, u32[]{:S(2)}, u32[]{:S(2)}) async-start(bf16[64,4,1280]{2,0,1:T(8,128)(2,1)} %bitcast.57), calls=%async_computation.3 | async-start | bytes 1310720 | tf_op jit(solution)/shard_map/all_to_all | solution.py:31
  78.3 80.0 %reduce-scatter.5.cloned.1.call-start = ((), (), s32[]{:S(2)}) async-start(), calls=%async_computation.9 | async-start | bytes 3276800 | tf_op jit(solution)/shard_map/reduce_scatter | solution.py:158
  88.0 24.5 %copy-start.1 = (pred[10,256,1024]{2,1,0:T(32,128)(4,1)}, pred[10,256,1024]{2,1,0:T(32,128)(4,1)S(1)}, u32[]{:S(2)}) copy-start(pred[10,256,1024]{2,1,0:T(32,128)(4,1)S(1)} %reshape.198) | copy-start | bytes 7864324
  108.6 4.0 %copy-start = (f32[10,256,1024]{2,1,0:T(8,128)}, f32[10,256,1024]{2,1,0:T(8,128)S(1)}, u32[]{:S(2)}) copy-start(f32[10,256,1024]{2,1,0:T(8,128)S(1)} %get-tuple-element.186) | copy-start | bytes 31457284
  108.6 4.0 %copy-start.9 = (bf16[256,10,128]{0,2,1:T(8,128)(2,1)S(1)}, bf16[256,10,128]{0,2,1:T(8,128)(2,1)}, u32[]{:S(2)}) copy-start(bf16[256,10,128]{0,2,1:T(8,128)(2,1)} %copy.65) | copy-start | bytes 1966084
  122.1 71.8 %reduce-scatter.3.cloned.1.call-start = ((), (), s32[]{:S(2)}) async-start(), calls=%async_computation.8 | async-start | bytes 3276800 | tf_op jit(solution)/shard_map/reduce_scatter | solution.py:155
  122.3 15.1 %slice-start = ((s8[10485760]{0:T(1024)(128)(4,1)}), s8[2097152]{0:T(1024)(128)(4,1)S(1)}, s32[]{:S(2)}) async-start(s8[10485760]{0:T(1024)(128)(4,1)} %bitcast.61), calls=%async_computation.10 | async-start | bytes 4194304
  127.1 10.4 %slice-start.1 = ((s8[10485760]{0:T(1024)(128)(4,1)}), s8[4194304]{0:T(1024)(128)(4,1)S(1)}, s32[]{:S(2)}) async-start(s8[10485760]{0:T(1024)(128)(4,1)} %bitcast.61), calls=%async_computation.11 | async-start | bytes 8388608
  127.1 10.3 %slice-start.2 = ((s8[10485760]{0:T(1024)(128)(4,1)}), s8[4194304]{0:T(1024)(128)(4,1)S(1)}, s32[]{:S(2)}) async-start(s8[10485760]{0:T(1024)(128)(4,1)} %bitcast.61), calls=%async_computation.12 | async-start | bytes 8388608
  127.1 10.8 %copy-start.2 = (pred[10,256,1024]{2,1,0:T(32,128)(4,1)S(1)}, pred[10,256,1024]{2,1,0:T(32,128)(4,1)}, u32[]{:S(2)}) copy-start(pred[10,256,1024]{2,1,0:T(32,128)(4,1)} %copy-done.1) | copy-start | bytes 7864324
  127.1 11.5 %copy-start.5 = (bf16[1024,1280]{0,1:T(8,128)(2,1)S(1)}, bf16[1024,1280]{0,1:T(8,128)(2,1)}, u32[]{:S(2)}) copy-start(bf16[1024,1280]{0,1:T(8,128)(2,1)} %copy.61) | copy-start | bytes 7864324
  127.1 11.6 %copy-start.10 = (bf16[256,10,128]{0,2,1:T(8,128)(2,1)S(1)}, bf16[256,10,128]{0,2,1:T(8,128)(2,1)}, u32[]{:S(2)}) copy-start(bf16[256,10,128]{0,2,1:T(8,128)(2,1)} %copy.65) | copy-start | bytes 1966084
  143.9 3.3 %copy-start.4 = (bf16[10,256,1024]{2,1,0:T(8,128)(2,1)}, bf16[10,256,1024]{2,1,0:T(8,128)(2,1)S(1)}, u32[]{:S(2)}) copy-start(bf16[10,256,1024]{2,1,0:T(8,128)(2,1)S(1)} %multiply_convert_fusion) | copy-start | bytes 15728644
  147.2 4.6 %copy-start.11 = (bf16[256,10,128]{0,2,1:T(8,128)(2,1)S(1)}, bf16[256,10,128]{0,2,1:T(8,128)(2,1)}, u32[]{:S(2)}) copy-start(bf16[256,10,128]{0,2,1:T(8,128)(2,1)} %get-tuple-element.188) | copy-start | bytes 1966084
  147.2 5.7 %copy-start.3 = (bf16[1024,1280]{0,1:T(8,128)(2,1)S(1)}, bf16[1024,1280]{0,1:T(8,128)(2,1)}, u32[]{:S(2)}) copy-start(bf16[1024,1280]{0,1:T(8,128)(2,1)} %copy.57) | copy-start | bytes 7864324
Sparse Core Ops, SparseCore 0:
  32.1 24.6 all-gather.2
  60.3 26.9 all-gather.4
  122.2 33.7 reduce-scatter.4
  159.1 34.6 reduce-scatter.2
where the time goes:
time: 201 us; the launch traced here: 200 us
  waiting for transfers between devices  70.7 us (35%)
  local copies, waits for them, and re-layouts  43.7 us (22%)
  matrix products  32.4 us (16%)
  blocking collectives  23.5 us (12%)
  between operations  14 us (7%)
  starting transfers between devices  11.5 us (6%)
  other arithmetic  4.52 us (2%)
    reduce_scatter x1, waiting for transfers between devices, local(): lax.psum_scatter(key_acc.astype(jnp.bfloat16), 'frame', scatter_dimension...  35.5 us
    all_to_all x1, blocking collectives, local(): lax.all_to_all(keys, 'head', split_axis=1, concat_axis=0, tiled=True)  23.5 us
    all_to_all x1, waiting for transfers between devices, local(): lax.all_to_all(values, 'head', split_axis=1, concat_axis=0, tiled=True)  15.5 us
    all_to_all x1, waiting for transfers between devices, local(): lax.all_to_all(queries, 'head', split_axis=1, concat_axis=0, tiled=True)  15.1 us
    dot_general x1, matrix products, forward_step(): jnp.einsum('hqk,khd->qhd', weights.astype(jnp.bfloat16), value_block, pre...  10.3 us
    reshape x1, local copies, waits for them, and re-layouts, expand_tiles(): spread.reshape(head_count, query_tiles * tile_size, key_tiles * tile_size)  6.51 us
    dot_general x1, matrix products, backward_step(): jnp.einsum('qhd,khd->hqk', grad_heads, value_block, preferred_element_typ...  5.17 us
    dot_general x1, matrix products, backward_step(): jnp.einsum('hqk,qhd->khd', probs_half, grad_heads, preferred_element_type...  5.04 us
  transfers between devices with their start and end apart: 7, of which 4 were waited for; matrix products, arithmetic and copies ran while one was open for 39% of the time, Pallas kernels for 0%

commit v1 on v0

v1 whole, which is shorter than its diff:
```python
import functools
import math

import jax
import jax.numpy as jnp
from jax import lax
from jax.experimental import pallas as pl
from jax.experimental.pallas import tpu as pltpu
from jax.sharding import PartitionSpec as P

HD = 128
TILE = 128
EXCLUDED = -1e30
LOG2E = 1.4426950408889634
F32 = jnp.float32
BF16 = jnp.bfloat16
VMEM_LIMIT = 48 * 1024 * 1024
VMEM = pl.BlockSpec(memory_space=pltpu.VMEM)
SMEM = pl.BlockSpec(memory_space=pltpu.SMEM)


def there(index, step, size):
    if size & (size - 1) == 0:
        return index ^ step
    return (index + step) % size


def back(index, step, size):
    return there(index, step if size & (size - 1) == 0 else size - step, size)


class Plan:
    def __init__(self, rows, width, head_axis, frame_axis):
        self.rows = rows
        self.zn = head_axis
        self.groups = width // HD // head_axis
        self.on = math.gcd(self.groups, frame_axis)
        self.inn = frame_axis // self.on
        self.mine = self.groups // self.on
        self.slab = rows * head_axis
        self.tq = self.slab * self.on
        self.tk = self.tq * self.inn

    def place(self):
        frame = lax.axis_index("frame")
        return lax.axis_index("head"), frame // self.inn, frame % self.inn

    def column(self, z, o, first):
        return pl.multiple_of((z * self.groups + o * self.mine + first) * HD, HD)

    def send(self, array, z_step=0, o_step=0, i_step=0, returning=False):
        go = back if returning else there
        pairs = []
        for z in range(self.zn):
            for o in range(self.on):
                for i in range(self.inn):
                    source = (z * self.on + o) * self.inn + i
                    target = (
                        go(z, z_step, self.zn) * self.on + go(o, o_step, self.on)
                    ) * self.inn + go(i, i_step, self.inn)
                    pairs.append((source, target))
        return lax.ppermute(array, ("head", "frame"), pairs)


def shape(*dims, dtype=BF16):
    return jax.ShapeDtypeStruct(dims, dtype)


def call_mover(body, operands, out_shape, name):
    total = sum(math.prod(s.shape) * 2 for s in out_shape)
    return pl.pallas_call(
        body,
        out_shape=out_shape,
        in_specs=[VMEM] * len(operands),
        out_specs=[VMEM] * len(out_shape),
        compiler_params=pltpu.CompilerParams(vmem_limit_bytes=VMEM_LIMIT),
        cost_estimate=pl.CostEstimate(flops=0, bytes_accessed=2 * total, transcendentals=0),
        name=name,
    )(*operands)


def pack_outer(plan, arrays, first, width):
    def body(*refs):
        ins, outs = refs[:4], refs[4:]
        z, o, _ = plan.place()
        for step, out in enumerate(outs, 1):
            for k in range(plan.zn):
                at = plan.column(there(z, k, plan.zn), there(o, step, plan.on), first)
                for a, ref in enumerate(ins):
                    out[k, a] = ref[:, pl.ds(at, width)]

    out = [shape(plan.zn, 4, plan.rows, width)] * (plan.on - 1)
    return call_mover(body, arrays, out, "pack_outer")


def pack_heads(plan, arrays, received, first, width):
    def body(*refs):
        ins, got = refs[:4], refs[4 : 4 + len(received)]
        z, o, _ = plan.place()
        for k, out in enumerate(refs[4 + len(received) :]):
            at = plan.column(there(z, k, plan.zn), o, first)
            for a, ref in enumerate(ins):
                out[0, a] = ref[:, pl.ds(at, width)]
            for step, ref in enumerate(got, 1):
                out[step] = ref[k]

    out = [shape(plan.on, 4, plan.rows, width)] * plan.zn
    return call_mover(body, [*arrays, *received], out, "pack_heads")


def join_rows(plan, pieces, width):
    def body(*refs):
        ins, (qg, kv) = refs[: plan.zn], refs[plan.zn :]
        z = lax.axis_index("head")
        for k, ref in enumerate(ins):
            row = back(z, k, plan.zn) * plan.rows
            for step in range(plan.on):
                at = pl.ds(pl.multiple_of(step * plan.slab + row, plan.rows), plan.rows)
                for a in range(2):
                    qg[a, at], kv[a, at] = ref[step, a], ref[step, 2 + a]

    out = [shape(2, plan.tq, width)] * 2
    return call_mover(body, pieces, out, "join_rows")


def attend_body(plan, first, heads, *refs):
    mask, qg, kvs = refs[0], refs[1], refs[2 : 2 + plan.inn]
    rest = refs[2 + plan.inn :]
    row_outs, key_outs = rest[: plan.on], rest[plan.on : plan.on + plan.inn]
    key_t, value_t, scores, weights, grads, key_acc, value_acc = rest[plan.on + plan.inn :]
    _, o, i = plan.place()
    scaling = 1.0 / math.sqrt(HD)
    slab, tiles = plan.slab, plan.slab // TILE
    nt = (((1,), (1,)), ((), ()))
    dot = functools.partial(jnp.dot, preferred_element_type=F32)
    spots = [
        (m, step, t) for m in range(plan.inn) for step in range(plan.on) for t in range(tiles)
    ]

    def one_head(h, carry):
        cols = pl.ds(pl.multiple_of(h * HD, HD), HD)
        head = o * plan.mine + first + h
        for n, (m, step, t) in enumerate(spots):
            at = pl.ds(step * slab + t * TILE, TILE)
            put = pl.ds(n * TILE, TILE)
            key_t[:, put] = kvs[m][0, at, cols].astype(F32).T.astype(BF16)
            value_t[:, put] = kvs[m][1, at, cols].astype(F32).T.astype(BF16)

        for q_step in range(plan.on):
            q_at = pl.ds(q_step * slab, slab)
            q, g = qg[0, q_at, cols], qg[1, q_at, cols]
            q_tile = (back(o, q_step, plan.on) * plan.inn + i) * tiles
            peaks = [jnp.full((8, TILE), EXCLUDED, F32)] * tiles
            for n, (m, step, t) in enumerate(spots):
                key = kvs[m][0, pl.ds(step * slab + t * TILE, TILE), cols]
                k_tile = (back(o, step, plan.on) * plan.inn + back(i, m, plan.inn)) * tiles + t
                s = lax.dot_general(key, q, nt, preferred_element_type=F32) * (scaling * LOG2E)
                for j in range(tiles):
                    part = jnp.where(
                        mask[head, q_tile + j, k_tile] == 1,
                        s[:, j * TILE : (j + 1) * TILE],
                        EXCLUDED,
                    )
                    scores[pl.ds(n * TILE, TILE), pl.ds(j * TILE, TILE)] = part
                    peaks[j] = jnp.maximum(
                        peaks[j], jnp.max(part.reshape(TILE // 8, 8, TILE), axis=0)
                    )
            peak = jnp.concatenate([jnp.max(p, axis=0, keepdims=True) for p in peaks], axis=1)
            total = jnp.zeros((8, slab), F32)
            for n in range(len(spots)):
                at = pl.ds(n * TILE, TILE)
                w = jnp.exp2(scores[at] - peak)
                total += jnp.sum(w.reshape(TILE // 8, 8, slab), axis=0)
                scores[at] = w
                weights[at] = w.astype(BF16)
            inverse = 1.0 / jnp.sum(total, axis=0, keepdims=True)
            attended_t = (dot(value_t[...], weights[...]) * inverse).astype(BF16).astype(F32)
            delta = jnp.sum(g.astype(F32).T * attended_t, axis=0, keepdims=True)
            row_outs[q_step][0, :, cols] = attended_t.T.astype(BF16)
            for n, (m, step, t) in enumerate(spots):
                at = pl.ds(n * TILE, TILE)
                value = kvs[m][1, pl.ds(step * slab + t * TILE, TILE), cols]
                p = scores[at] * inverse
                dp = lax.dot_general(value, g, nt, preferred_element_type=F32)
                weights[at] = p.astype(BF16)
                grads[at] = (p * (dp - delta)).astype(BF16)
            query_t = dot(key_t[...], grads[...]) * scaling
            row_outs[q_step][1, :, cols] = query_t.T.astype(BF16)
            key_part, value_part = dot(grads[...], q), dot(weights[...], g)
            if q_step:
                key_part, value_part = key_part + key_acc[...], value_part + value_acc[...]
            if q_step < plan.on - 1:
                key_acc[...], value_acc[...] = key_part, value_part
            else:
                for m, out in enumerate(key_outs):
                    mine = slice(m * plan.tq, (m + 1) * plan.tq)
                    out[0, :, cols] = (key_part[mine] * scaling).astype(out.dtype)
                    out[1, :, cols] = value_part[mine].astype(out.dtype)
        return carry

    lax.fori_loop(0, heads, one_head, 0)


def attend(plan, mask, qg, kvs, first, heads):
    width = heads * HD
    out = [shape(2, plan.slab, width)] * plan.on
    out += [shape(2, plan.tq, width, dtype=F32)]
    out += [shape(2, plan.tq, width)] * (plan.inn - 1)
    return pl.pallas_call(
        functools.partial(attend_body, plan, first, heads),
        out_shape=out,
        in_specs=[SMEM] + [VMEM] * (1 + plan.inn),
        out_specs=[VMEM] * len(out),
        scratch_shapes=[
            pltpu.VMEM((HD, plan.tk), BF16),
            pltpu.VMEM((HD, plan.tk), BF16),
            pltpu.VMEM((plan.tk, plan.slab), F32),
            pltpu.VMEM((plan.tk, plan.slab), BF16),
            pltpu.VMEM((plan.tk, plan.slab), BF16),
            pltpu.VMEM((plan.tk, HD), F32),
            pltpu.VMEM((plan.tk, HD), F32),
        ],
        compiler_params=pltpu.CompilerParams(vmem_limit_bytes=VMEM_LIMIT),
        cost_estimate=pl.CostEstimate(
            flops=12 * heads * plan.tq * plan.tk * HD * 4,
            bytes_accessed=2 * width * (4 * plan.tq + 6 * plan.tk),
            transcendentals=heads * plan.tq * plan.tk,
        ),
        name="attend",
    )(mask, qg, *kvs)


def add_parts(plan, own, parts, width):
    def body(*refs):
        total = refs[0][...]
        for ref in refs[1 : 1 + len(parts)]:
            total += ref[...].astype(F32)
        for step, out in enumerate(refs[1 + len(parts) :]):
            out[...] = total[:, step * plan.slab : (step + 1) * plan.slab].astype(BF16)

    return pl.pallas_call(
        body,
        out_shape=[shape(2, plan.slab, width)] * plan.on,
        in_specs=[VMEM] * (1 + len(parts)),
        out_specs=[VMEM] * plan.on,
        compiler_params=pltpu.CompilerParams(vmem_limit_bytes=VMEM_LIMIT),
        cost_estimate=pl.CostEstimate(
            flops=2 * plan.tq * width * len(parts),
            bytes_accessed=2 * plan.tq * width * (6 + 2 * len(parts)),
            transcendentals=0,
        ),
        name="add_parts",
    )(own, *parts)


def place_all(plan, pieces):
    def body(*refs):
        ins, outs = refs[: len(pieces)], refs[len(pieces) :]
        _, o, _ = plan.place()
        for ref, (step, first, heads, which, _) in zip(ins, pieces, strict=True):
            at = pl.multiple_of((there(o, step, plan.on) * plan.mine + first) * HD, HD)
            for a in range(2):
                outs[which + a][:, pl.ds(at, heads * HD)] = ref[a]

    out = [shape(plan.slab, plan.groups * HD)] * 4
    return call_mover(body, [p[-1] for p in pieces], out, "place_all")


def chunk_sizes(plan):
    return [1] * plan.mine


def local(queries, keys, values, out_grad, tile_mask):
    plan = Plan(*queries.shape, lax.axis_size("head"), lax.axis_size("frame"))
    arrays = (queries, out_grad, keys, values)
    pieces = []
    first = 0
    for heads in chunk_sizes(plan):
        width = heads * HD
        received = []
        if plan.on > 1:
            outgoing = pack_outer(plan, arrays, first, width)
            received = [plan.send(a, o_step=s) for s, a in enumerate(outgoing, 1)]
        packed = pack_heads(plan, arrays, received, first, width)
        rows = [packed[0]] + [plan.send(a, z_step=k) for k, a in enumerate(packed) if k]
        qg, kv = join_rows(plan, rows, width)
        kvs = [kv] + [plan.send(kv, i_step=m) for m in range(1, plan.inn)]
        results = attend(plan, tile_mask, qg, kvs, first, heads)
        row_parts, key_parts = results[: plan.on], results[plan.on :]
        parts = [
            plan.send(a, i_step=m, returning=True) for m, a in enumerate(key_parts) if m
        ]
        key_sums = add_parts(plan, key_parts[0], parts, width)
        for which, group in ((0, row_parts), (2, key_sums)):
            for step, array in enumerate(group):
                if step:
                    array = plan.send(array, o_step=step, returning=True)
                pieces.append((step, first, heads, which, array))
        first += heads
    attended, query_grad, key_grad, value_grad = place_all(plan, pieces)
    return attended, query_grad, key_grad, value_grad


def solution(mesh):
    rows = P(("dp", "frame", "head"), None)
    out = P(("dp", "frame"), "head")
    return jax.shard_map(
        local,
        mesh=mesh,
        in_specs=(rows, rows, rows, rows, P("head", None, None)),
        out_specs=(out, out, out, out),
        check_vma=False,
    )
```

time: 201 us -> 138 us (0.69)
  starting transfers between devices: 11.5 us -> 63.6 us
  local copies, waits for them, and re-layouts: 43.7 us -> 4.47 us
  matrix products: 32.4 us -> 0 us
  waiting for transfers between devices: 70.7 us -> 45.8 us
  blocking collectives: 23.5 us -> 0 us
  Pallas kernels: 0 us -> 22.6 us
  between operations: 14 us -> 0.89 us
  other arithmetic: 4.52 us -> 0 us
    ppermute x0 -> x40, starting transfers between devices: none -> 63.6 us  [send(): return lax.ppermute(array, ('head', 'frame'), pairs)]
    ppermute x0 -> x40, waiting for transfers between devices: none -> 45.8 us  [send(): return lax.ppermute(array, ('head', 'frame'), pairs)]
    reduce_scatter x2 -> x0, waiting for transfers between devices: 35.5 us -> none  [the longest x1 35.5 us: local(): lax.psum_scatter(key_acc.astype(jnp.bfloat16), 'frame', scatter_dimension...]
    all_to_all x3 -> x0, waiting for transfers between devices: 34.4 us -> none  [the longest x1 15.5 us: local(): lax.all_to_all(values, 'head', split_axis=1, concat_axis=0, tiled=True)]
    dot_general x6 -> x0, matrix products: 32.4 us -> none  [the longest x1 10.3 us: forward_step(): jnp.einsum('hqk,khd->qhd', weights.astype(jnp.bfloat16), value_block, pre...]
    all_to_all x1 -> x0, blocking collectives: 23.5 us -> none  [local(): lax.all_to_all(keys, 'head', split_axis=1, concat_axis=0, tiled=True)]
    pallas_call x0 -> x26, Pallas kernels: none -> 22.6 us  [the longest x5 19.4 us: attend(): pl.pallas_call(functools.partial(attend_body, plan, first, heads), out_sh...]
    reshape x5 -> x0, local copies, waits for them, and re-layouts: 14.5 us -> none  [the longest x1 6.51 us: expand_tiles(): spread.reshape(head_count, query_tiles * tile_size, key_tiles * tile_size)]
  transfers between devices with their start and end apart: 7 -> 40, of which waited for: 4 -> 19; matrix products, arithmetic and copies ran while one was open for 39% -> 0% of each run, Pallas kernels for 0% -> 15%
where the time goes in v1:
time: 138 us; the launch traced here: 137 us
  starting transfers between devices  63.6 us (46%)
  waiting for transfers between devices  45.8 us (33%)
  Pallas kernels  22.6 us (16%)
  local copies, waits for them, and re-layouts  4.47 us (3%)
    ppermute x40, starting transfers between devices, send(): return lax.ppermute(array, ('head', 'frame'), pairs)  63.6 us
    ppermute x40, waiting for transfers between devices, send(): return lax.ppermute(array, ('head', 'frame'), pairs)  45.8 us
    pallas_call x5, Pallas kernels, attend(): pl.pallas_call(functools.partial(attend_body, plan, first, heads), out_sh...  19.4 us
    unnamed x15, local copies, waits for them, and re-layouts  4.47 us
    pallas_call x16, Pallas kernels, call_mover(): pl.pallas_call(body, out_shape=out_shape, in_specs=[VMEM] * len(operands)...  2.98 us
  transfers between devices with their start and end apart: 40, of which 19 were waited for; matrix products, arithmetic and copies ran while one was open for 0% of the time, Pallas kernels for 15%

profile of v1, /device:TPU:0, one launch (start us, length us, event | category | flops | bytes accessed | tf_op | source)
XLA Modules:
  0.0 137.4 jit_solution(3742262403719427123)
XLA Ops:
  5.1 3.0 %collective-permute-start.32 = (bf16[4,4,64,128]{3,2,1,0:T(8,128)(2,1)S(1)}, bf16[4,4,64,128]{3,2,1,0:T(8,128)(2,1)S(1)}, u32[]{:S(2)}, u32[]{:S(2)}) collective-permute-start(bf16[4,4,64,128]{3,2,1,0:T(8,128)(2,1)S(1)} %pack_outer.9), channel_id=1, source_target_pairs={{0,2},{1,3},{2,0},{3,1},{4,6},{5,7},{6,4},{7,5},{8,10},{9,11},{10,... | collective-permute-start | bytes 786440 | tf_op jit(solution)/shard_map/ppermute | solution.py:62
  12.7 2.5 %collective-permute-done.32.refs_4_ = bf16[4,4,64,128]{3,2,1,0:T(8,128)(2,1)S(1)} collective-permute-done((bf16[4,4,64,128]{3,2,1,0:T(8,128)(2,1)S(1)}, bf16[4,4,64,128]{3,2,1,0:T(8,128)(2,1)S(1)}, u32[]{:S(2)}, u32[]{:S(2)}) %collective-permute-start.32) | collective-permute-done | bytes 262176 | tf_op jit(solution)/shard_map/ppermute | solution.py:62
  17.5 3.3 %collective-permute-done.refs_4_ = bf16[4,4,64,128]{3,2,1,0:T(8,128)(2,1)S(1)} collective-permute-done((bf16[4,4,64,128]{3,2,1,0:T(8,128)(2,1)S(1)}, bf16[4,4,64,128]{3,2,1,0:T(8,128)(2,1)S(1)}, u32[]{:S(2)}, u32[]{:S(2)}) %collective-permute-start) | collective-permute-done | bytes 262176 | tf_op jit(solution)/shard_map/ppermute | solution.py:62
  20.8 3.1 %collective-permute-start.34 = (bf16[2,4,64,128]{3,2,1,0:T(8,128)(2,1)S(1)}, bf16[2,4,64,128]{3,2,1,0:T(8,128)(2,1)S(1)}, u32[]{:S(2)}, u32[]{:S(2)}) collective-permute-start(bf16[2,4,64,128]{3,2,1,0:T(8,128)(2,1)S(1)} %get-tuple-element.114), channel_id=1, source_target_pairs={{0,8},{1,9},{2,10},{3,11},{4,12},{5,13},{6,14},{7,15},{8,0},{9,1},... | collective-permute-start | bytes 393224 | tf_op jit(solution)/shard_map/ppermute | solution.py:62
  24.0 2.5 %collective-permute-done.8.refs_4_ = bf16[4,4,64,128]{3,2,1,0:T(8,128)(2,1)S(1)} collective-permute-done((bf16[4,4,64,128]{3,2,1,0:T(8,128)(2,1)S(1)}, bf16[4,4,64,128]{3,2,1,0:T(8,128)(2,1)S(1)}, u32[]{:S(2)}, u32[]{:S(2)}) %collective-permute-start.8) | collective-permute-done | bytes 262176 | tf_op jit(solution)/shard_map/ppermute | solution.py:62
  26.5 4.1 %collective-permute-start.35 = (bf16[2,4,64,128]{3,2,1,0:T(8,128)(2,1)S(1)}, bf16[2,4,64,128]{3,2,1,0:T(8,128)(2,1)S(1)}, u32[]{:S(2)}, u32[]{:S(2)}) collective-permute-start(bf16[2,4,64,128]{3,2,1,0:T(8,128)(2,1)S(1)} %get-tuple-element.115), channel_id=1, source_target_pairs={{0,12},{1,13},{2,14},{3,15},{4,8},{5,9},{6,10},{7,11},{8,4},{9,5},... | collective-permute-start | bytes 393224 | tf_op jit(solution)/shard_map/ppermute | solution.py:62
  34.2 2.7 %collective-permute-done.24.refs_4_ = bf16[4,4,64,128]{3,2,1,0:T(8,128)(2,1)S(1)} collective-permute-done((bf16[4,4,64,128]{3,2,1,0:T(8,128)(2,1)S(1)}, bf16[4,4,64,128]{3,2,1,0:T(8,128)(2,1)S(1)}, u32[]{:S(2)}, u32[]{:S(2)}) %collective-permute-start.24) | collective-permute-done | bytes 262176 | tf_op jit(solution)/shard_map/ppermute | solution.py:62
  36.9 2.8 %collective-permute-start.2 = (bf16[2,4,64,128]{3,2,1,0:T(8,128)(2,1)S(1)}, bf16[2,4,64,128]{3,2,1,0:T(8,128)(2,1)S(1)}, u32[]{:S(2)}, u32[]{:S(2)}) collective-permute-start(bf16[2,4,64,128]{3,2,1,0:T(8,128)(2,1)S(1)} %get-tuple-element.66), channel_id=1, source_target_pairs={{0,8},{1,9},{2,10},{3,11},{4,12},{5,13},{6,14},{7,15},{8,0},{9,1},... | collective-permute-start | bytes 393224 | tf_op jit(solution)/shard_map/ppermute | solution.py:62
  41.4 2.8 %collective-permute-start.10 = (bf16[2,4,64,128]{3,2,1,0:T(8,128)(2,1)S(1)}, bf16[2,4,64,128]{3,2,1,0:T(8,128)(2,1)S(1)}, u32[]{:S(2)}, u32[]{:S(2)}) collective-permute-start(bf16[2,4,64,128]{3,2,1,0:T(8,128)(2,1)S(1)} %get-tuple-element.78), channel_id=1, source_target_pairs={{0,8},{1,9},{2,10},{3,11},{4,12},{5,13},{6,14},{7,15},{8,0},{9,1},... | collective-permute-start | bytes 393224 | tf_op jit(solution)/shard_map/ppermute | solution.py:62
  45.8 4.1 %collective-permute-done.2.refs_2_ = bf16[2,4,64,128]{3,2,1,0:T(8,128)(2,1)S(1)} collective-permute-done((bf16[2,4,64,128]{3,2,1,0:T(8,128)(2,1)S(1)}, bf16[2,4,64,128]{3,2,1,0:T(8,128)(2,1)S(1)}, u32[]{:S(2)}, u32[]{:S(2)}) %collective-permute-start.2) | collective-permute-done | bytes 131104 | tf_op jit(solution)/shard_map/ppermute | solution.py:62
  50.5 8.6 %collective-permute-start.18 = (bf16[2,4,64,128]{3,2,1,0:T(8,128)(2,1)S(1)}, bf16[2,4,64,128]{3,2,1,0:T(8,128)(2,1)S(1)}, u32[]{:S(2)}, u32[]{:S(2)}) collective-permute-start(bf16[2,4,64,128]{3,2,1,0:T(8,128)(2,1)S(1)} %get-tuple-element.90), channel_id=1, source_target_pairs={{0,8},{1,9},{2,10},{3,11},{4,12},{5,13},{6,14},{7,15},{8,0},{9,1},... | collective-permute-start | bytes 393224 | tf_op jit(solution)/shard_map/ppermute | solution.py:62
  59.2 2.6 %collective-permute-done.10.refs_2_ = bf16[2,4,64,128]{3,2,1,0:T(8,128)(2,1)S(1)} collective-permute-done((bf16[2,4,64,128]{3,2,1,0:T(8,128)(2,1)S(1)}, bf16[2,4,64,128]{3,2,1,0:T(8,128)(2,1)S(1)}, u32[]{:S(2)}, u32[]{:S(2)}) %collective-permute-start.10) | collective-permute-done | bytes 131104 | tf_op jit(solution)/shard_map/ppermute | solution.py:62
  62.9 6.4 %collective-permute-start.25 = (bf16[2,4,64,128]{3,2,1,0:T(8,128)(2,1)S(1)}, bf16[2,4,64,128]{3,2,1,0:T(8,128)(2,1)S(1)}, u32[]{:S(2)}, u32[]{:S(2)}) collective-permute-start(bf16[2,4,64,128]{3,2,1,0:T(8,128)(2,1)S(1)} %get-tuple-element.101), channel_id=1, source_target_pairs={{0,4},{1,5},{2,6},{3,7},{4,0},{5,1},{6,2},{7,3},{8,12},{9,13},{10,... | collective-permute-start | bytes 393224 | tf_op jit(solution)/shard_map/ppermute | solution.py:62
  71.6 2.5 %collective-permute-start.27 = (bf16[2,4,64,128]{3,2,1,0:T(8,128)(2,1)S(1)}, bf16[2,4,64,128]{3,2,1,0:T(8,128)(2,1)S(1)}, u32[]{:S(2)}, u32[]{:S(2)}) collective-permute-start(bf16[2,4,64,128]{3,2,1,0:T(8,128)(2,1)S(1)} %get-tuple-element.103), channel_id=1, source_target_pairs={{0,12},{1,13},{2,14},{3,15},{4,8},{5,9},{6,10},{7,11},{8,4},{9,5},... | collective-permute-start | bytes 393224 | tf_op jit(solution)/shard_map/ppermute | solution.py:62
  75.0 7.8 %collective-permute-done.26.refs_2_ = bf16[2,4,64,128]{3,2,1,0:T(8,128)(2,1)S(1)} collective-permute-done((bf16[2,4,64,128]{3,2,1,0:T(8,128)(2,1)S(1)}, bf16[2,4,64,128]{3,2,1,0:T(8,128)(2,1)S(1)}, u32[]{:S(2)}, u32[]{:S(2)}) %collective-permute-start.26) | collective-permute-done | bytes 131104 | tf_op jit(solution)/shard_map/ppermute | solution.py:62
  83.5 3.8 %attend.9 = (bf16[2,256,128]{2,1,0:T(8,128)(2,1)S(1)}, bf16[2,256,128]{2,1,0:T(8,128)(2,1)S(1)}, f32[2,512,128]{2,1,0:T(8,128)S(1)}, bf16[2,512,128]{2,1,0:T(8,128)(2,1)S(1)}) custom-call(s32[10,8,8]{2,1,0:T(8,128)S(1)} %copy.9.refs_0_, bf16[2,512,128]{2,1,0:T(8,128)(2,1)S(1)} %get-tuple-element.116.refs_1_, ...), custom_call_target="tpu_custom_call" | custom-call | flops 3221225472 | bytes 2097152 | tf_op jit(solution)/shard_map/attend/pallas_call | solution.py:209
  87.4 3.8 %attend.5 = (bf16[2,256,128]{2,1,0:T(8,128)(2,1)S(1)}, bf16[2,256,128]{2,1,0:T(8,128)(2,1)S(1)}, f32[2,512,128]{2,1,0:T(8,128)S(1)}, bf16[2,512,128]{2,1,0:T(8,128)(2,1)S(1)}) custom-call(s32[10,8,8]{2,1,0:T(8,128)S(1)} %copy.9.refs_0_, bf16[2,512,128]{2,1,0:T(8,128)(2,1)S(1)} %get-tuple-element.68.refs_1_, ...), custom_call_target="tpu_custom_call" | custom-call | flops 3221225472 | bytes 2097152 | tf_op jit(solution)/shard_map/attend/pallas_call | solution.py:209
  91.8 3.8 %attend.6 = (bf16[2,256,128]{2,1,0:T(8,128)(2,1)S(1)}, bf16[2,256,128]{2,1,0:T(8,128)(2,1)S(1)}, f32[2,512,128]{2,1,0:T(8,128)S(1)}, bf16[2,512,128]{2,1,0:T(8,128)(2,1)S(1)}) custom-call(s32[10,8,8]{2,1,0:T(8,128)S(1)} %copy.9.refs_0_, bf16[2,512,128]{2,1,0:T(8,128)(2,1)S(1)} %get-tuple-element.80.refs_1_, ...), custom_call_target="tpu_custom_call" | custom-call | flops 3221225472 | bytes 2097152 | tf_op jit(solution)/shard_map/attend/pallas_call | solution.py:209
  95.8 4.0 %attend.7 = (bf16[2,256,128]{2,1,0:T(8,128)(2,1)S(1)}, bf16[2,256,128]{2,1,0:T(8,128)(2,1)S(1)}, f32[2,512,128]{2,1,0:T(8,128)S(1)}, bf16[2,512,128]{2,1,0:T(8,128)(2,1)S(1)}) custom-call(s32[10,8,8]{2,1,0:T(8,128)S(1)} %copy.9.refs_0_, bf16[2,512,128]{2,1,0:T(8,128)(2,1)S(1)} %get-tuple-element.92.refs_1_, ...), custom_call_target="tpu_custom_call" | custom-call | flops 3221225472 | bytes 2097152 | tf_op jit(solution)/shard_map/attend/pallas_call | solution.py:209
  100.4 3.8 %attend.8 = (bf16[2,256,128]{2,1,0:T(8,128)(2,1)S(1)}, bf16[2,256,128]{2,1,0:T(8,128)(2,1)S(1)}, f32[2,512,128]{2,1,0:T(8,128)S(1)}, bf16[2,512,128]{2,1,0:T(8,128)(2,1)S(1)}) custom-call(s32[10,8,8]{2,1,0:T(8,128)S(1)} %copy.9.refs_0_, bf16[2,512,128]{2,1,0:T(8,128)(2,1)S(1)} %get-tuple-element.104.refs_1_, ...), custom_call_target="tpu_custom_call" | custom-call | flops 3221225472 | bytes 2097152 | tf_op jit(solution)/shard_map/attend/pallas_call | solution.py:209
  124.7 2.8 %collective-permute-done.7.refs_3_ = bf16[2,256,128]{2,1,0:T(8,128)(2,1)S(1)} collective-permute-done((bf16[2,256,128]{2,1,0:T(8,128)(2,1)S(1)}, bf16[2,256,128]{2,1,0:T(8,128)(2,1)S(1)}, u32[]{:S(2)}, u32[]{:S(2)}) %collective-permute-start.7) | collective-permute-done | bytes 131104 | tf_op jit(solution)/shard_map/ppermute | solution.py:62
  127.5 2.8 %collective-permute-done.15.refs_7_ = bf16[2,256,128]{2,1,0:T(8,128)(2,1)S(1)} collective-permute-done((bf16[2,256,128]{2,1,0:T(8,128)(2,1)S(1)}, bf16[2,256,128]{2,1,0:T(8,128)(2,1)S(1)}, u32[]{:S(2)}, u32[]{:S(2)}) %collective-permute-start.15) | collective-permute-done | bytes 131104 | tf_op jit(solution)/shard_map/ppermute | solution.py:62
  130.3 2.8 %collective-permute-done.23.refs_11_ = bf16[2,256,128]{2,1,0:T(8,128)(2,1)S(1)} collective-permute-done((bf16[2,256,128]{2,1,0:T(8,128)(2,1)S(1)}, bf16[2,256,128]{2,1,0:T(8,128)(2,1)S(1)}, u32[]{:S(2)}, u32[]{:S(2)}) %collective-permute-start.23) | collective-permute-done | bytes 131104 | tf_op jit(solution)/shard_map/ppermute | solution.py:62
  133.1 2.3 %collective-permute-done.31.refs_15_ = bf16[2,256,128]{2,1,0:T(8,128)(2,1)S(1)} collective-permute-done((bf16[2,256,128]{2,1,0:T(8,128)(2,1)S(1)}, bf16[2,256,128]{2,1,0:T(8,128)(2,1)S(1)}, u32[]{:S(2)}, u32[]{:S(2)}) %collective-permute-start.31) | collective-permute-done | bytes 131104 | tf_op jit(solution)/shard_map/ppermute | solution.py:62
  (97 shorter events, 47.5 us)
Async XLA Ops:
  8.3 18.1 %collective-permute-start.8 = (bf16[4,4,64,128]{3,2,1,0:T(8,128)(2,1)S(1)}, bf16[4,4,64,128]{3,2,1,0:T(8,128)(2,1)S(1)}, u32[]{:S(2)}, u32[]{:S(2)}) collective-permute-start(bf16[4,4,64,128]{3,2,1,0:T(8,128)(2,1)S(1)} %pack_outer.6), channel_id=1, source_target_pairs={{0,2},{1,3},{2,0},{3,1},{4,6},{5,7},{6,4},{7,5},{8,10},{9,11},{10,... | collective-permute-start | bytes 786440 | tf_op jit(solution)/shard_map/ppermute | solution.py:62
  10.5 21.6 %collective-permute-start.16 = (bf16[4,4,64,128]{3,2,1,0:T(8,128)(2,1)S(1)}, bf16[4,4,64,128]{3,2,1,0:T(8,128)(2,1)S(1)}, u32[]{:S(2)}, u32[]{:S(2)}) collective-permute-start(bf16[4,4,64,128]{3,2,1,0:T(8,128)(2,1)S(1)} %pack_outer.7), channel_id=1, source_target_pairs={{0,2},{1,3},{2,0},{3,1},{4,6},{5,7},{6,4},{7,5},{8,10},{9,11},{10,... | collective-permute-start | bytes 786440 | tf_op jit(solution)/shard_map/ppermute | solution.py:62
  10.6 26.2 %collective-permute-start.24 = (bf16[4,4,64,128]{3,2,1,0:T(8,128)(2,1)S(1)}, bf16[4,4,64,128]{3,2,1,0:T(8,128)(2,1)S(1)}, u32[]{:S(2)}, u32[]{:S(2)}) collective-permute-start(bf16[4,4,64,128]{3,2,1,0:T(8,128)(2,1)S(1)} %pack_outer.8), channel_id=1, source_target_pairs={{0,2},{1,3},{2,0},{3,1},{4,6},{5,7},{6,4},{7,5},{8,10},{9,11},{10,... | collective-permute-start | bytes 786440 | tf_op jit(solution)/shard_map/ppermute | solution.py:62
  15.3 24.4 %collective-permute-start.33 = (bf16[2,4,64,128]{3,2,1,0:T(8,128)(2,1)S(1)}, bf16[2,4,64,128]{3,2,1,0:T(8,128)(2,1)S(1)}, u32[]{:S(2)}, u32[]{:S(2)}) collective-permute-start(bf16[2,4,64,128]{3,2,1,0:T(8,128)(2,1)S(1)} %get-tuple-element.113), channel_id=1, source_target_pairs={{0,4},{1,5},{2,6},{3,7},{4,0},{5,1},{6,2},{7,3},{8,12},{9,13},{10,... | collective-permute-start | bytes 393224 | tf_op jit(solution)/shard_map/ppermute | solution.py:62
  20.8 20.3 %collective-permute-start.34 = (bf16[2,4,64,128]{3,2,1,0:T(8,128)(2,1)S(1)}, bf16[2,4,64,128]{3,2,1,0:T(8,128)(2,1)S(1)}, u32[]{:S(2)}, u32[]{:S(2)}) collective-permute-start(bf16[2,4,64,128]{3,2,1,0:T(8,128)(2,1)S(1)} %get-tuple-element.114), channel_id=1, source_target_pairs={{0,8},{1,9},{2,10},{3,11},{4,12},{5,13},{6,14},{7,15},{8,0},{9,1},... | collective-permute-start | bytes 393224 | tf_op jit(solution)/shard_map/ppermute | solution.py:62
  26.5 15.0 %collective-permute-start.35 = (bf16[2,4,64,128]{3,2,1,0:T(8,128)(2,1)S(1)}, bf16[2,4,64,128]{3,2,1,0:T(8,128)(2,1)S(1)}, u32[]{:S(2)}, u32[]{:S(2)}) collective-permute-start(bf16[2,4,64,128]{3,2,1,0:T(8,128)(2,1)S(1)} %get-tuple-element.115), channel_id=1, source_target_pairs={{0,12},{1,13},{2,14},{3,15},{4,8},{5,9},{6,10},{7,11},{8,4},{9,5},... | collective-permute-start | bytes 393224 | tf_op jit(solution)/shard_map/ppermute | solution.py:62
  41.1 18.0 %collective-permute-start.9 = (bf16[2,4,64,128]{3,2,1,0:T(8,128)(2,1)S(1)}, bf16[2,4,64,128]{3,2,1,0:T(8,128)(2,1)S(1)}, u32[]{:S(2)}, u32[]{:S(2)}) collective-permute-start(bf16[2,4,64,128]{3,2,1,0:T(8,128)(2,1)S(1)} %get-tuple-element.77), channel_id=1, source_target_pairs={{0,4},{1,5},{2,6},{3,7},{4,0},{5,1},{6,2},{7,3},{8,12},{9,13},{10,... | collective-permute-start | bytes 393224 | tf_op jit(solution)/shard_map/ppermute | solution.py:62
  41.4 20.3 %collective-permute-start.10 = (bf16[2,4,64,128]{3,2,1,0:T(8,128)(2,1)S(1)}, bf16[2,4,64,128]{3,2,1,0:T(8,128)(2,1)S(1)}, u32[]{:S(2)}, u32[]{:S(2)}) collective-permute-start(bf16[2,4,64,128]{3,2,1,0:T(8,128)(2,1)S(1)} %get-tuple-element.78), channel_id=1, source_target_pairs={{0,8},{1,9},{2,10},{3,11},{4,12},{5,13},{6,14},{7,15},{8,0},{9,1},... | collective-permute-start | bytes 393224 | tf_op jit(solution)/shard_map/ppermute | solution.py:62
  44.3 18.6 %collective-permute-start.11 = (bf16[2,4,64,128]{3,2,1,0:T(8,128)(2,1)S(1)}, bf16[2,4,64,128]{3,2,1,0:T(8,128)(2,1)S(1)}, u32[]{:S(2)}, u32[]{:S(2)}) collective-permute-start(bf16[2,4,64,128]{3,2,1,0:T(8,128)(2,1)S(1)} %get-tuple-element.79), channel_id=1, source_target_pairs={{0,12},{1,13},{2,14},{3,15},{4,8},{5,9},{6,10},{7,11},{8,4},{9,5},... | collective-permute-start | bytes 393224 | tf_op jit(solution)/shard_map/ppermute | solution.py:62
  49.9 19.5 %collective-permute-start.17 = (bf16[2,4,64,128]{3,2,1,0:T(8,128)(2,1)S(1)}, bf16[2,4,64,128]{3,2,1,0:T(8,128)(2,1)S(1)}, u32[]{:S(2)}, u32[]{:S(2)}) collective-permute-start(bf16[2,4,64,128]{3,2,1,0:T(8,128)(2,1)S(1)} %get-tuple-element.89), channel_id=1, source_target_pairs={{0,4},{1,5},{2,6},{3,7},{4,0},{5,1},{6,2},{7,3},{8,12},{9,13},{10,... | collective-permute-start | bytes 393224 | tf_op jit(solution)/shard_map/ppermute | solution.py:62
  50.5 21.1 %collective-permute-start.18 = (bf16[2,4,64,128]{3,2,1,0:T(8,128)(2,1)S(1)}, bf16[2,4,64,128]{3,2,1,0:T(8,128)(2,1)S(1)}, u32[]{:S(2)}, u32[]{:S(2)}) collective-permute-start(bf16[2,4,64,128]{3,2,1,0:T(8,128)(2,1)S(1)} %get-tuple-element.90), channel_id=1, source_target_pairs={{0,8},{1,9},{2,10},{3,11},{4,12},{5,13},{6,14},{7,15},{8,0},{9,1},... | collective-permute-start | bytes 393224 | tf_op jit(solution)/shard_map/ppermute | solution.py:62
  59.1 24.3 %collective-permute-start.36 = (bf16[2,512,128]{2,1,0:T(8,128)(2,1)S(1)}, bf16[2,512,128]{2,1,0:T(8,128)(2,1)S(1)}, u32[]{:S(2)}, u32[]{:S(2)}) collective-permute-start(bf16[2,512,128]{2,1,0:T(8,128)(2,1)S(1)} %get-tuple-element.117.refs_2_), channel_id=1, source_target_pairs={{0,1},{1,0},{2,3},{3,2},{4,5},{5,4},{6,7},{7,6},{8,9},{9,8},{10,11... | collective-permute-start | bytes 786440 | tf_op jit(solution)/shard_map/ppermute | solution.py:62
  69.4 13.5 %collective-permute-start.26 = (bf16[2,4,64,128]{3,2,1,0:T(8,128)(2,1)S(1)}, bf16[2,4,64,128]{3,2,1,0:T(8,128)(2,1)S(1)}, u32[]{:S(2)}, u32[]{:S(2)}) collective-permute-start(bf16[2,4,64,128]{3,2,1,0:T(8,128)(2,1)S(1)} %get-tuple-element.102), channel_id=1, source_target_pairs={{0,8},{1,9},{2,10},{3,11},{4,12},{5,13},{6,14},{7,15},{8,0},{9,1},... | collective-permute-start | bytes 393224 | tf_op jit(solution)/shard_map/ppermute | solution.py:62
  74.3 13.1 %collective-permute-start.4 = (bf16[2,512,128]{2,1,0:T(8,128)(2,1)S(1)}, bf16[2,512,128]{2,1,0:T(8,128)(2,1)S(1)}, u32[]{:S(2)}, u32[]{:S(2)}) collective-permute-start(bf16[2,512,128]{2,1,0:T(8,128)(2,1)S(1)} %get-tuple-element.69.refs_2_), channel_id=1, source_target_pairs={{0,1},{1,0},{2,3},{3,2},{4,5},{5,4},{6,7},{7,6},{8,9},{9,8},{10,11... | collective-permute-start | bytes 786440 | tf_op jit(solution)/shard_map/ppermute | solution.py:62
  74.5 17.3 %collective-permute-start.12 = (bf16[2,512,128]{2,1,0:T(8,128)(2,1)S(1)}, bf16[2,512,128]{2,1,0:T(8,128)(2,1)S(1)}, u32[]{:S(2)}, u32[]{:S(2)}) collective-permute-start(bf16[2,512,128]{2,1,0:T(8,128)(2,1)S(1)} %get-tuple-element.81.refs_2_), channel_id=1, source_target_pairs={{0,1},{1,0},{2,3},{3,2},{4,5},{5,4},{6,7},{7,6},{8,9},{9,8},{10,11... | collective-permute-start | bytes 786440 | tf_op jit(solution)/shard_map/ppermute | solution.py:62
  82.9 17.4 %collective-permute-start.28 = (bf16[2,512,128]{2,1,0:T(8,128)(2,1)S(1)}, bf16[2,512,128]{2,1,0:T(8,128)(2,1)S(1)}, u32[]{:S(2)}, u32[]{:S(2)}) collective-permute-start(bf16[2,512,128]{2,1,0:T(8,128)(2,1)S(1)} %get-tuple-element.105.refs_2_), channel_id=1, source_target_pairs={{0,1},{1,0},{2,3},{3,2},{4,5},{5,4},{6,7},{7,6},{8,9},{9,8},{10,11... | collective-permute-start | bytes 786440 | tf_op jit(solution)/shard_map/ppermute | solution.py:62
  87.3 17.0 %collective-permute-start.38 = (bf16[2,512,128]{2,1,0:T(8,128)(2,1)S(1)}, bf16[2,512,128]{2,1,0:T(8,128)(2,1)S(1)}, u32[]{:S(2)}, u32[]{:S(2)}) collective-permute-start(bf16[2,512,128]{2,1,0:T(8,128)(2,1)S(1)} %get-tuple-element.121), channel_id=1, source_target_pairs={{0,1},{1,0},{2,3},{3,2},{4,5},{5,4},{6,7},{7,6},{8,9},{9,8},{10,11... | collective-permute-start | bytes 786440 | tf_op jit(solution)/shard_map/ppermute | solution.py:62
  91.3 14.6 %collective-permute-start.6 = (bf16[2,512,128]{2,1,0:T(8,128)(2,1)S(1)}, bf16[2,512,128]{2,1,0:T(8,128)(2,1)S(1)}, u32[]{:S(2)}, u32[]{:S(2)}) collective-permute-start(bf16[2,512,128]{2,1,0:T(8,128)(2,1)S(1)} %get-tuple-element.73), channel_id=1, source_target_pairs={{0,1},{1,0},{2,3},{3,2},{4,5},{5,4},{6,7},{7,6},{8,9},{9,8},{10,11... | collective-permute-start | bytes 786440 | tf_op jit(solution)/shard_map/ppermute | solution.py:62
  108.4 13.5 %collective-permute-start.29 = (bf16[2,256,128]{2,1,0:T(8,128)(2,1)S(1)}, bf16[2,256,128]{2,1,0:T(8,128)(2,1)S(1)}, u32[]{:S(2)}, u32[]{:S(2)}) collective-permute-start(bf16[2,256,128]{2,1,0:T(8,128)(2,1)S(1)} %get-tuple-element.107), channel_id=1, source_target_pairs={{0,2},{1,3},{2,0},{3,1},{4,6},{5,7},{6,4},{7,5},{8,10},{9,11},{10,... | collective-permute-start | bytes 393224 | tf_op jit(solution)/shard_map/ppermute | solution.py:62
  110.7 14.0 %collective-permute-start.39 = (bf16[2,256,128]{2,1,0:T(8,128)(2,1)S(1)}, bf16[2,256,128]{2,1,0:T(8,128)(2,1)S(1)}, u32[]{:S(2)}, u32[]{:S(2)}) collective-permute-start(bf16[2,256,128]{2,1,0:T(8,128)(2,1)S(1)} %get-tuple-element.123), channel_id=1, source_target_pairs={{0,2},{1,3},{2,0},{3,1},{4,6},{5,7},{6,4},{7,5},{8,10},{9,11},{10,... | collective-permute-start | bytes 393224 | tf_op jit(solution)/shard_map/ppermute | solution.py:62
  113.5 14.0 %collective-permute-start.7 = (bf16[2,256,128]{2,1,0:T(8,128)(2,1)S(1)}, bf16[2,256,128]{2,1,0:T(8,128)(2,1)S(1)}, u32[]{:S(2)}, u32[]{:S(2)}) collective-permute-start(bf16[2,256,128]{2,1,0:T(8,128)(2,1)S(1)} %get-tuple-element.75), channel_id=1, source_target_pairs={{0,2},{1,3},{2,0},{3,1},{4,6},{5,7},{6,4},{7,5},{8,10},{9,11},{10,... | collective-permute-start | bytes 393224 | tf_op jit(solution)/shard_map/ppermute | solution.py:62
  116.3 14.0 %collective-permute-start.15 = (bf16[2,256,128]{2,1,0:T(8,128)(2,1)S(1)}, bf16[2,256,128]{2,1,0:T(8,128)(2,1)S(1)}, u32[]{:S(2)}, u32[]{:S(2)}) collective-permute-start(bf16[2,256,128]{2,1,0:T(8,128)(2,1)S(1)} %get-tuple-element.87), channel_id=1, source_target_pairs={{0,2},{1,3},{2,0},{3,1},{4,6},{5,7},{6,4},{7,5},{8,10},{9,11},{10,... | collective-permute-start | bytes 393224 | tf_op jit(solution)/shard_map/ppermute | solution.py:62
  119.1 14.0 %collective-permute-start.23 = (bf16[2,256,128]{2,1,0:T(8,128)(2,1)S(1)}, bf16[2,256,128]{2,1,0:T(8,128)(2,1)S(1)}, u32[]{:S(2)}, u32[]{:S(2)}) collective-permute-start(bf16[2,256,128]{2,1,0:T(8,128)(2,1)S(1)} %get-tuple-element.99), channel_id=1, source_target_pairs={{0,2},{1,3},{2,0},{3,1},{4,6},{5,7},{6,4},{7,5},{8,10},{9,11},{10,... | collective-permute-start | bytes 393224 | tf_op jit(solution)/shard_map/ppermute | solution.py:62
  121.9 13.6 %collective-permute-start.31 = (bf16[2,256,128]{2,1,0:T(8,128)(2,1)S(1)}, bf16[2,256,128]{2,1,0:T(8,128)(2,1)S(1)}, u32[]{:S(2)}, u32[]{:S(2)}) collective-permute-start(bf16[2,256,128]{2,1,0:T(8,128)(2,1)S(1)} %get-tuple-element.111), channel_id=1, source_target_pairs={{0,2},{1,3},{2,0},{3,1},{4,6},{5,7},{6,4},{7,5},{8,10},{9,11},{10,... | collective-permute-start | bytes 393224 | tf_op jit(solution)/shard_map/ppermute | solution.py:62
  (23 other events, 219.1 us)

commit v2 on v1

--- a/solution.py
+++ b/solution.py
@@ -15,6 +15,9 @@
 F32 = jnp.float32
 BF16 = jnp.bfloat16
 VMEM_LIMIT = 48 * 1024 * 1024
+SMALL = pl.CostEstimate(flops=1024, bytes_accessed=1024, transcendentals=0)
+LARGE = pl.CostEstimate(flops=1 << 33, bytes_accessed=1024, transcendentals=0)
+HBM = pl.BlockSpec(memory_space=pltpu.HBM)
 VMEM = pl.BlockSpec(memory_space=pltpu.VMEM)
 SMEM = pl.BlockSpec(memory_space=pltpu.SMEM)
 
@@ -33,6 +36,7 @@
     def __init__(self, rows, width, head_axis, frame_axis):
         self.rows = rows
         self.zn = head_axis
+        self.steps = [0, 3, 2, 1] if head_axis == 4 else list(range(head_axis))
         self.groups = width // HD // head_axis
         self.on = math.gcd(self.groups, frame_axis)
         self.inn = frame_axis // self.on
@@ -66,7 +70,7 @@
     return jax.ShapeDtypeStruct(dims, dtype)
 
 
-def call_mover(body, operands, out_shape, name):
+def call_mover(body, operands, out_shape, name, weight=SMALL):
     total = sum(math.prod(s.shape) * 2 for s in out_shape)
     return pl.pallas_call(
         body,
@@ -74,53 +78,73 @@
         in_specs=[VMEM] * len(operands),
         out_specs=[VMEM] * len(out_shape),
         compiler_params=pltpu.CompilerParams(vmem_limit_bytes=VMEM_LIMIT),
-        cost_estimate=pl.CostEstimate(flops=0, bytes_accessed=2 * total, transcendentals=0),
+        cost_estimate=weight,
         name=name,
     )(*operands)
 
 
-def pack_outer(plan, arrays, first, width):
+def pack_all(plan, arrays, chunks):
     def body(*refs):
-        ins, outs = refs[:4], refs[4:]
+        ins, outs, held, sem = refs[:4], refs[4:-2], refs[-2], refs[-1]
         z, o, _ = plan.place()
-        for step, out in enumerate(outs, 1):
-            for k in range(plan.zn):
-                at = plan.column(there(z, k, plan.zn), there(o, step, plan.on), first)
-                for a, ref in enumerate(ins):
-                    out[k, a] = ref[:, pl.ds(at, width)]
-
-    out = [shape(plan.zn, 4, plan.rows, width)] * (plan.on - 1)
-    return call_mover(body, arrays, out, "pack_outer")
-
-
-def pack_heads(plan, arrays, received, first, width):
+        copies = [pltpu.make_async_copy(ref, held.at[a], sem.at[a]) for a, ref in enumerate(ins)]
+        for copy in copies:
+            copy.start()
+        for copy in copies:
+            copy.wait()
+        n = 0
+        for first, heads in chunks:
+            for step in range(plan.on):
+                for k in range(plan.zn):
+                    at = plan.column(there(z, k, plan.zn), there(o, step, plan.on), first)
+                    outs[n][k] = held[:, :, pl.ds(at, heads * HD)]
+                n += 1
+
+    out = [
+        shape(plan.zn, 4, plan.rows, heads * HD) for _, heads in chunks for _ in range(plan.on)
+    ]
+    total = sum(math.prod(s.shape) * 2 for s in out)
+    return pl.pallas_call(
+        body,
+        out_shape=out,
+        in_specs=[HBM] * 4,
+        out_specs=[VMEM] * len(out),
+        scratch_shapes=[
+            pltpu.VMEM((4, *arrays[0].shape), BF16),
+            pltpu.SemaphoreType.DMA((4,)),
+        ],
+        compiler_params=pltpu.CompilerParams(vmem_limit_bytes=VMEM_LIMIT),
+        cost_estimate=SMALL,
+        name="pack_all",
+    )(*[pltpu.with_memory_space_constraint(a, pltpu.HBM) for a in arrays])
+
+
+def pack_heads(plan, groups, width, weight=SMALL):
     def body(*refs):
-        ins, got = refs[:4], refs[4 : 4 + len(received)]
-        z, o, _ = plan.place()
-        for k, out in enumerate(refs[4 + len(received) :]):
-            at = plan.column(there(z, k, plan.zn), o, first)
-            for a, ref in enumerate(ins):
-                out[0, a] = ref[:, pl.ds(at, width)]
-            for step, ref in enumerate(got, 1):
+        ins, outs = refs[: len(groups)], refs[len(groups) :]
+        for k, out in zip(plan.steps, outs, strict=True):
+            for step, ref in enumerate(ins):
                 out[step] = ref[k]
 
-    out = [shape(plan.on, 4, plan.rows, width)] * plan.zn
-    return call_mover(body, [*arrays, *received], out, "pack_heads")
-
-
-def join_rows(plan, pieces, width):
+    out = [shape(len(groups), 4, plan.rows, width)] * plan.zn
+    return call_mover(body, groups, out, "pack_heads", weight)
+
+
+def join_rows(plan, sets, width):
     def body(*refs):
-        ins, (qg, kv) = refs[: plan.zn], refs[plan.zn :]
+        ins, (qg, kv) = refs[:-2], refs[-2:]
         z = lax.axis_index("head")
-        for k, ref in enumerate(ins):
-            row = back(z, k, plan.zn) * plan.rows
-            for step in range(plan.on):
-                at = pl.ds(pl.multiple_of(step * plan.slab + row, plan.rows), plan.rows)
+        for n, ref in enumerate(ins):
+            start = sum(s[0].shape[0] for s in sets[: n // plan.zn])
+            row = back(z, plan.steps[n % plan.zn], plan.zn) * plan.rows
+            for step in range(ref.shape[0]):
+                at = (start + step) * plan.slab + row
+                at = pl.ds(pl.multiple_of(at, plan.rows), plan.rows)
                 for a in range(2):
                     qg[a, at], kv[a, at] = ref[step, a], ref[step, 2 + a]
 
     out = [shape(2, plan.tq, width)] * 2
-    return call_mover(body, pieces, out, "join_rows")
+    return call_mover(body, [a for s in sets for a in s], out, "join_rows")
 
 
 def attend_body(plan, first, heads, *refs):
@@ -221,84 +245,180 @@
             pltpu.VMEM((plan.tk, HD), F32),
         ],
         compiler_params=pltpu.CompilerParams(vmem_limit_bytes=VMEM_LIMIT),
-        cost_estimate=pl.CostEstimate(
-            flops=12 * heads * plan.tq * plan.tk * HD * 4,
-            bytes_accessed=2 * width * (4 * plan.tq + 6 * plan.tk),
-            transcendentals=heads * plan.tq * plan.tk,
-        ),
+        cost_estimate=SMALL,
         name="attend",
     )(mask, qg, *kvs)
 
 
-def add_parts(plan, own, parts, width):
+def add_parts(plan, own, parts, row_parts, width):
     def body(*refs):
         total = refs[0][...]
         for ref in refs[1 : 1 + len(parts)]:
             total += ref[...].astype(F32)
-        for step, out in enumerate(refs[1 + len(parts) :]):
-            out[...] = total[:, step * plan.slab : (step + 1) * plan.slab].astype(BF16)
+        rows = refs[1 + len(parts) : 1 + len(parts) + len(row_parts)]
+        for step, out in enumerate(refs[1 + len(parts) + len(rows) :]):
+            at = slice(step * plan.slab, (step + 1) * plan.slab)
+            if rows:
+                out[:2] = rows[step][...]
+                out[2:] = total[:, at].astype(BF16)
+            else:
+                out[...] = total[:, at].astype(BF16)
 
     return pl.pallas_call(
         body,
-        out_shape=[shape(2, plan.slab, width)] * plan.on,
-        in_specs=[VMEM] * (1 + len(parts)),
+        out_shape=[shape(4 if row_parts else 2, plan.slab, width)] * plan.on,
+        in_specs=[VMEM] * (1 + len(parts) + len(row_parts)),
         out_specs=[VMEM] * plan.on,
         compiler_params=pltpu.CompilerParams(vmem_limit_bytes=VMEM_LIMIT),
         cost_estimate=pl.CostEstimate(
-            flops=2 * plan.tq * width * len(parts),
-            bytes_accessed=2 * plan.tq * width * (6 + 2 * len(parts)),
+            flops=2 * plan.tq * HD * len(parts),
+            bytes_accessed=2 * plan.tq * HD * (8 + 2 * len(parts)),
             transcendentals=0,
         ),
         name="add_parts",
-    )(own, *parts)
-
-
-def place_all(plan, pieces):
+    )(own, *parts, *row_parts)
+
+
+def place(plan, pieces, first, heads, outs):
     def body(*refs):
-        ins, outs = refs[: len(pieces)], refs[len(pieces) :]
+        ins, sem = refs[: len(pieces)], refs[-1]
+        targets = refs[-5:-1]
         _, o, _ = plan.place()
-        for ref, (step, first, heads, which, _) in zip(ins, pieces, strict=True):
+        copies = []
+        for ref, (step, which, _) in zip(ins, pieces, strict=True):
             at = pl.multiple_of((there(o, step, plan.on) * plan.mine + first) * HD, HD)
-            for a in range(2):
-                outs[which + a][:, pl.ds(at, heads * HD)] = ref[a]
+            for a in range(ref.shape[0]):
+                target = targets[which + a].at[:, pl.ds(at, heads * HD)]
+                copies.append(pltpu.make_async_copy(ref.at[a], target, sem.at[len(copies)]))
+        for copy in copies:
+            copy.start()
+        for copy in copies:
+            copy.wait()
 
     out = [shape(plan.slab, plan.groups * HD)] * 4
-    return call_mover(body, [p[-1] for p in pieces], out, "place_all")
-
-
-def chunk_sizes(plan):
-    return [1] * plan.mine
+    return pl.pallas_call(
+        body,
+        out_shape=out,
+        in_specs=[VMEM] * len(pieces) + [HBM] * len(outs),
+        out_specs=[HBM] * 4,
+        input_output_aliases={len(pieces) + n: n for n in range(len(outs))},
+        scratch_shapes=[pltpu.SemaphoreType.DMA((4 * plan.on,))],
+        compiler_params=pltpu.CompilerParams(vmem_limit_bytes=VMEM_LIMIT),
+        cost_estimate=LARGE,
+        name="place",
+    )(*[p[-1] for p in pieces], *outs)
+
+
+def chunk_list(plan):
+    sizes = [2] * (plan.mine // 2) + [1] * (plan.mine % 2)
+    return [(sum(sizes[:n]), size) for n, size in enumerate(sizes)]
+
+
+def after(arrays, others):
+    if not others:
+        return list(arrays)
+    return list(lax.optimization_barrier((tuple(arrays), tuple(others)))[0])
+
+
+class Queue:
+    def __init__(self, plan, window):
+        self.plan, self.window, self.results = plan, window, []
+
+    def send(self, array, others=(), **steps):
+        waits = list(others)
+        if len(self.results) >= self.window:
+            waits.append(self.results[-self.window])
+        result = self.plan.send(after([array], waits)[0], **steps)
+        self.results.append(result)
+        return result
+
+
+class Line:
+    def __init__(self):
+        self.last = ()
+
+    def tie(self, arrays):
+        return after(arrays, self.last)
+
+    def ran(self, results):
+        self.last = (results[-1],)
+        return results
 
 
 def local(queries, keys, values, out_grad, tile_mask):
     plan = Plan(*queries.shape, lax.axis_size("head"), lax.axis_size("frame"))
-    arrays = (queries, out_grad, keys, values)
-    pieces = []
-    first = 0
-    for heads in chunk_sizes(plan):
-        width = heads * HD
-        received = []
-        if plan.on > 1:
-            outgoing = pack_outer(plan, arrays, first, width)
-            received = [plan.send(a, o_step=s) for s, a in enumerate(outgoing, 1)]
-        packed = pack_heads(plan, arrays, received, first, width)
-        rows = [packed[0]] + [plan.send(a, z_step=k) for k, a in enumerate(packed) if k]
-        qg, kv = join_rows(plan, rows, width)
-        kvs = [kv] + [plan.send(kv, i_step=m) for m in range(1, plan.inn)]
-        results = attend(plan, tile_mask, qg, kvs, first, heads)
+    chunks = chunk_list(plan)
+    line, outer, depth = Line(), Queue(plan, 3), Queue(plan, 3)
+    packed = line.ran(pack_all(plan, (queries, out_grad, keys, values), chunks))
+    packed = [packed[n * plan.on : (n + 1) * plan.on] for n in range(len(chunks))]
+    received = []
+
+    def fetch(n):
+        received.append([outer.send(a, o_step=s) for s, a in enumerate(packed[n][1:], 1)])
+
+    def exchange(n, group, weight=SMALL):
+        heads = chunks[n][1]
+        ready = line.ran(pack_heads(plan, line.tie(group), heads * HD, weight))
+        moved = [depth.send(a, z_step=k) for k, a in zip(plan.steps[1:], ready[1:], strict=True)]
+        return [ready[0], *moved]
+
+    def join(n):
+        rows = [line.tie(arrived[n][0]), *arrived[n][1:]]
+        qg, kv = line.ran(join_rows(plan, rows, chunks[n][1] * HD))
+        return qg, [kv] + [plan.send(kv, i_step=m) for m in range(1, plan.inn)]
+
+    def work(n):
+        first, heads = chunks[n]
+        qg, kvs = joined[n]
+        tied = line.tie([qg])[0]
+        results = line.ran(attend(plan, tile_mask, tied, kvs, first, heads))
         row_parts, key_parts = results[: plan.on], results[plan.on :]
-        parts = [
-            plan.send(a, i_step=m, returning=True) for m, a in enumerate(key_parts) if m
-        ]
-        key_sums = add_parts(plan, key_parts[0], parts, width)
-        for which, group in ((0, row_parts), (2, key_sums)):
-            for step, array in enumerate(group):
-                if step:
-                    array = plan.send(array, o_step=step, returning=True)
-                pieces.append((step, first, heads, which, array))
-        first += heads
-    attended, query_grad, key_grad, value_grad = place_all(plan, pieces)
-    return attended, query_grad, key_grad, value_grad
+        parts = [plan.send(a, i_step=m, returning=True) for m, a in enumerate(key_parts) if m]
+        return row_parts, key_parts[0], parts
+
+    def give_back(group):
+        return [outer.send(a, o_step=s, returning=True) if s else a for s, a in enumerate(group)]
+
+    def sums(n, row_parts, own, parts, together):
+        width = chunks[n][1] * HD
+        together = row_parts if together else []
+        both = line.ran(add_parts(plan, line.tie([own])[0], parts, together, width))
+        groups = [give_back(both)] if together else [row_parts, give_back(both)]
+        return [(s, 2 * w, a) for w, group in enumerate(groups) for s, a in enumerate(group)]
+
+    def put(n, pieces, outs):
+        step, which, array = pieces[0]
+        pieces = [(step, which, line.tie([array])[0]), *pieces[1:]]
+        return line.ran(place(plan, pieces, *chunks[n], outs))
+
+    last = len(chunks) - 1
+    arrived, joined, pieces, outs = [], [], [], []
+    fetch(0)
+    if last:
+        fetch(1)
+    arrived.append([exchange(0, [packed[0][0]])])
+    if plan.on > 1:
+        arrived[0].append(exchange(0, received[0]))
+    if last:
+        arrived.append([exchange(1, [packed[1][0], *received[1]])])
+    joined.append(join(0))
+    for n in range(last):
+        if n + 2 <= last:
+            fetch(n + 2)
+        results = work(n)
+        joined.append(join(n + 1))
+        if n + 2 <= last:
+            arrived.append([exchange(n + 2, [packed[n + 2][0], *received[n + 2]], LARGE)])
+        if n:
+            outs = put(n - 1, pieces[n - 1], outs)
+        pieces.append(sums(n, *results, True))
+    row_parts, own, parts = work(last)
+    row_parts = give_back(row_parts)
+    final = sums(last, row_parts, own, parts, False)
+    if last:
+        outs = put(last - 1, pieces[last - 1], outs)
+    outs = put(last, final, outs)
+    return tuple(outs)
 
 
 def solution(mesh):

time: 138 us -> 95.6 us (0.69)
  starting transfers between devices: 63.6 us -> 28.7 us
  waiting for transfers between devices: 45.8 us -> 41.2 us
  local copies, waits for them, and re-layouts: 4.47 us -> 0.12 us
  Pallas kernels: 22.6 us -> 24.6 us
    ppermute x40 -> x25, starting transfers between devices: 63.6 us -> 28.7 us  [send(): return lax.ppermute(array, ('head', 'frame'), pairs)]
    pallas_call x5 -> x7, Pallas kernels: 0.24 us -> 5.39 us  [the longest x3 2.89 us: place(): pl.pallas_call(body, out_shape=out, in_specs=[VMEM] * len(pieces) + [HBM]...]
    ppermute x40 -> x25, waiting for transfers between devices: 45.8 us -> 41.2 us  [send(): return lax.ppermute(array, ('head', 'frame'), pairs)]
    unnamed x15 -> x3, local copies, waits for them, and re-layouts: 4.47 us -> 0.12 us
    pallas_call x5 -> x3, Pallas kernels: 19.4 us -> 17 us  [attend(): pl.pallas_call(functools.partial(attend_body, plan, first, heads), out_sh...]
    pallas_call x16 -> x7, Pallas kernels: 2.98 us -> 2.13 us  [call_mover(): pl.pallas_call(body, out_shape=out_shape, in_specs=[VMEM] * len(operands)...]
  transfers between devices with their start and end apart: 40 -> 25, of which waited for: 19 -> 9; matrix products, arithmetic and copies ran while one was open for 0% -> 0% of each run, Pallas kernels for 15% -> 23%
where the time goes in v2:
time: 95.6 us; the launch traced here: 95.4 us
  waiting for transfers between devices  41.2 us (43%)
  starting transfers between devices  28.7 us (30%)
  Pallas kernels  24.6 us (26%)
    ppermute x25, waiting for transfers between devices, send(): return lax.ppermute(array, ('head', 'frame'), pairs)  41.2 us
    ppermute x25, starting transfers between devices, send(): return lax.ppermute(array, ('head', 'frame'), pairs)  28.7 us
    pallas_call x3, Pallas kernels, attend(): pl.pallas_call(functools.partial(attend_body, plan, first, heads), out_sh...  17 us
    pallas_call x3, Pallas kernels, place(): pl.pallas_call(body, out_shape=out, in_specs=[VMEM] * len(pieces) + [HBM]...  2.89 us
    pallas_call x7, Pallas kernels, call_mover(): pl.pallas_call(body, out_shape=out_shape, in_specs=[VMEM] * len(operands)...  2.13 us
    pallas_call x1, Pallas kernels, pack_all(): pl.pallas_call(body, out_shape=out, in_specs=[HBM] * 4, out_specs=[VMEM]...  2.12 us
  transfers between devices with their start and end apart: 25, of which 9 were waited for; matrix products, arithmetic and copies ran while one was open for 0% of the time, Pallas kernels for 23%

profile of v2, /device:TPU:0, one launch (start us, length us, event | category | flops | bytes accessed | tf_op | source)
XLA Modules:
  0.0 95.4 jit_solution(14310623937576414943)
XLA Ops:
  0.6 2.1 %pack_all.1 = (bf16[4,4,64,256]{3,2,1,0:T(8,128)(2,1)S(1)}, bf16[4,4,64,256]{3,2,1,0:T(8,128)(2,1)S(1)}, bf16[4,4,64,256]{3,2,1,0:T(8,128)(2,1)S(1)}, bf16[4,4,6...) custom-call(bf16[64,5120]{1,0:T(8,128)(2,1)} %refs_0_.4, ...), custom_call_target="tpu_custom_call" | custom-call | flops 1024 | bytes 1024 | tf_op jit(solution)/shard_map/pack_all/pallas_call | solution.py:107
  2.8 3.0 %collective-permute-start.2 = (bf16[4,4,64,256]{3,2,1,0:T(8,128)(2,1)S(1)}, bf16[4,4,64,256]{3,2,1,0:T(8,128)(2,1)S(1)}, u32[]{:S(2)}, u32[]{:S(2)}) collective-permute-start(bf16[4,4,64,256]{3,2,1,0:T(8,128)(2,1)S(1)} %get-tuple-element.102), channel_id=1, source_target_pairs={{0,2},{1,3},{2,0},{3,1},{4,6},{5,7},{6,4},{7,5},{8,10},{9,11},{10,... | collective-permute-start | bytes 1572872 | tf_op jit(solution)/shard_map/ppermute | solution.py:66
  5.9 4.1 %collective-permute-start.3 = (bf16[1,4,64,256]{3,2,1,0:T(8,128)(2,1)S(1)}, bf16[1,4,64,256]{3,2,1,0:T(8,128)(2,1)S(1)}, u32[]{:S(2)}, u32[]{:S(2)}) collective-permute-start(bf16[1,4,64,256]{3,2,1,0:T(8,128)(2,1)S(1)} %get-tuple-element.113), channel_id=1, source_target_pairs={{0,12},{1,13},{2,14},{3,15},{4,8},{5,9},{6,10},{7,11},{8,4},{9,5},... | collective-permute-start | bytes 393224 | tf_op jit(solution)/shard_map/ppermute | solution.py:66
  10.7 7.9 %collective-permute-done.2.refs_0_ = bf16[4,4,64,256]{3,2,1,0:T(8,128)(2,1)S(1)} collective-permute-done((bf16[4,4,64,256]{3,2,1,0:T(8,128)(2,1)S(1)}, bf16[4,4,64,256]{3,2,1,0:T(8,128)(2,1)S(1)}, u32[]{:S(2)}, u32[]{:S(2)}) %collective-permute-start.2) | collective-permute-done | bytes 524320 | tf_op jit(solution)/shard_map/ppermute | solution.py:66
  18.6 4.2 %collective-permute-start.4 = (bf16[1,4,64,256]{3,2,1,0:T(8,128)(2,1)S(1)}, bf16[1,4,64,256]{3,2,1,0:T(8,128)(2,1)S(1)}, u32[]{:S(2)}, u32[]{:S(2)}) collective-permute-start(bf16[1,4,64,256]{3,2,1,0:T(8,128)(2,1)S(1)} %get-tuple-element.114), channel_id=1, source_target_pairs={{0,12},{1,13},{2,14},{3,15},{4,8},{5,9},{6,10},{7,11},{8,4},{9,5},... | collective-permute-start | bytes 393224 | tf_op jit(solution)/shard_map/ppermute | solution.py:66
  23.6 5.4 %collective-permute-done.1.refs_1_ = bf16[4,4,64,256]{3,2,1,0:T(8,128)(2,1)S(1)} collective-permute-done((bf16[4,4,64,256]{3,2,1,0:T(8,128)(2,1)S(1)}, bf16[4,4,64,256]{3,2,1,0:T(8,128)(2,1)S(1)}, u32[]{:S(2)}, u32[]{:S(2)}) %collective-permute-start.1) | collective-permute-done | bytes 524320 | tf_op jit(solution)/shard_map/ppermute | solution.py:66
  29.8 2.0 %collective-permute-done.7.refs_6_ = bf16[1,4,64,256]{3,2,1,0:T(8,128)(2,1)S(1)} collective-permute-done((bf16[1,4,64,256]{3,2,1,0:T(8,128)(2,1)S(1)}, bf16[1,4,64,256]{3,2,1,0:T(8,128)(2,1)S(1)}, u32[]{:S(2)}, u32[]{:S(2)}) %collective-permute-start.7) | collective-permute-done | bytes 131104 | tf_op jit(solution)/shard_map/ppermute | solution.py:66
  32.0 2.6 %collective-permute-start.5 = (bf16[2,4,64,256]{3,2,1,0:T(8,128)(2,1)}, bf16[2,4,64,256]{3,2,1,0:T(8,128)(2,1)S(1)}, u32[]{:S(2)}, u32[]{:S(2)}) collective-permute-start(bf16[2,4,64,256]{3,2,1,0:T(8,128)(2,1)} %get-tuple-element.115), channel_id=1, source_target_pairs={{0,12},{1,13},{2,14},{3,15},{4,8},{5,9},{6,10},{7,11},{8,4},{9,5},... | collective-permute-start | bytes 786440 | tf_op jit(solution)/shard_map/ppermute | solution.py:66
  34.6 1.9 %collective-permute-start.11 = (bf16[2,4,64,256]{3,2,1,0:T(8,128)(2,1)S(1)}, bf16[2,4,64,256]{3,2,1,0:T(8,128)(2,1)S(1)}, u32[]{:S(2)}, u32[]{:S(2)}) collective-permute-start(bf16[2,4,64,256]{3,2,1,0:T(8,128)(2,1)S(1)} %get-tuple-element.123), channel_id=1, source_target_pairs={{0,4},{1,5},{2,6},{3,7},{4,0},{5,1},{6,2},{7,3},{8,12},{9,13},{10,... | collective-permute-start | bytes 786440 | tf_op jit(solution)/shard_map/ppermute | solution.py:66
  36.5 1.5 %collective-permute-start = (bf16[4,4,64,128]{3,2,1,0:T(8,128)(2,1)S(1)}, bf16[4,4,64,128]{3,2,1,0:T(8,128)(2,1)}, u32[]{:S(2)}, u32[]{:S(2)}) collective-permute-start(bf16[4,4,64,128]{3,2,1,0:T(8,128)(2,1)S(1)} %get-tuple-element.99), channel_id=1, source_target_pairs={{0,2},{1,3},{2,0},{3,1},{4,6},{5,7},{6,4},{7,5},{8,10},{9,11},{10,... | collective-permute-start | bytes 786440 | tf_op jit(solution)/shard_map/ppermute | solution.py:66
  38.1 6.6 %attend.3 = (bf16[2,256,256]{2,1,0:T(8,128)(2,1)S(1)}, bf16[2,256,256]{2,1,0:T(8,128)(2,1)S(1)}, f32[2,512,256]{2,1,0:T(8,128)S(1)}, bf16[2,512,256]{2,1,0:T(8,128)(2,1)S(1)}) custom-call(s32[10,8,8]{2,1,0:T(8,128)S(1)} %copy.19.refs_0_, bf16[2,512,256]{2,1,0:T(8,128)(2,1)S(1)} %get-tuple-element.130.refs_1_, ...), custom_call_target="tpu_custom_call" | custom-call | flops 1024 | bytes 1024 | tf_op jit(solution)/shard_map/attend/pallas_call | solution.py:233
  44.8 12.3 %collective-permute-done.8.refs_2_ = bf16[2,4,64,256]{3,2,1,0:T(8,128)(2,1)S(1)} collective-permute-done((bf16[2,4,64,256]{3,2,1,0:T(8,128)(2,1)}, bf16[2,4,64,256]{3,2,1,0:T(8,128)(2,1)S(1)}, u32[]{:S(2)}, u32[]{:S(2)}) %collective-permute-start.8) | collective-permute-done | bytes 262176 | tf_op jit(solution)/shard_map/ppermute | solution.py:66
  58.4 1.6 %collective-permute-start.18 = (bf16[4,256,256]{2,1,0:T(8,128)(2,1)S(1)}, bf16[4,256,256]{2,1,0:T(8,128)(2,1)S(1)}, u32[]{:S(2)}, u32[]{:S(2)}) collective-permute-start(bf16[4,256,256]{2,1,0:T(8,128)(2,1)S(1)} %get-tuple-element.164), channel_id=1, source_target_pairs={{0,2},{1,3},{2,0},{3,1},{4,6},{5,7},{6,4},{7,5},{8,10},{9,11},{10,... | collective-permute-start | bytes 1572872 | tf_op jit(solution)/shard_map/ppermute | solution.py:66
  60.0 2.4 %collective-permute-start.13 = (bf16[2,4,64,128]{3,2,1,0:T(8,128)(2,1)S(1)}, bf16[2,4,64,128]{3,2,1,0:T(8,128)(2,1)S(1)}, u32[]{:S(2)}, u32[]{:S(2)}) collective-permute-start(bf16[2,4,64,128]{3,2,1,0:T(8,128)(2,1)S(1)} %get-tuple-element.142), channel_id=1, source_target_pairs={{0,12},{1,13},{2,14},{3,15},{4,8},{5,9},{6,10},{7,11},{8,4},{9,5},... | collective-permute-start | bytes 393224 | tf_op jit(solution)/shard_map/ppermute | solution.py:66
  62.4 2.0 %collective-permute-start.15 = (bf16[2,4,64,128]{3,2,1,0:T(8,128)(2,1)S(1)}, bf16[2,4,64,128]{3,2,1,0:T(8,128)(2,1)S(1)}, u32[]{:S(2)}, u32[]{:S(2)}) collective-permute-start(bf16[2,4,64,128]{3,2,1,0:T(8,128)(2,1)S(1)} %get-tuple-element.146), channel_id=1, source_target_pairs={{0,4},{1,5},{2,6},{3,7},{4,0},{5,1},{6,2},{7,3},{8,12},{9,13},{10,... | collective-permute-start | bytes 393224 | tf_op jit(solution)/shard_map/ppermute | solution.py:66
  64.4 6.6 %attend.4 = (bf16[2,256,256]{2,1,0:T(8,128)(2,1)S(1)}, bf16[2,256,256]{2,1,0:T(8,128)(2,1)S(1)}, f32[2,512,256]{2,1,0:T(8,128)S(1)}, bf16[2,512,256]{2,1,0:T(8,128)(2,1)S(1)}) custom-call(s32[10,8,8]{2,1,0:T(8,128)S(1)} %copy.19.refs_0_, bf16[2,512,256]{2,1,0:T(8,128)(2,1)S(1)} %get-tuple-element.153.refs_1_, ...), custom_call_target="tpu_custom_call" | custom-call | flops 1024 | bytes 1024 | tf_op jit(solution)/shard_map/attend/pallas_call | solution.py:233
  71.1 2.1 %collective-permute-done.14.refs_2_ = bf16[2,4,64,128]{3,2,1,0:T(8,128)(2,1)S(1)} collective-permute-done((bf16[2,4,64,128]{3,2,1,0:T(8,128)(2,1)S(1)}, bf16[2,4,64,128]{3,2,1,0:T(8,128)(2,1)S(1)}, u32[]{:S(2)}, u32[]{:S(2)}) %collective-permute-start.14) | collective-permute-done | bytes 131104 | tf_op jit(solution)/shard_map/ppermute | solution.py:66
  73.4 1.0 %place.3 = (bf16[256,1280]{1,0:T(8,128)(2,1)}, bf16[256,1280]{1,0:T(8,128)(2,1)}, bf16[256,1280]{1,0:T(8,128)(2,1)}, bf16[256,1280]{1,0:T(8,128)(2,1)}) custom-call(bf16[4,256,256]{2,1,0:T(8,128)(2,1)S(1)} %get-tuple-element.163.refs_0_, bf16[4,256,256]{2,1,0:T(8,128)(2,1)S(1)} %collective-permute-done.18.refs_1_), custom_call_target="tpu_custom_call" | custom-call | flops 8589934592 | bytes 1024 | tf_op jit(solution)/shard_map/place/pallas_call | solution.py:299
  75.6 3.8 %attend.5 = (bf16[2,256,128]{2,1,0:T(8,128)(2,1)S(1)}, bf16[2,256,128]{2,1,0:T(8,128)(2,1)S(1)}, f32[2,512,128]{2,1,0:T(8,128)S(1)}, bf16[2,512,128]{2,1,0:T(8,128)(2,1)S(1)}) custom-call(s32[10,8,8]{2,1,0:T(8,128)S(1)} %copy.19.refs_0_, bf16[2,512,128]{2,1,0:T(8,128)(2,1)S(1)} %get-tuple-element.170.refs_1_, ...), custom_call_target="tpu_custom_call" | custom-call | flops 1024 | bytes 1024 | tf_op jit(solution)/shard_map/attend/pallas_call | solution.py:233
  79.5 1.2 %collective-permute-start.23 = (bf16[2,256,128]{2,1,0:T(8,128)(2,1)S(1)}, bf16[2,256,128]{2,1,0:T(8,128)(2,1)S(1)}, u32[]{:S(2)}, u32[]{:S(2)}) collective-permute-start(bf16[2,256,128]{2,1,0:T(8,128)(2,1)S(1)} %get-tuple-element.185), channel_id=1, source_target_pairs={{0,2},{1,3},{2,0},{3,1},{4,6},{5,7},{6,4},{7,5},{8,10},{9,11},{10,... | collective-permute-start | bytes 393224 | tf_op jit(solution)/shard_map/ppermute | solution.py:66
  81.1 1.2 %collective-permute-start.24 = (bf16[2,256,128]{2,1,0:T(8,128)(2,1)S(1)}, bf16[2,256,128]{2,1,0:T(8,128)(2,1)S(1)}, u32[]{:S(2)}, u32[]{:S(2)}) collective-permute-start(bf16[2,256,128]{2,1,0:T(8,128)(2,1)S(1)} %get-tuple-element.187), channel_id=1, source_target_pairs={{0,2},{1,3},{2,0},{3,1},{4,6},{5,7},{6,4},{7,5},{8,10},{9,11},{10,... | collective-permute-start | bytes 393224 | tf_op jit(solution)/shard_map/ppermute | solution.py:66
  82.3 7.1 %collective-permute-done.22.refs_1_ = bf16[4,256,256]{2,1,0:T(8,128)(2,1)S(1)} collective-permute-done((bf16[4,256,256]{2,1,0:T(8,128)(2,1)S(1)}, bf16[4,256,256]{2,1,0:T(8,128)(2,1)S(1)}, u32[]{:S(2)}, u32[]{:S(2)}) %collective-permute-start.22) | collective-permute-done | bytes 524320 | tf_op jit(solution)/shard_map/ppermute | solution.py:66
  90.5 1.8 %collective-permute-done.23.refs_1_ = bf16[2,256,128]{2,1,0:T(8,128)(2,1)S(1)} collective-permute-done((bf16[2,256,128]{2,1,0:T(8,128)(2,1)S(1)}, bf16[2,256,128]{2,1,0:T(8,128)(2,1)S(1)}, u32[]{:S(2)}, u32[]{:S(2)}) %collective-permute-start.23) | collective-permute-done | bytes 131104 | tf_op jit(solution)/shard_map/ppermute | solution.py:66
  92.3 2.3 %collective-permute-done.24.refs_3_ = bf16[2,256,128]{2,1,0:T(8,128)(2,1)S(1)} collective-permute-done((bf16[2,256,128]{2,1,0:T(8,128)(2,1)S(1)}, bf16[2,256,128]{2,1,0:T(8,128)(2,1)S(1)}, u32[]{:S(2)}, u32[]{:S(2)}) %collective-permute-start.24) | collective-permute-done | bytes 131104 | tf_op jit(solution)/shard_map/ppermute | solution.py:66
  (46 shorter events, 7.8 us)
Async XLA Ops:
  2.8 15.8 %collective-permute-start.2 = (bf16[4,4,64,256]{3,2,1,0:T(8,128)(2,1)S(1)}, bf16[4,4,64,256]{3,2,1,0:T(8,128)(2,1)S(1)}, u32[]{:S(2)}, u32[]{:S(2)}) collective-permute-start(bf16[4,4,64,256]{3,2,1,0:T(8,128)(2,1)S(1)} %get-tuple-element.102), channel_id=1, source_target_pairs={{0,2},{1,3},{2,0},{3,1},{4,6},{5,7},{6,4},{7,5},{8,10},{9,11},{10,... | collective-permute-start | bytes 1572872 | tf_op jit(solution)/shard_map/ppermute | solution.py:66
  5.8 23.2 %collective-permute-start.1 = (bf16[4,4,64,256]{3,2,1,0:T(8,128)(2,1)S(1)}, bf16[4,4,64,256]{3,2,1,0:T(8,128)(2,1)S(1)}, u32[]{:S(2)}, u32[]{:S(2)}) collective-permute-start(bf16[4,4,64,256]{3,2,1,0:T(8,128)(2,1)S(1)} %get-tuple-element.101), channel_id=1, source_target_pairs={{0,2},{1,3},{2,0},{3,1},{4,6},{5,7},{6,4},{7,5},{8,10},{9,11},{10,... | collective-permute-start | bytes 1572872 | tf_op jit(solution)/shard_map/ppermute | solution.py:66
  5.9 12.7 %collective-permute-start.3 = (bf16[1,4,64,256]{3,2,1,0:T(8,128)(2,1)S(1)}, bf16[1,4,64,256]{3,2,1,0:T(8,128)(2,1)S(1)}, u32[]{:S(2)}, u32[]{:S(2)}) collective-permute-start(bf16[1,4,64,256]{3,2,1,0:T(8,128)(2,1)S(1)} %get-tuple-element.113), channel_id=1, source_target_pairs={{0,12},{1,13},{2,14},{3,15},{4,8},{5,9},{6,10},{7,11},{8,4},{9,5},... | collective-permute-start | bytes 393224 | tf_op jit(solution)/shard_map/ppermute | solution.py:66
  10.0 12.8 %collective-permute-start.6 = (bf16[1,4,64,256]{3,2,1,0:T(8,128)(2,1)S(1)}, bf16[1,4,64,256]{3,2,1,0:T(8,128)(2,1)S(1)}, u32[]{:S(2)}, u32[]{:S(2)}) collective-permute-start(bf16[1,4,64,256]{3,2,1,0:T(8,128)(2,1)S(1)} %get-tuple-element.118), channel_id=1, source_target_pairs={{0,8},{1,9},{2,10},{3,11},{4,12},{5,13},{6,14},{7,15},{8,0},{9,1},... | collective-permute-start | bytes 393224 | tf_op jit(solution)/shard_map/ppermute | solution.py:66
  10.0 12.8 %collective-permute-start.9 = (bf16[1,4,64,256]{3,2,1,0:T(8,128)(2,1)S(1)}, bf16[1,4,64,256]{3,2,1,0:T(8,128)(2,1)S(1)}, u32[]{:S(2)}, u32[]{:S(2)}) collective-permute-start(bf16[1,4,64,256]{3,2,1,0:T(8,128)(2,1)S(1)} %get-tuple-element.105), channel_id=1, source_target_pairs={{0,4},{1,5},{2,6},{3,7},{4,0},{5,1},{6,2},{7,3},{8,12},{9,13},{10,... | collective-permute-start | bytes 393224 | tf_op jit(solution)/shard_map/ppermute | solution.py:66
  18.6 11.2 %collective-permute-start.4 = (bf16[1,4,64,256]{3,2,1,0:T(8,128)(2,1)S(1)}, bf16[1,4,64,256]{3,2,1,0:T(8,128)(2,1)S(1)}, u32[]{:S(2)}, u32[]{:S(2)}) collective-permute-start(bf16[1,4,64,256]{3,2,1,0:T(8,128)(2,1)S(1)} %get-tuple-element.114), channel_id=1, source_target_pairs={{0,12},{1,13},{2,14},{3,15},{4,8},{5,9},{6,10},{7,11},{8,4},{9,5},... | collective-permute-start | bytes 393224 | tf_op jit(solution)/shard_map/ppermute | solution.py:66
  22.8 9.1 %collective-permute-start.7 = (bf16[1,4,64,256]{3,2,1,0:T(8,128)(2,1)S(1)}, bf16[1,4,64,256]{3,2,1,0:T(8,128)(2,1)S(1)}, u32[]{:S(2)}, u32[]{:S(2)}) collective-permute-start(bf16[1,4,64,256]{3,2,1,0:T(8,128)(2,1)S(1)} %get-tuple-element.119), channel_id=1, source_target_pairs={{0,8},{1,9},{2,10},{3,11},{4,12},{5,13},{6,14},{7,15},{8,0},{9,1},... | collective-permute-start | bytes 393224 | tf_op jit(solution)/shard_map/ppermute | solution.py:66
  22.8 9.0 %collective-permute-start.10 = (bf16[1,4,64,256]{3,2,1,0:T(8,128)(2,1)S(1)}, bf16[1,4,64,256]{3,2,1,0:T(8,128)(2,1)S(1)}, u32[]{:S(2)}, u32[]{:S(2)}) collective-permute-start(bf16[1,4,64,256]{3,2,1,0:T(8,128)(2,1)S(1)} %get-tuple-element.122), channel_id=1, source_target_pairs={{0,4},{1,5},{2,6},{3,7},{4,0},{5,1},{6,2},{7,3},{8,12},{9,13},{10,... | collective-permute-start | bytes 393224 | tf_op jit(solution)/shard_map/ppermute | solution.py:66
  32.0 6.2 %collective-permute-start.12 = (bf16[2,512,256]{2,1,0:T(8,128)(2,1)S(1)}, bf16[2,512,256]{2,1,0:T(8,128)(2,1)S(1)}, u32[]{:S(2)}, u32[]{:S(2)}) collective-permute-start(bf16[2,512,256]{2,1,0:T(8,128)(2,1)S(1)} %get-tuple-element.131.refs_2_), channel_id=1, source_target_pairs={{0,1},{1,0},{2,3},{3,2},{4,5},{5,4},{6,7},{7,6},{8,9},{9,8},{10,11... | collective-permute-start | bytes 1572872 | tf_op jit(solution)/shard_map/ppermute | solution.py:66
  32.0 12.8 %collective-permute-start.5 = (bf16[2,4,64,256]{3,2,1,0:T(8,128)(2,1)}, bf16[2,4,64,256]{3,2,1,0:T(8,128)(2,1)S(1)}, u32[]{:S(2)}, u32[]{:S(2)}) collective-permute-start(bf16[2,4,64,256]{3,2,1,0:T(8,128)(2,1)} %get-tuple-element.115), channel_id=1, source_target_pairs={{0,12},{1,13},{2,14},{3,15},{4,8},{5,9},{6,10},{7,11},{8,4},{9,5},... | collective-permute-start | bytes 786440 | tf_op jit(solution)/shard_map/ppermute | solution.py:66
  34.6 22.5 %collective-permute-start.8 = (bf16[2,4,64,256]{3,2,1,0:T(8,128)(2,1)}, bf16[2,4,64,256]{3,2,1,0:T(8,128)(2,1)S(1)}, u32[]{:S(2)}, u32[]{:S(2)}) collective-permute-start(bf16[2,4,64,256]{3,2,1,0:T(8,128)(2,1)} %get-tuple-element.120), channel_id=1, source_target_pairs={{0,8},{1,9},{2,10},{3,11},{4,12},{5,13},{6,14},{7,15},{8,0},{9,1},... | collective-permute-start | bytes 786440 | tf_op jit(solution)/shard_map/ppermute | solution.py:66
  34.6 22.5 %collective-permute-start.11 = (bf16[2,4,64,256]{3,2,1,0:T(8,128)(2,1)S(1)}, bf16[2,4,64,256]{3,2,1,0:T(8,128)(2,1)S(1)}, u32[]{:S(2)}, u32[]{:S(2)}) collective-permute-start(bf16[2,4,64,256]{3,2,1,0:T(8,128)(2,1)S(1)} %get-tuple-element.123), channel_id=1, source_target_pairs={{0,4},{1,5},{2,6},{3,7},{4,0},{5,1},{6,2},{7,3},{8,12},{9,13},{10,... | collective-permute-start | bytes 786440 | tf_op jit(solution)/shard_map/ppermute | solution.py:66
  36.5 20.8 %collective-permute-start = (bf16[4,4,64,128]{3,2,1,0:T(8,128)(2,1)S(1)}, bf16[4,4,64,128]{3,2,1,0:T(8,128)(2,1)}, u32[]{:S(2)}, u32[]{:S(2)}) collective-permute-start(bf16[4,4,64,128]{3,2,1,0:T(8,128)(2,1)S(1)} %get-tuple-element.99), channel_id=1, source_target_pairs={{0,2},{1,3},{2,0},{3,1},{4,6},{5,7},{6,4},{7,5},{8,10},{9,11},{10,... | collective-permute-start | bytes 786440 | tf_op jit(solution)/shard_map/ppermute | solution.py:66
  44.7 13.5 %collective-permute-start.16 = (bf16[2,512,256]{2,1,0:T(8,128)(2,1)S(1)}, bf16[2,512,256]{2,1,0:T(8,128)(2,1)S(1)}, u32[]{:S(2)}, u32[]{:S(2)}) collective-permute-start(bf16[2,512,256]{2,1,0:T(8,128)(2,1)S(1)} %get-tuple-element.132), channel_id=1, source_target_pairs={{0,1},{1,0},{2,3},{3,2},{4,5},{5,4},{6,7},{7,6},{8,9},{9,8},{10,11... | collective-permute-start | bytes 1572872 | tf_op jit(solution)/shard_map/ppermute | solution.py:66
  57.2 7.2 %collective-permute-start.17 = (bf16[2,512,256]{2,1,0:T(8,128)(2,1)S(1)}, bf16[2,512,256]{2,1,0:T(8,128)(2,1)S(1)}, u32[]{:S(2)}, u32[]{:S(2)}) collective-permute-start(bf16[2,512,256]{2,1,0:T(8,128)(2,1)S(1)} %get-tuple-element.137.refs_2_), channel_id=1, source_target_pairs={{0,1},{1,0},{2,3},{3,2},{4,5},{5,4},{6,7},{7,6},{8,9},{9,8},{10,11... | collective-permute-start | bytes 1572872 | tf_op jit(solution)/shard_map/ppermute | solution.py:66
  58.4 15.0 %collective-permute-start.18 = (bf16[4,256,256]{2,1,0:T(8,128)(2,1)S(1)}, bf16[4,256,256]{2,1,0:T(8,128)(2,1)S(1)}, u32[]{:S(2)}, u32[]{:S(2)}) collective-permute-start(bf16[4,256,256]{2,1,0:T(8,128)(2,1)S(1)} %get-tuple-element.164), channel_id=1, source_target_pairs={{0,2},{1,3},{2,0},{3,1},{4,6},{5,7},{6,4},{7,5},{8,10},{9,11},{10,... | collective-permute-start | bytes 1572872 | tf_op jit(solution)/shard_map/ppermute | solution.py:66
  60.0 11.1 %collective-permute-start.13 = (bf16[2,4,64,128]{3,2,1,0:T(8,128)(2,1)S(1)}, bf16[2,4,64,128]{3,2,1,0:T(8,128)(2,1)S(1)}, u32[]{:S(2)}, u32[]{:S(2)}) collective-permute-start(bf16[2,4,64,128]{3,2,1,0:T(8,128)(2,1)S(1)} %get-tuple-element.142), channel_id=1, source_target_pairs={{0,12},{1,13},{2,14},{3,15},{4,8},{5,9},{6,10},{7,11},{8,4},{9,5},... | collective-permute-start | bytes 393224 | tf_op jit(solution)/shard_map/ppermute | solution.py:66
  62.4 10.8 %collective-permute-start.14 = (bf16[2,4,64,128]{3,2,1,0:T(8,128)(2,1)S(1)}, bf16[2,4,64,128]{3,2,1,0:T(8,128)(2,1)S(1)}, u32[]{:S(2)}, u32[]{:S(2)}) collective-permute-start(bf16[2,4,64,128]{3,2,1,0:T(8,128)(2,1)S(1)} %get-tuple-element.144), channel_id=1, source_target_pairs={{0,8},{1,9},{2,10},{3,11},{4,12},{5,13},{6,14},{7,15},{8,0},{9,1},... | collective-permute-start | bytes 393224 | tf_op jit(solution)/shard_map/ppermute | solution.py:66
  62.4 10.8 %collective-permute-start.15 = (bf16[2,4,64,128]{3,2,1,0:T(8,128)(2,1)S(1)}, bf16[2,4,64,128]{3,2,1,0:T(8,128)(2,1)S(1)}, u32[]{:S(2)}, u32[]{:S(2)}) collective-permute-start(bf16[2,4,64,128]{3,2,1,0:T(8,128)(2,1)S(1)} %get-tuple-element.146), channel_id=1, source_target_pairs={{0,4},{1,5},{2,6},{3,7},{4,0},{5,1},{6,2},{7,3},{8,12},{9,13},{10,... | collective-permute-start | bytes 393224 | tf_op jit(solution)/shard_map/ppermute | solution.py:66
  71.0 3.5 %collective-permute-start.19 = (bf16[2,512,256]{2,1,0:T(8,128)(2,1)S(1)}, bf16[2,512,256]{2,1,0:T(8,128)(2,1)S(1)}, u32[]{:S(2)}, u32[]{:S(2)}) collective-permute-start(bf16[2,512,256]{2,1,0:T(8,128)(2,1)S(1)} %get-tuple-element.154), channel_id=1, source_target_pairs={{0,1},{1,0},{2,3},{3,2},{4,5},{5,4},{6,7},{7,6},{8,9},{9,8},{10,11... | collective-permute-start | bytes 1572872 | tf_op jit(solution)/shard_map/ppermute | solution.py:66
  73.2 2.3 %collective-permute-start.20 = (bf16[2,512,128]{2,1,0:T(8,128)(2,1)S(1)}, bf16[2,512,128]{2,1,0:T(8,128)(2,1)S(1)}, u32[]{:S(2)}, u32[]{:S(2)}) collective-permute-start(bf16[2,512,128]{2,1,0:T(8,128)(2,1)S(1)} %get-tuple-element.162.refs_2_), channel_id=1, source_target_pairs={{0,1},{1,0},{2,3},{3,2},{4,5},{5,4},{6,7},{7,6},{8,9},{9,8},{10,11... | collective-permute-start | bytes 786440 | tf_op jit(solution)/shard_map/ppermute | solution.py:66
  74.6 14.8 %collective-permute-start.22 = (bf16[4,256,256]{2,1,0:T(8,128)(2,1)S(1)}, bf16[4,256,256]{2,1,0:T(8,128)(2,1)S(1)}, u32[]{:S(2)}, u32[]{:S(2)}) collective-permute-start(bf16[4,256,256]{2,1,0:T(8,128)(2,1)S(1)} %get-tuple-element.178), channel_id=1, source_target_pairs={{0,2},{1,3},{2,0},{3,1},{4,6},{5,7},{6,4},{7,5},{8,10},{9,11},{10,... | collective-permute-start | bytes 1572872 | tf_op jit(solution)/shard_map/ppermute | solution.py:66
  79.5 12.8 %collective-permute-start.23 = (bf16[2,256,128]{2,1,0:T(8,128)(2,1)S(1)}, bf16[2,256,128]{2,1,0:T(8,128)(2,1)S(1)}, u32[]{:S(2)}, u32[]{:S(2)}) collective-permute-start(bf16[2,256,128]{2,1,0:T(8,128)(2,1)S(1)} %get-tuple-element.185), channel_id=1, source_target_pairs={{0,2},{1,3},{2,0},{3,1},{4,6},{5,7},{6,4},{7,5},{8,10},{9,11},{10,... | collective-permute-start | bytes 393224 | tf_op jit(solution)/shard_map/ppermute | solution.py:66
  81.1 13.4 %collective-permute-start.24 = (bf16[2,256,128]{2,1,0:T(8,128)(2,1)S(1)}, bf16[2,256,128]{2,1,0:T(8,128)(2,1)S(1)}, u32[]{:S(2)}, u32[]{:S(2)}) collective-permute-start(bf16[2,256,128]{2,1,0:T(8,128)(2,1)S(1)} %get-tuple-element.187), channel_id=1, source_target_pairs={{0,2},{1,3},{2,0},{3,1},{4,6},{5,7},{6,4},{7,5},{8,10},{9,11},{10,... | collective-permute-start | bytes 393224 | tf_op jit(solution)/shard_map/ppermute | solution.py:66
  (2 other events, 7.8 us)

commit v3 on v2

--- a/solution.py
+++ b/solution.py
@@ -36,7 +36,7 @@
     def __init__(self, rows, width, head_axis, frame_axis):
         self.rows = rows
         self.zn = head_axis
-        self.steps = [0, 3, 2, 1] if head_axis == 4 else list(range(head_axis))
+        self.steps = [0, 1, 3, 2] if head_axis == 4 else list(range(head_axis))
         self.groups = width // HD // head_axis
         self.on = math.gcd(self.groups, frame_axis)
         self.inn = frame_axis // self.on
@@ -83,7 +83,7 @@
     )(*operands)
 
 
-def pack_all(plan, arrays, chunks):
+def pack_columns(plan, arrays, blocks):
     def body(*refs):
         ins, outs, held, sem = refs[:4], refs[4:-2], refs[-2], refs[-1]
         z, o, _ = plan.place()
@@ -92,18 +92,13 @@
             copy.start()
         for copy in copies:
             copy.wait()
-        n = 0
-        for first, heads in chunks:
-            for step in range(plan.on):
-                for k in range(plan.zn):
-                    at = plan.column(there(z, k, plan.zn), there(o, step, plan.on), first)
-                    outs[n][k] = held[:, :, pl.ds(at, heads * HD)]
-                n += 1
-
-    out = [
-        shape(plan.zn, 4, plan.rows, heads * HD) for _, heads in chunks for _ in range(plan.on)
-    ]
-    total = sum(math.prod(s.shape) * 2 for s in out)
+        for out, (step, first, heads) in zip(outs, blocks, strict=True):
+            for k in range(plan.zn):
+                at = plan.column(there(z, k, plan.zn), there(o, step, plan.on), first)
+                out[k] = held[:, :, pl.ds(at, heads * HD)]
+
+    out = [shape(plan.zn, 4, plan.rows, heads * HD) for _, _, heads in blocks]
+    arrays = [pltpu.with_memory_space_constraint(a, pltpu.HBM) for a in arrays]
     return pl.pallas_call(
         body,
         out_shape=out,
@@ -115,19 +110,19 @@
         ],
         compiler_params=pltpu.CompilerParams(vmem_limit_bytes=VMEM_LIMIT),
         cost_estimate=SMALL,
-        name="pack_all",
-    )(*[pltpu.with_memory_space_constraint(a, pltpu.HBM) for a in arrays])
+        name="pack_columns",
+    )(*arrays)
 
 
 def pack_heads(plan, groups, width, weight=SMALL):
     def body(*refs):
         ins, outs = refs[: len(groups)], refs[len(groups) :]
         for k, out in zip(plan.steps, outs, strict=True):
-            for step, ref in enumerate(ins):
-                out[step] = ref[k]
+            for step, (ref, (_, at)) in enumerate(zip(ins, groups, strict=True)):
+                out[step] = ref[k, :, :, at : at + width]
 
     out = [shape(len(groups), 4, plan.rows, width)] * plan.zn
-    return call_mover(body, groups, out, "pack_heads", weight)
+    return call_mover(body, [array for array, _ in groups], out, "pack_heads", weight)
 
 
 def join_rows(plan, sets, width):
@@ -147,11 +142,11 @@
     return call_mover(body, [a for s in sets for a in s], out, "join_rows")
 
 
-def attend_body(plan, first, heads, *refs):
+def attend_body(plan, first, heads, split, *refs):
     mask, qg, kvs = refs[0], refs[1], refs[2 : 2 + plan.inn]
     rest = refs[2 + plan.inn :]
-    row_outs, key_outs = rest[: plan.on], rest[plan.on : plan.on + plan.inn]
-    key_t, value_t, scores, weights, grads, key_acc, value_acc = rest[plan.on + plan.inn :]
+    row_outs, key_outs = rest[: plan.on], rest[plan.on : -7]
+    key_t, value_t, scores, weights, grads, key_acc, value_acc = rest[-7:]
     _, o, i = plan.place()
     scaling = 1.0 / math.sqrt(HD)
     slab, tiles = plan.slab, plan.slab // TILE
@@ -216,22 +211,31 @@
             if q_step < plan.on - 1:
                 key_acc[...], value_acc[...] = key_part, value_part
             else:
-                for m, out in enumerate(key_outs):
+                for m in range(plan.inn):
                     mine = slice(m * plan.tq, (m + 1) * plan.tq)
-                    out[0, :, cols] = (key_part[mine] * scaling).astype(out.dtype)
-                    out[1, :, cols] = value_part[mine].astype(out.dtype)
+                    parts = (key_part[mine] * scaling, value_part[mine])
+                    if m and split:
+                        for out, part in zip(key_outs[2 * m - 1 : 2 * m + 1], parts, strict=True):
+                            out[:, cols] = part.astype(out.dtype)
+                    else:
+                        out = key_outs[m]
+                        out[0, :, cols] = parts[0].astype(out.dtype)
+                        out[1, :, cols] = parts[1].astype(out.dtype)
         return carry
 
     lax.fori_loop(0, heads, one_head, 0)
 
 
-def attend(plan, mask, qg, kvs, first, heads):
+def attend(plan, mask, qg, kvs, first, heads, split):
     width = heads * HD
     out = [shape(2, plan.slab, width)] * plan.on
     out += [shape(2, plan.tq, width, dtype=F32)]
-    out += [shape(2, plan.tq, width)] * (plan.inn - 1)
+    if split:
+        out += [shape(plan.tq, width)] * (2 * plan.inn - 2)
+    else:
+        out += [shape(2, plan.tq, width)] * (plan.inn - 1)
     return pl.pallas_call(
-        functools.partial(attend_body, plan, first, heads),
+        functools.partial(attend_body, plan, first, heads, split),
         out_shape=out,
         in_specs=[SMEM] + [VMEM] * (1 + plan.inn),
         out_specs=[VMEM] * len(out),
@@ -252,17 +256,19 @@
 
 def add_parts(plan, own, parts, row_parts, width):
     def body(*refs):
-        total = refs[0][...]
-        for ref in refs[1 : 1 + len(parts)]:
-            total += ref[...].astype(F32)
+        total = [refs[0][0], refs[0][1]]
+        for n, ref in enumerate(refs[1 : 1 + len(parts)]):
+            if len(ref.shape) == 2:
+                total[n % 2] += ref[...].astype(F32)
+            else:
+                total = [part + ref[a].astype(F32) for a, part in enumerate(total)]
         rows = refs[1 + len(parts) : 1 + len(parts) + len(row_parts)]
         for step, out in enumerate(refs[1 + len(parts) + len(rows) :]):
             at = slice(step * plan.slab, (step + 1) * plan.slab)
             if rows:
                 out[:2] = rows[step][...]
-                out[2:] = total[:, at].astype(BF16)
-            else:
-                out[...] = total[:, at].astype(BF16)
+            for a, part in enumerate(total):
+                out[2 * (len(rows) > 0) + a] = part[at].astype(BF16)
 
     return pl.pallas_call(
         body,
@@ -310,8 +316,14 @@
 
 
 def chunk_list(plan):
-    sizes = [2] * (plan.mine // 2) + [1] * (plan.mine % 2)
+    sizes = [2, 2, 1] if plan.mine == 5 else [1] * plan.mine
     return [(sum(sizes[:n]), size) for n, size in enumerate(sizes)]
+
+
+def fetch_list(chunks):
+    if len(chunks) < 4:
+        return chunks
+    return [*chunks[:2], (chunks[2][0], sum(heads for _, heads in chunks[2:]))]
 
 
 def after(arrays, others):
@@ -348,17 +360,30 @@
 def local(queries, keys, values, out_grad, tile_mask):
     plan = Plan(*queries.shape, lax.axis_size("head"), lax.axis_size("frame"))
     chunks = chunk_list(plan)
-    line, outer, depth = Line(), Queue(plan, 3), Queue(plan, 3)
-    packed = line.ran(pack_all(plan, (queries, out_grad, keys, values), chunks))
-    packed = [packed[n * plan.on : (n + 1) * plan.on] for n in range(len(chunks))]
+    line, inward, outer, depth = Line(), Queue(plan, 2), Queue(plan, 3), Queue(plan, 3)
+    spans = fetch_list(chunks)
+    last = len(chunks) - 1
+    arrays = (queries, out_grad, keys, values)
+    blocks = [(s, first, heads) for first, heads in spans for s in range(1, plan.on)]
+    packed = line.ran(pack_columns(plan, arrays, blocks + [(0, *c) for c in chunks]))
+    outgoing, own = packed[: len(blocks)], packed[len(blocks) :]
     received = []
 
-    def fetch(n):
-        received.append([outer.send(a, o_step=s) for s, a in enumerate(packed[n][1:], 1)])
+    def fetch(n, waits=()):
+        group = outgoing[n * (plan.on - 1) : (n + 1) * (plan.on - 1)]
+        received.append([inward.send(a, waits, o_step=s) for s, a in enumerate(group, 1)])
+
+    def others(n):
+        first, heads = chunks[n]
+        for got, (start, count) in zip(received, spans, strict=True):
+            if start <= first and first + heads <= start + count:
+                return [(a, (first - start) * HD) for a in got]
 
     def exchange(n, group, weight=SMALL):
         heads = chunks[n][1]
-        ready = line.ran(pack_heads(plan, line.tie(group), heads * HD, weight))
+        arrays = line.tie([array for array, _ in group])
+        group = [(array, at) for array, (_, at) in zip(arrays, group, strict=True)]
+        ready = line.ran(pack_heads(plan, group, heads * HD, weight))
         moved = [depth.send(a, z_step=k) for k, a in zip(plan.steps[1:], ready[1:], strict=True)]
         return [ready[0], *moved]
 
@@ -371,9 +396,14 @@
         first, heads = chunks[n]
         qg, kvs = joined[n]
         tied = line.tie([qg])[0]
-        results = line.ran(attend(plan, tile_mask, tied, kvs, first, heads))
+        split = n == last
+        results = line.ran(attend(plan, tile_mask, tied, kvs, first, heads, split))
         row_parts, key_parts = results[: plan.on], results[plan.on :]
-        parts = [plan.send(a, i_step=m, returning=True) for m, a in enumerate(key_parts) if m]
+        parts = [
+            plan.send(a, i_step=(m + 1) // 2 if split else m, returning=True)
+            for m, a in enumerate(key_parts)
+            if m
+        ]
         return row_parts, key_parts[0], parts
 
     def give_back(group):
@@ -391,30 +421,28 @@
         pieces = [(step, which, line.tie([array])[0]), *pieces[1:]]
         return line.ran(place(plan, pieces, *chunks[n], outs))
 
-    last = len(chunks) - 1
     arrived, joined, pieces, outs = [], [], [], []
-    fetch(0)
+    for n in range(min(2, len(spans))):
+        fetch(n)
+    arrived.append([exchange(0, [(own[0], 0)])])
+    if plan.on > 1:
+        arrived[0].append(exchange(0, [(a, 0) for a in received[0]]))
     if last:
-        fetch(1)
-    arrived.append([exchange(0, [packed[0][0]])])
-    if plan.on > 1:
-        arrived[0].append(exchange(0, received[0]))
-    if last:
-        arrived.append([exchange(1, [packed[1][0], *received[1]])])
+        arrived.append([exchange(1, [(own[1], 0), *others(1)])])
     joined.append(join(0))
+    for n in range(2, len(spans)):
+        fetch(n)
     for n in range(last):
-        if n + 2 <= last:
-            fetch(n + 2)
         results = work(n)
         joined.append(join(n + 1))
         if n + 2 <= last:
-            arrived.append([exchange(n + 2, [packed[n + 2][0], *received[n + 2]], LARGE)])
+            arrived.append([exchange(n + 2, [(own[n + 2], 0), *others(n + 2)], SMALL if n else LARGE)])
         if n:
             outs = put(n - 1, pieces[n - 1], outs)
         pieces.append(sums(n, *results, True))
-    row_parts, own, parts = work(last)
+    row_parts, key_parts, parts = work(last)
     row_parts = give_back(row_parts)
-    final = sums(last, row_parts, own, parts, False)
+    final = sums(last, row_parts, key_parts, parts, False)
     if last:
         outs = put(last - 1, pieces[last - 1], outs)
     outs = put(last, final, outs)

time: 95.6 us -> 94.3 us (0.986)
  waiting for transfers between devices: 41.2 us -> 36.9 us
  starting transfers between devices: 28.7 us -> 31.8 us
    ppermute x25 -> x26, waiting for transfers between devices: 41.2 us -> 36.9 us  [send(): return lax.ppermute(array, ('head', 'frame'), pairs)]
    ppermute x25 -> x26, starting transfers between devices: 28.7 us -> 31.8 us  [send(): return lax.ppermute(array, ('head', 'frame'), pairs)]
  transfers between devices with their start and end apart: 25 -> 26, of which waited for: 9 -> 13; matrix products, arithmetic and copies ran while one was open for 0% -> 0% of each run, Pallas kernels for 23% -> 23%
where the time goes in v3:
time: 94.3 us; the launch traced here: 94.1 us
  waiting for transfers between devices  36.9 us (39%)
  starting transfers between devices  31.8 us (34%)
  Pallas kernels  24.6 us (26%)
    ppermute x26, waiting for transfers between devices, send(): return lax.ppermute(array, ('head', 'frame'), pairs)  36.9 us
    ppermute x26, starting transfers between devices, send(): return lax.ppermute(array, ('head', 'frame'), pairs)  31.8 us
    pallas_call x3, Pallas kernels, attend(): pl.pallas_call(functools.partial(attend_body, plan, first, heads, split),...  17 us
    pallas_call x3, Pallas kernels, place(): pl.pallas_call(body, out_shape=out, in_specs=[VMEM] * len(pieces) + [HBM]...  2.91 us
    pallas_call x7, Pallas kernels, call_mover(): pl.pallas_call(body, out_shape=out_shape, in_specs=[VMEM] * len(operands)...  2.14 us
    pallas_call x1, Pallas kernels, pack_columns(): pl.pallas_call(body, out_shape=out, in_specs=[HBM] * 4, out_specs=[VMEM]...  2.12 us
  transfers between devices with their start and end apart: 26, of which 13 were waited for; matrix products, arithmetic and copies ran while one was open for 0% of the time, Pallas kernels for 23%

profile of v3, /device:TPU:0, one launch (start us, length us, event | category | flops | bytes accessed | tf_op | source)
XLA Modules:
  0.0 94.1 jit_solution(11538250588722895448)
XLA Ops:
  0.6 2.1 %pack_columns.1 = (bf16[4,4,64,256]{3,2,1,0:T(8,128)(2,1)S(1)}, bf16[4,4,64,256]{3,2,1,0:T(8,128)(2,1)S(1)}, bf16[4,4,64,128]{3,2,1,0:T(8,128)(2,1)S(1)}, bf16[4...) custom-call(bf16[64,5120]{1,0:T(8,128)(2,1)} %refs_0_.4, ...), custom_call_target="tpu_custom_call" | custom-call | flops 1024 | bytes 1024 | tf_op jit(solution)/shard_map/pack_columns/pallas_call | solution.py:102
  2.8 3.0 %collective-permute-start = (bf16[4,4,64,256]{3,2,1,0:T(8,128)(2,1)S(1)}, bf16[4,4,64,256]{3,2,1,0:T(8,128)(2,1)S(1)}, u32[]{:S(2)}, u32[]{:S(2)}) collective-permute-start(bf16[4,4,64,256]{3,2,1,0:T(8,128)(2,1)S(1)} %get-tuple-element.99), channel_id=1, source_target_pairs={{0,2},{1,3},{2,0},{3,1},{4,6},{5,7},{6,4},{7,5},{8,10},{9,11},{10,... | collective-permute-start | bytes 1572872 | tf_op jit(solution)/shard_map/ppermute | solution.py:66
  5.9 3.1 %collective-permute-start.9 = (bf16[1,4,64,256]{3,2,1,0:T(8,128)(2,1)S(1)}, bf16[1,4,64,256]{3,2,1,0:T(8,128)(2,1)S(1)}, u32[]{:S(2)}, u32[]{:S(2)}) collective-permute-start(bf16[1,4,64,256]{3,2,1,0:T(8,128)(2,1)S(1)} %get-tuple-element.105), channel_id=1, source_target_pairs={{0,8},{1,9},{2,10},{3,11},{4,12},{5,13},{6,14},{7,15},{8,0},{9,1},... | collective-permute-start | bytes 393224 | tf_op jit(solution)/shard_map/ppermute | solution.py:66
  9.0 1.3 %collective-permute-start.6 = (bf16[1,4,64,256]{3,2,1,0:T(8,128)(2,1)S(1)}, bf16[1,4,64,256]{3,2,1,0:T(8,128)(2,1)S(1)}, u32[]{:S(2)}, u32[]{:S(2)}) collective-permute-start(bf16[1,4,64,256]{3,2,1,0:T(8,128)(2,1)S(1)} %get-tuple-element.118), channel_id=1, source_target_pairs={{0,12},{1,13},{2,14},{3,15},{4,8},{5,9},{6,10},{7,11},{8,4},{9,5},... | collective-permute-start | bytes 393224 | tf_op jit(solution)/shard_map/ppermute | solution.py:66
  10.6 8.0 %collective-permute-done.refs_0_ = bf16[4,4,64,256]{3,2,1,0:T(8,128)(2,1)S(1)} collective-permute-done((bf16[4,4,64,256]{3,2,1,0:T(8,128)(2,1)S(1)}, bf16[4,4,64,256]{3,2,1,0:T(8,128)(2,1)S(1)}, u32[]{:S(2)}, u32[]{:S(2)}) %collective-permute-start) | collective-permute-done | bytes 524320 | tf_op jit(solution)/shard_map/ppermute | solution.py:66
  18.8 3.0 %collective-permute-start.10 = (bf16[1,4,64,256]{3,2,1,0:T(8,128)(2,1)S(1)}, bf16[1,4,64,256]{3,2,1,0:T(8,128)(2,1)S(1)}, u32[]{:S(2)}, u32[]{:S(2)}) collective-permute-start(bf16[1,4,64,256]{3,2,1,0:T(8,128)(2,1)S(1)} %get-tuple-element.122), channel_id=1, source_target_pairs={{0,8},{1,9},{2,10},{3,11},{4,12},{5,13},{6,14},{7,15},{8,0},{9,1},... | collective-permute-start | bytes 393224 | tf_op jit(solution)/shard_map/ppermute | solution.py:66
  21.8 1.3 %collective-permute-start.7 = (bf16[1,4,64,256]{3,2,1,0:T(8,128)(2,1)S(1)}, bf16[1,4,64,256]{3,2,1,0:T(8,128)(2,1)S(1)}, u32[]{:S(2)}, u32[]{:S(2)}) collective-permute-start(bf16[1,4,64,256]{3,2,1,0:T(8,128)(2,1)S(1)} %get-tuple-element.119), channel_id=1, source_target_pairs={{0,12},{1,13},{2,14},{3,15},{4,8},{5,9},{6,10},{7,11},{8,4},{9,5},... | collective-permute-start | bytes 393224 | tf_op jit(solution)/shard_map/ppermute | solution.py:66
  23.6 5.4 %collective-permute-done.2.refs_1_ = bf16[4,4,64,256]{3,2,1,0:T(8,128)(2,1)S(1)} collective-permute-done((bf16[4,4,64,256]{3,2,1,0:T(8,128)(2,1)S(1)}, bf16[4,4,64,256]{3,2,1,0:T(8,128)(2,1)S(1)}, u32[]{:S(2)}, u32[]{:S(2)}) %collective-permute-start.2) | collective-permute-done | bytes 524320 | tf_op jit(solution)/shard_map/ppermute | solution.py:66
  30.6 4.0 %collective-permute-start.11 = (bf16[2,4,64,256]{3,2,1,0:T(8,128)(2,1)}, bf16[2,4,64,256]{3,2,1,0:T(8,128)(2,1)S(1)}, u32[]{:S(2)}, u32[]{:S(2)}) collective-permute-start(bf16[2,4,64,256]{3,2,1,0:T(8,128)(2,1)} %get-tuple-element.123), channel_id=1, source_target_pairs={{0,8},{1,9},{2,10},{3,11},{4,12},{5,13},{6,14},{7,15},{8,0},{9,1},... | collective-permute-start | bytes 786440 | tf_op jit(solution)/shard_map/ppermute | solution.py:66
  35.3 1.5 %collective-permute-start.1 = (bf16[4,4,64,128]{3,2,1,0:T(8,128)(2,1)S(1)}, bf16[4,4,64,128]{3,2,1,0:T(8,128)(2,1)}, u32[]{:S(2)}, u32[]{:S(2)}) collective-permute-start(bf16[4,4,64,128]{3,2,1,0:T(8,128)(2,1)S(1)} %get-tuple-element.100), channel_id=1, source_target_pairs={{0,2},{1,3},{2,0},{3,1},{4,6},{5,7},{6,4},{7,5},{8,10},{9,11},{10,... | collective-permute-start | bytes 786440 | tf_op jit(solution)/shard_map/ppermute | solution.py:66
  36.9 6.6 %attend.3 = (bf16[2,256,256]{2,1,0:T(8,128)(2,1)S(1)}, bf16[2,256,256]{2,1,0:T(8,128)(2,1)S(1)}, f32[2,512,256]{2,1,0:T(8,128)S(1)}, bf16[2,512,256]{2,1,0:T(8,128)(2,1)S(1)}) custom-call(s32[10,8,8]{2,1,0:T(8,128)S(1)} %copy.19.refs_0_, bf16[2,512,256]{2,1,0:T(8,128)(2,1)S(1)} %get-tuple-element.130.refs_1_, ...), custom_call_target="tpu_custom_call" | custom-call | flops 1024 | bytes 1024 | tf_op jit(solution)/shard_map/attend/pallas_call | solution.py:237
  43.6 9.7 %collective-permute-done.11.refs_3_ = bf16[2,4,64,256]{3,2,1,0:T(8,128)(2,1)S(1)} collective-permute-done((bf16[2,4,64,256]{3,2,1,0:T(8,128)(2,1)}, bf16[2,4,64,256]{3,2,1,0:T(8,128)(2,1)S(1)}, u32[]{:S(2)}, u32[]{:S(2)}) %collective-permute-start.11) | collective-permute-done | bytes 262176 | tf_op jit(solution)/shard_map/ppermute | solution.py:66
  55.5 1.6 %collective-permute-start.18 = (bf16[4,256,256]{2,1,0:T(8,128)(2,1)S(1)}, bf16[4,256,256]{2,1,0:T(8,128)(2,1)S(1)}, u32[]{:S(2)}, u32[]{:S(2)}) collective-permute-start(bf16[4,256,256]{2,1,0:T(8,128)(2,1)S(1)} %get-tuple-element.152), channel_id=1, source_target_pairs={{0,2},{1,3},{2,0},{3,1},{4,6},{5,7},{6,4},{7,5},{8,10},{9,11},{10,... | collective-permute-start | bytes 1572872 | tf_op jit(solution)/shard_map/ppermute | solution.py:66
  57.0 5.7 %collective-permute-start.15 = (bf16[2,4,64,128]{3,2,1,0:T(8,128)(2,1)S(1)}, bf16[2,4,64,128]{3,2,1,0:T(8,128)(2,1)S(1)}, u32[]{:S(2)}, u32[]{:S(2)}) collective-permute-start(bf16[2,4,64,128]{3,2,1,0:T(8,128)(2,1)S(1)} %get-tuple-element.146), channel_id=1, source_target_pairs={{0,8},{1,9},{2,10},{3,11},{4,12},{5,13},{6,14},{7,15},{8,0},{9,1},... | collective-permute-start | bytes 393224 | tf_op jit(solution)/shard_map/ppermute | solution.py:66
  62.7 1.7 %collective-permute-start.14 = (bf16[2,4,64,128]{3,2,1,0:T(8,128)(2,1)S(1)}, bf16[2,4,64,128]{3,2,1,0:T(8,128)(2,1)S(1)}, u32[]{:S(2)}, u32[]{:S(2)}) collective-permute-start(bf16[2,4,64,128]{3,2,1,0:T(8,128)(2,1)S(1)} %get-tuple-element.144), channel_id=1, source_target_pairs={{0,12},{1,13},{2,14},{3,15},{4,8},{5,9},{6,10},{7,11},{8,4},{9,5},... | collective-permute-start | bytes 393224 | tf_op jit(solution)/shard_map/ppermute | solution.py:66
  64.5 6.6 %attend.4 = (bf16[2,256,256]{2,1,0:T(8,128)(2,1)S(1)}, bf16[2,256,256]{2,1,0:T(8,128)(2,1)S(1)}, f32[2,512,256]{2,1,0:T(8,128)S(1)}, bf16[2,512,256]{2,1,0:T(8,128)(2,1)S(1)}) custom-call(s32[10,8,8]{2,1,0:T(8,128)S(1)} %copy.19.refs_0_, bf16[2,512,256]{2,1,0:T(8,128)(2,1)S(1)} %get-tuple-element.153.refs_1_, ...), custom_call_target="tpu_custom_call" | custom-call | flops 1024 | bytes 1024 | tf_op jit(solution)/shard_map/attend/pallas_call | solution.py:237
  71.2 1.5 %collective-permute-done.15.refs_3_ = bf16[2,4,64,128]{3,2,1,0:T(8,128)(2,1)S(1)} collective-permute-done((bf16[2,4,64,128]{3,2,1,0:T(8,128)(2,1)S(1)}, bf16[2,4,64,128]{3,2,1,0:T(8,128)(2,1)S(1)}, u32[]{:S(2)}, u32[]{:S(2)}) %collective-permute-start.15) | collective-permute-done | bytes 131104 | tf_op jit(solution)/shard_map/ppermute | solution.py:66
  75.5 1.5 %collective-permute-done.20.refs_3_ = bf16[2,512,128]{2,1,0:T(8,128)(2,1)S(1)} collective-permute-done((bf16[2,512,128]{2,1,0:T(8,128)(2,1)S(1)}, bf16[2,512,128]{2,1,0:T(8,128)(2,1)S(1)}, u32[]{:S(2)}, u32[]{:S(2)}) %collective-permute-start.20) | collective-permute-done | bytes 262176 | tf_op jit(solution)/shard_map/ppermute | solution.py:66
  77.0 3.8 %attend.5 = (bf16[2,256,128]{2,1,0:T(8,128)(2,1)S(1)}, bf16[2,256,128]{2,1,0:T(8,128)(2,1)S(1)}, f32[2,512,128]{2,1,0:T(8,128)S(1)}, bf16[512,128]{1,0:T(8,128)(2,1)S(1)}, bf16[512,128]{1,0:T(8,128)(2,1)S(1)}) custom-call(s32[10,8,8]{2,1,0:T(8,128)S(1)} %copy.19.refs_0_, bf16[2,512,128]{2,1,0:T(8,128)(2,1)S(1)} %get-tuple-element.169.refs_1_, ...), custom_call_target="tpu_custom_call" | custom-call | flops 1024 | bytes 1024 | tf_op jit(solution)/shard_map/attend/pallas_call | solution.py:237
  81.4 1.5 %collective-permute-start.24 = (bf16[2,256,128]{2,1,0:T(8,128)(2,1)S(1)}, bf16[2,256,128]{2,1,0:T(8,128)(2,1)S(1)}, u32[]{:S(2)}, u32[]{:S(2)}) collective-permute-start(bf16[2,256,128]{2,1,0:T(8,128)(2,1)S(1)} %get-tuple-element.183), channel_id=1, source_target_pairs={{0,2},{1,3},{2,0},{3,1},{4,6},{5,7},{6,4},{7,5},{8,10},{9,11},{10,... | collective-permute-start | bytes 393224 | tf_op jit(solution)/shard_map/ppermute | solution.py:66
  83.0 1.1 %collective-permute-start.25 = (bf16[2,256,128]{2,1,0:T(8,128)(2,1)S(1)}, bf16[2,256,128]{2,1,0:T(8,128)(2,1)S(1)}, u32[]{:S(2)}, u32[]{:S(2)}) collective-permute-start(bf16[2,256,128]{2,1,0:T(8,128)(2,1)S(1)} %get-tuple-element.185), channel_id=1, source_target_pairs={{0,2},{1,3},{2,0},{3,1},{4,6},{5,7},{6,4},{7,5},{8,10},{9,11},{10,... | collective-permute-start | bytes 393224 | tf_op jit(solution)/shard_map/ppermute | solution.py:66
  84.1 5.7 %collective-permute-done.23.refs_1_ = bf16[4,256,256]{2,1,0:T(8,128)(2,1)S(1)} collective-permute-done((bf16[4,256,256]{2,1,0:T(8,128)(2,1)S(1)}, bf16[4,256,256]{2,1,0:T(8,128)(2,1)S(1)}, u32[]{:S(2)}, u32[]{:S(2)}) %collective-permute-start.23) | collective-permute-done | bytes 524320 | tf_op jit(solution)/shard_map/ppermute | solution.py:66
  90.8 1.1 %collective-permute-done.24.refs_1_ = bf16[2,256,128]{2,1,0:T(8,128)(2,1)S(1)} collective-permute-done((bf16[2,256,128]{2,1,0:T(8,128)(2,1)S(1)}, bf16[2,256,128]{2,1,0:T(8,128)(2,1)S(1)}, u32[]{:S(2)}, u32[]{:S(2)}) %collective-permute-start.24) | collective-permute-done | bytes 131104 | tf_op jit(solution)/shard_map/ppermute | solution.py:66
  91.9 1.4 %collective-permute-done.25.refs_3_ = bf16[2,256,128]{2,1,0:T(8,128)(2,1)S(1)} collective-permute-done((bf16[2,256,128]{2,1,0:T(8,128)(2,1)S(1)}, bf16[2,256,128]{2,1,0:T(8,128)(2,1)S(1)}, u32[]{:S(2)}, u32[]{:S(2)}) %collective-permute-start.25) | collective-permute-done | bytes 131104 | tf_op jit(solution)/shard_map/ppermute | solution.py:66
  (48 shorter events, 11.0 us)
Async XLA Ops:
  2.8 15.8 %collective-permute-start = (bf16[4,4,64,256]{3,2,1,0:T(8,128)(2,1)S(1)}, bf16[4,4,64,256]{3,2,1,0:T(8,128)(2,1)S(1)}, u32[]{:S(2)}, u32[]{:S(2)}) collective-permute-start(bf16[4,4,64,256]{3,2,1,0:T(8,128)(2,1)S(1)} %get-tuple-element.99), channel_id=1, source_target_pairs={{0,2},{1,3},{2,0},{3,1},{4,6},{5,7},{6,4},{7,5},{8,10},{9,11},{10,... | collective-permute-start | bytes 1572872 | tf_op jit(solution)/shard_map/ppermute | solution.py:66
  5.8 23.2 %collective-permute-start.2 = (bf16[4,4,64,256]{3,2,1,0:T(8,128)(2,1)S(1)}, bf16[4,4,64,256]{3,2,1,0:T(8,128)(2,1)S(1)}, u32[]{:S(2)}, u32[]{:S(2)}) collective-permute-start(bf16[4,4,64,256]{3,2,1,0:T(8,128)(2,1)S(1)} %get-tuple-element.102), channel_id=1, source_target_pairs={{0,2},{1,3},{2,0},{3,1},{4,6},{5,7},{6,4},{7,5},{8,10},{9,11},{10,... | collective-permute-start | bytes 1572872 | tf_op jit(solution)/shard_map/ppermute | solution.py:66
  5.9 12.9 %collective-permute-start.9 = (bf16[1,4,64,256]{3,2,1,0:T(8,128)(2,1)S(1)}, bf16[1,4,64,256]{3,2,1,0:T(8,128)(2,1)S(1)}, u32[]{:S(2)}, u32[]{:S(2)}) collective-permute-start(bf16[1,4,64,256]{3,2,1,0:T(8,128)(2,1)S(1)} %get-tuple-element.105), channel_id=1, source_target_pairs={{0,8},{1,9},{2,10},{3,11},{4,12},{5,13},{6,14},{7,15},{8,0},{9,1},... | collective-permute-start | bytes 393224 | tf_op jit(solution)/shard_map/ppermute | solution.py:66
  9.0 12.8 %collective-permute-start.6 = (bf16[1,4,64,256]{3,2,1,0:T(8,128)(2,1)S(1)}, bf16[1,4,64,256]{3,2,1,0:T(8,128)(2,1)S(1)}, u32[]{:S(2)}, u32[]{:S(2)}) collective-permute-start(bf16[1,4,64,256]{3,2,1,0:T(8,128)(2,1)S(1)} %get-tuple-element.118), channel_id=1, source_target_pairs={{0,12},{1,13},{2,14},{3,15},{4,8},{5,9},{6,10},{7,11},{8,4},{9,5},... | collective-permute-start | bytes 393224 | tf_op jit(solution)/shard_map/ppermute | solution.py:66
  10.3 12.8 %collective-permute-start.3 = (bf16[1,4,64,256]{3,2,1,0:T(8,128)(2,1)S(1)}, bf16[1,4,64,256]{3,2,1,0:T(8,128)(2,1)S(1)}, u32[]{:S(2)}, u32[]{:S(2)}) collective-permute-start(bf16[1,4,64,256]{3,2,1,0:T(8,128)(2,1)S(1)} %get-tuple-element.113), channel_id=1, source_target_pairs={{0,4},{1,5},{2,6},{3,7},{4,0},{5,1},{6,2},{7,3},{8,12},{9,13},{10,... | collective-permute-start | bytes 393224 | tf_op jit(solution)/shard_map/ppermute | solution.py:66
  18.8 11.4 %collective-permute-start.10 = (bf16[1,4,64,256]{3,2,1,0:T(8,128)(2,1)S(1)}, bf16[1,4,64,256]{3,2,1,0:T(8,128)(2,1)S(1)}, u32[]{:S(2)}, u32[]{:S(2)}) collective-permute-start(bf16[1,4,64,256]{3,2,1,0:T(8,128)(2,1)S(1)} %get-tuple-element.122), channel_id=1, source_target_pairs={{0,8},{1,9},{2,10},{3,11},{4,12},{5,13},{6,14},{7,15},{8,0},{9,1},... | collective-permute-start | bytes 393224 | tf_op jit(solution)/shard_map/ppermute | solution.py:66
  21.8 8.3 %collective-permute-start.7 = (bf16[1,4,64,256]{3,2,1,0:T(8,128)(2,1)S(1)}, bf16[1,4,64,256]{3,2,1,0:T(8,128)(2,1)S(1)}, u32[]{:S(2)}, u32[]{:S(2)}) collective-permute-start(bf16[1,4,64,256]{3,2,1,0:T(8,128)(2,1)S(1)} %get-tuple-element.119), channel_id=1, source_target_pairs={{0,12},{1,13},{2,14},{3,15},{4,8},{5,9},{6,10},{7,11},{8,4},{9,5},... | collective-permute-start | bytes 393224 | tf_op jit(solution)/shard_map/ppermute | solution.py:66
  23.1 7.3 %collective-permute-start.4 = (bf16[1,4,64,256]{3,2,1,0:T(8,128)(2,1)S(1)}, bf16[1,4,64,256]{3,2,1,0:T(8,128)(2,1)S(1)}, u32[]{:S(2)}, u32[]{:S(2)}) collective-permute-start(bf16[1,4,64,256]{3,2,1,0:T(8,128)(2,1)S(1)} %get-tuple-element.114), channel_id=1, source_target_pairs={{0,4},{1,5},{2,6},{3,7},{4,0},{5,1},{6,2},{7,3},{8,12},{9,13},{10,... | collective-permute-start | bytes 393224 | tf_op jit(solution)/shard_map/ppermute | solution.py:66
  30.5 6.4 %collective-permute-start.12 = (bf16[2,512,256]{2,1,0:T(8,128)(2,1)S(1)}, bf16[2,512,256]{2,1,0:T(8,128)(2,1)S(1)}, u32[]{:S(2)}, u32[]{:S(2)}) collective-permute-start(bf16[2,512,256]{2,1,0:T(8,128)(2,1)S(1)} %get-tuple-element.131.refs_2_), channel_id=1, source_target_pairs={{0,1},{1,0},{2,3},{3,2},{4,5},{5,4},{6,7},{7,6},{8,9},{9,8},{10,11... | collective-permute-start | bytes 1572872 | tf_op jit(solution)/shard_map/ppermute | solution.py:66
  30.6 22.7 %collective-permute-start.11 = (bf16[2,4,64,256]{3,2,1,0:T(8,128)(2,1)}, bf16[2,4,64,256]{3,2,1,0:T(8,128)(2,1)S(1)}, u32[]{:S(2)}, u32[]{:S(2)}) collective-permute-start(bf16[2,4,64,256]{3,2,1,0:T(8,128)(2,1)} %get-tuple-element.123), channel_id=1, source_target_pairs={{0,8},{1,9},{2,10},{3,11},{4,12},{5,13},{6,14},{7,15},{8,0},{9,1},... | collective-permute-start | bytes 786440 | tf_op jit(solution)/shard_map/ppermute | solution.py:66
  34.6 18.6 %collective-permute-start.8 = (bf16[2,4,64,256]{3,2,1,0:T(8,128)(2,1)}, bf16[2,4,64,256]{3,2,1,0:T(8,128)(2,1)S(1)}, u32[]{:S(2)}, u32[]{:S(2)}) collective-permute-start(bf16[2,4,64,256]{3,2,1,0:T(8,128)(2,1)} %get-tuple-element.120), channel_id=1, source_target_pairs={{0,12},{1,13},{2,14},{3,15},{4,8},{5,9},{6,10},{7,11},{8,4},{9,5},... | collective-permute-start | bytes 786440 | tf_op jit(solution)/shard_map/ppermute | solution.py:66
  35.1 19.1 %collective-permute-start.5 = (bf16[2,4,64,256]{3,2,1,0:T(8,128)(2,1)S(1)}, bf16[2,4,64,256]{3,2,1,0:T(8,128)(2,1)S(1)}, u32[]{:S(2)}, u32[]{:S(2)}) collective-permute-start(bf16[2,4,64,256]{3,2,1,0:T(8,128)(2,1)S(1)} %get-tuple-element.115), channel_id=1, source_target_pairs={{0,4},{1,5},{2,6},{3,7},{4,0},{5,1},{6,2},{7,3},{8,12},{9,13},{10,... | collective-permute-start | bytes 786440 | tf_op jit(solution)/shard_map/ppermute | solution.py:66
  35.3 19.0 %collective-permute-start.1 = (bf16[4,4,64,128]{3,2,1,0:T(8,128)(2,1)S(1)}, bf16[4,4,64,128]{3,2,1,0:T(8,128)(2,1)}, u32[]{:S(2)}, u32[]{:S(2)}) collective-permute-start(bf16[4,4,64,128]{3,2,1,0:T(8,128)(2,1)S(1)} %get-tuple-element.100), channel_id=1, source_target_pairs={{0,2},{1,3},{2,0},{3,1},{4,6},{5,7},{6,4},{7,5},{8,10},{9,11},{10,... | collective-permute-start | bytes 786440 | tf_op jit(solution)/shard_map/ppermute | solution.py:66
  43.5 11.8 %collective-permute-start.16 = (bf16[2,512,256]{2,1,0:T(8,128)(2,1)S(1)}, bf16[2,512,256]{2,1,0:T(8,128)(2,1)S(1)}, u32[]{:S(2)}, u32[]{:S(2)}) collective-permute-start(bf16[2,512,256]{2,1,0:T(8,128)(2,1)S(1)} %get-tuple-element.132), channel_id=1, source_target_pairs={{0,1},{1,0},{2,3},{3,2},{4,5},{5,4},{6,7},{7,6},{8,9},{9,8},{10,11... | collective-permute-start | bytes 1572872 | tf_op jit(solution)/shard_map/ppermute | solution.py:66
  54.2 10.3 %collective-permute-start.17 = (bf16[2,512,256]{2,1,0:T(8,128)(2,1)S(1)}, bf16[2,512,256]{2,1,0:T(8,128)(2,1)S(1)}, u32[]{:S(2)}, u32[]{:S(2)}) collective-permute-start(bf16[2,512,256]{2,1,0:T(8,128)(2,1)S(1)} %get-tuple-element.137.refs_2_), channel_id=1, source_target_pairs={{0,1},{1,0},{2,3},{3,2},{4,5},{5,4},{6,7},{7,6},{8,9},{9,8},{10,11... | collective-permute-start | bytes 1572872 | tf_op jit(solution)/shard_map/ppermute | solution.py:66
  55.5 18.2 %collective-permute-start.18 = (bf16[4,256,256]{2,1,0:T(8,128)(2,1)S(1)}, bf16[4,256,256]{2,1,0:T(8,128)(2,1)S(1)}, u32[]{:S(2)}, u32[]{:S(2)}) collective-permute-start(bf16[4,256,256]{2,1,0:T(8,128)(2,1)S(1)} %get-tuple-element.152), channel_id=1, source_target_pairs={{0,2},{1,3},{2,0},{3,1},{4,6},{5,7},{6,4},{7,5},{8,10},{9,11},{10,... | collective-permute-start | bytes 1572872 | tf_op jit(solution)/shard_map/ppermute | solution.py:66
  57.0 15.6 %collective-permute-start.15 = (bf16[2,4,64,128]{3,2,1,0:T(8,128)(2,1)S(1)}, bf16[2,4,64,128]{3,2,1,0:T(8,128)(2,1)S(1)}, u32[]{:S(2)}, u32[]{:S(2)}) collective-permute-start(bf16[2,4,64,128]{3,2,1,0:T(8,128)(2,1)S(1)} %get-tuple-element.146), channel_id=1, source_target_pairs={{0,8},{1,9},{2,10},{3,11},{4,12},{5,13},{6,14},{7,15},{8,0},{9,1},... | collective-permute-start | bytes 393224 | tf_op jit(solution)/shard_map/ppermute | solution.py:66
  62.7 9.9 %collective-permute-start.14 = (bf16[2,4,64,128]{3,2,1,0:T(8,128)(2,1)S(1)}, bf16[2,4,64,128]{3,2,1,0:T(8,128)(2,1)S(1)}, u32[]{:S(2)}, u32[]{:S(2)}) collective-permute-start(bf16[2,4,64,128]{3,2,1,0:T(8,128)(2,1)S(1)} %get-tuple-element.144), channel_id=1, source_target_pairs={{0,12},{1,13},{2,14},{3,15},{4,8},{5,9},{6,10},{7,11},{8,4},{9,5},... | collective-permute-start | bytes 393224 | tf_op jit(solution)/shard_map/ppermute | solution.py:66
  64.5 9.1 %collective-permute-start.13 = (bf16[2,4,64,128]{3,2,1,0:T(8,128)(2,1)S(1)}, bf16[2,4,64,128]{3,2,1,0:T(8,128)(2,1)S(1)}, u32[]{:S(2)}, u32[]{:S(2)}) collective-permute-start(bf16[2,4,64,128]{3,2,1,0:T(8,128)(2,1)S(1)} %get-tuple-element.142), channel_id=1, source_target_pairs={{0,4},{1,5},{2,6},{3,7},{4,0},{5,1},{6,2},{7,3},{8,12},{9,13},{10,... | collective-permute-start | bytes 393224 | tf_op jit(solution)/shard_map/ppermute | solution.py:66
  71.1 3.6 %collective-permute-start.19 = (bf16[2,512,256]{2,1,0:T(8,128)(2,1)S(1)}, bf16[2,512,256]{2,1,0:T(8,128)(2,1)S(1)}, u32[]{:S(2)}, u32[]{:S(2)}) collective-permute-start(bf16[2,512,256]{2,1,0:T(8,128)(2,1)S(1)} %get-tuple-element.154), channel_id=1, source_target_pairs={{0,1},{1,0},{2,3},{3,2},{4,5},{5,4},{6,7},{7,6},{8,9},{9,8},{10,11... | collective-permute-start | bytes 1572872 | tf_op jit(solution)/shard_map/ppermute | solution.py:66
  74.9 14.9 %collective-permute-start.23 = (bf16[4,256,256]{2,1,0:T(8,128)(2,1)S(1)}, bf16[4,256,256]{2,1,0:T(8,128)(2,1)S(1)}, u32[]{:S(2)}, u32[]{:S(2)}) collective-permute-start(bf16[4,256,256]{2,1,0:T(8,128)(2,1)S(1)} %get-tuple-element.168), channel_id=1, source_target_pairs={{0,2},{1,3},{2,0},{3,1},{4,6},{5,7},{6,4},{7,5},{8,10},{9,11},{10,... | collective-permute-start | bytes 1572872 | tf_op jit(solution)/shard_map/ppermute | solution.py:66
  80.8 2.1 %collective-permute-start.21 = (bf16[512,128]{1,0:T(8,128)(2,1)S(1)}, bf16[512,128]{1,0:T(8,128)(2,1)S(1)}, u32[]{:S(2)}, u32[]{:S(2)}) collective-permute-start(bf16[512,128]{1,0:T(8,128)(2,1)S(1)} %get-tuple-element.175), channel_id=1, source_target_pairs={{0,1},{1,0},{2,3},{3,2},{4,5},{5,4},{6,7},{7,6},{8,9},{9,8},{10,11... | collective-permute-start | bytes 393224 | tf_op jit(solution)/shard_map/ppermute | solution.py:66
  81.4 10.5 %collective-permute-start.24 = (bf16[2,256,128]{2,1,0:T(8,128)(2,1)S(1)}, bf16[2,256,128]{2,1,0:T(8,128)(2,1)S(1)}, u32[]{:S(2)}, u32[]{:S(2)}) collective-permute-start(bf16[2,256,128]{2,1,0:T(8,128)(2,1)S(1)} %get-tuple-element.183), channel_id=1, source_target_pairs={{0,2},{1,3},{2,0},{3,1},{4,6},{5,7},{6,4},{7,5},{8,10},{9,11},{10,... | collective-permute-start | bytes 393224 | tf_op jit(solution)/shard_map/ppermute | solution.py:66
  83.0 10.3 %collective-permute-start.25 = (bf16[2,256,128]{2,1,0:T(8,128)(2,1)S(1)}, bf16[2,256,128]{2,1,0:T(8,128)(2,1)S(1)}, u32[]{:S(2)}, u32[]{:S(2)}) collective-permute-start(bf16[2,256,128]{2,1,0:T(8,128)(2,1)S(1)} %get-tuple-element.185), channel_id=1, source_target_pairs={{0,2},{1,3},{2,0},{3,1},{4,6},{5,7},{6,4},{7,5},{8,10},{9,11},{10,... | collective-permute-start | bytes 393224 | tf_op jit(solution)/shard_map/ppermute | solution.py:66
  (3 other events, 9.8 us)

commit v4 on v3

--- a/solution.py
+++ b/solution.py
@@ -37,6 +37,7 @@
         self.rows = rows
         self.zn = head_axis
         self.steps = [0, 1, 3, 2] if head_axis == 4 else list(range(head_axis))
+        self.first_steps = [0, 3, 2, 1] if head_axis == 4 else list(range(head_axis))
         self.groups = width // HD // head_axis
         self.on = math.gcd(self.groups, frame_axis)
         self.inn = frame_axis // self.on
@@ -114,10 +115,10 @@
     )(*arrays)
 
 
-def pack_heads(plan, groups, width, weight=SMALL):
+def pack_heads(plan, groups, width, steps, weight=SMALL):
     def body(*refs):
         ins, outs = refs[: len(groups)], refs[len(groups) :]
-        for k, out in zip(plan.steps, outs, strict=True):
+        for k, out in zip(steps, outs, strict=True):
             for step, (ref, (_, at)) in enumerate(zip(ins, groups, strict=True)):
                 out[step] = ref[k, :, :, at : at + width]
 
@@ -125,13 +126,13 @@
     return call_mover(body, [array for array, _ in groups], out, "pack_heads", weight)
 
 
-def join_rows(plan, sets, width):
+def join_rows(plan, sets, width, orders):
     def body(*refs):
         ins, (qg, kv) = refs[:-2], refs[-2:]
         z = lax.axis_index("head")
         for n, ref in enumerate(ins):
             start = sum(s[0].shape[0] for s in sets[: n // plan.zn])
-            row = back(z, plan.steps[n % plan.zn], plan.zn) * plan.rows
+            row = back(z, orders[n // plan.zn][n % plan.zn], plan.zn) * plan.rows
             for step in range(ref.shape[0]):
                 at = (start + step) * plan.slab + row
                 at = pl.ds(pl.multiple_of(at, plan.rows), plan.rows)
@@ -310,13 +311,21 @@
         input_output_aliases={len(pieces) + n: n for n in range(len(outs))},
         scratch_shapes=[pltpu.SemaphoreType.DMA((4 * plan.on,))],
         compiler_params=pltpu.CompilerParams(vmem_limit_bytes=VMEM_LIMIT),
-        cost_estimate=LARGE,
+        cost_estimate=SMALL,
         name="place",
     )(*[p[-1] for p in pieces], *outs)
 
 
+def take_in(arrays):
+    def body(*refs):
+        for n in range(len(arrays)):
+            refs[len(arrays) + n][...] = refs[n][...]
+
+    return call_mover(body, arrays, [shape(*a.shape) for a in arrays], "take_in", LARGE)
+
+
 def chunk_list(plan):
-    sizes = [2, 2, 1] if plan.mine == 5 else [1] * plan.mine
+    sizes = [2, 1, 1, 1] if plan.mine == 5 else [1] * plan.mine
     return [(sum(sizes[:n]), size) for n, size in enumerate(sizes)]
 
 
@@ -365,8 +374,9 @@
     last = len(chunks) - 1
     arrays = (queries, out_grad, keys, values)
     blocks = [(s, first, heads) for first, heads in spans for s in range(1, plan.on)]
-    packed = line.ran(pack_columns(plan, arrays, blocks + [(0, *c) for c in chunks]))
-    outgoing, own = packed[: len(blocks)], packed[len(blocks) :]
+    early = [(0, *c) for c in chunks[:2]]
+    packed = line.ran(pack_columns(plan, arrays, blocks + early))
+    outgoing, own = packed[: len(blocks)], list(packed[len(blocks) :])
     received = []
 
     def fetch(n, waits=()):
@@ -379,17 +389,18 @@
             if start <= first and first + heads <= start + count:
                 return [(a, (first - start) * HD) for a in got]
 
-    def exchange(n, group, weight=SMALL):
+    def exchange(n, group, weight=SMALL, steps=plan.steps):
         heads = chunks[n][1]
         arrays = line.tie([array for array, _ in group])
         group = [(array, at) for array, (_, at) in zip(arrays, group, strict=True)]
-        ready = line.ran(pack_heads(plan, group, heads * HD, weight))
-        moved = [depth.send(a, z_step=k) for k, a in zip(plan.steps[1:], ready[1:], strict=True)]
+        ready = line.ran(pack_heads(plan, group, heads * HD, steps, weight))
+        moved = [depth.send(a, z_step=k) for k, a in zip(steps[1:], ready[1:], strict=True)]
         return [ready[0], *moved]
 
     def join(n):
         rows = [line.tie(arrived[n][0]), *arrived[n][1:]]
-        qg, kv = line.ran(join_rows(plan, rows, chunks[n][1] * HD))
+        orders = [plan.steps if n or m else plan.first_steps for m in range(len(rows))]
+        qg, kv = line.ran(join_rows(plan, rows, chunks[n][1] * HD, orders))
         return qg, [kv] + [plan.send(kv, i_step=m) for m in range(1, plan.inn)]
 
     def work(n):
@@ -424,7 +435,7 @@
     arrived, joined, pieces, outs = [], [], [], []
     for n in range(min(2, len(spans))):
         fetch(n)
-    arrived.append([exchange(0, [(own[0], 0)])])
+    arrived.append([exchange(0, [(own[0], 0)], steps=plan.first_steps)])
     if plan.on > 1:
         arrived[0].append(exchange(0, [(a, 0) for a in received[0]]))
     if last:
@@ -434,17 +445,25 @@
         fetch(n)
     for n in range(last):
         results = work(n)
+        if n == 0 and last > 1:
+            late = [(0, *c) for c in chunks[2:]]
+            own += line.ran(pack_columns(plan, line.tie(arrays), late))
+        if n >= 2:
+            outs = put(n - 2, pieces[n - 2], outs)
         joined.append(join(n + 1))
         if n + 2 <= last:
             arrived.append([exchange(n + 2, [(own[n + 2], 0), *others(n + 2)], SMALL if n else LARGE)])
-        if n:
-            outs = put(n - 1, pieces[n - 1], outs)
+        if n and plan.on > 1:
+            came = [piece for piece in pieces[n - 1] if piece[0]]
+            copies = line.ran(take_in(line.tie([a for _, _, a in came])))
+            kept = [piece for piece in pieces[n - 1] if not piece[0]]
+            pieces[n - 1] = kept + [(s, w, a) for (s, w, _), a in zip(came, copies, strict=True)]
         pieces.append(sums(n, *results, True))
     row_parts, key_parts, parts = work(last)
     row_parts = give_back(row_parts)
     final = sums(last, row_parts, key_parts, parts, False)
-    if last:
-        outs = put(last - 1, pieces[last - 1], outs)
+    for n in range(max(0, last - 2), last):
+        outs = put(n, pieces[n], outs)
     outs = put(last, final, outs)
     return tuple(outs)
 

time: 94.3 us -> 93 us (0.986)
  waiting for transfers between devices: 36.9 us -> 32.9 us
  Pallas kernels: 24.6 us -> 27.3 us
    ppermute x26 -> x32, waiting for transfers between devices: 36.9 us -> 32.9 us  [send(): return lax.ppermute(array, ('head', 'frame'), pairs)]
    pallas_call x1 -> x2, Pallas kernels: 2.12 us -> 3.91 us  [pack_columns(): pl.pallas_call(body, out_shape=out, in_specs=[HBM] * 4, out_specs=[VMEM]...]
    pallas_call x3 -> x4, Pallas kernels: 17 us -> 18.3 us  [attend(): pl.pallas_call(functools.partial(attend_body, plan, first, heads, split),...]
    pallas_call x7 -> x11, Pallas kernels: 2.14 us -> 1.18 us  [call_mover(): pl.pallas_call(body, out_shape=out_shape, in_specs=[VMEM] * len(operands)...]
    pallas_call x3 -> x4, Pallas kernels: 2.91 us -> 3.58 us  [place(): pl.pallas_call(body, out_shape=out, in_specs=[VMEM] * len(pieces) + [HBM]...]
    ppermute x26 -> x32, starting transfers between devices: 31.8 us -> 31.5 us  [send(): return lax.ppermute(array, ('head', 'frame'), pairs)]
  transfers between devices with their start and end apart: 26 -> 32, of which waited for: 13 -> 15; matrix products, arithmetic and copies ran while one was open for 0% -> 0% of each run, Pallas kernels for 23% -> 26%
where the time goes in v4:
time: 93 us; the launch traced here: 92.9 us
  waiting for transfers between devices  32.9 us (35%)
  starting transfers between devices  31.5 us (34%)
  Pallas kernels  27.3 us (29%)
  between operations  1.07 us (1%)
    ppermute x32, waiting for transfers between devices, send(): return lax.ppermute(array, ('head', 'frame'), pairs)  32.9 us
    ppermute x32, starting transfers between devices, send(): return lax.ppermute(array, ('head', 'frame'), pairs)  31.5 us
    pallas_call x4, Pallas kernels, attend(): pl.pallas_call(functools.partial(attend_body, plan, first, heads, split),...  18.3 us
    pallas_call x2, Pallas kernels, pack_columns(): pl.pallas_call(body, out_shape=out, in_specs=[HBM] * 4, out_specs=[VMEM]...  3.91 us
    pallas_call x4, Pallas kernels, place(): pl.pallas_call(body, out_shape=out, in_specs=[VMEM] * len(pieces) + [HBM]...  3.58 us
  transfers between devices with their start and end apart: 32, of which 15 were waited for; matrix products, arithmetic and copies ran while one was open for 0% of the time, Pallas kernels for 26%

profile of v4, /device:TPU:0, one launch (start us, length us, event | category | flops | bytes accessed | tf_op | source)
XLA Modules:
  0.0 92.9 jit_solution(7695057984555364893)
XLA Ops:
  0.6 2.1 %pack_columns.2 = (bf16[4,4,64,256]{3,2,1,0:T(8,128)(2,1)S(1)}, bf16[4,4,64,128]{3,2,1,0:T(8,128)(2,1)S(1)}, bf16[4,4,64,256]{3,2,1,0:T(8,128)(2,1)S(1)}, bf16[4...) custom-call(bf16[64,5120]{1,0:T(8,128)(2,1)} %refs_0_.6, bf16[64,5120]{1,0:T(8,128)(2,1)} %refs_1_.2, ...), custom_call_target="tpu_custom_call" | custom-call | flops 1024 | bytes 1024 | tf_op jit(solution)/shard_map/pack_columns/pallas_call | solution.py:103
  2.7 3.0 %collective-permute-start.4 = (bf16[4,4,64,256]{3,2,1,0:T(8,128)(2,1)S(1)}, bf16[4,4,64,256]{3,2,1,0:T(8,128)(2,1)S(1)}, u32[]{:S(2)}, u32[]{:S(2)}) collective-permute-start(bf16[4,4,64,256]{3,2,1,0:T(8,128)(2,1)S(1)} %get-tuple-element.141), channel_id=1, source_target_pairs={{0,2},{1,3},{2,0},{3,1},{4,6},{5,7},{6,4},{7,5},{8,10},{9,11},{10,... | collective-permute-start | bytes 1572872 | tf_op jit(solution)/shard_map/ppermute | solution.py:67
  5.8 3.7 %collective-permute-start = (bf16[1,4,64,256]{3,2,1,0:T(8,128)(2,1)S(1)}, bf16[1,4,64,256]{3,2,1,0:T(8,128)(2,1)S(1)}, u32[]{:S(2)}, u32[]{:S(2)}) collective-permute-start(bf16[1,4,64,256]{3,2,1,0:T(8,128)(2,1)S(1)} %get-tuple-element.137), channel_id=1, source_target_pairs={{0,12},{1,13},{2,14},{3,15},{4,8},{5,9},{6,10},{7,11},{8,4},{9,5},... | collective-permute-start | bytes 393224 | tf_op jit(solution)/shard_map/ppermute | solution.py:67
  10.6 7.9 %collective-permute-done.4.refs_0_ = bf16[4,4,64,256]{3,2,1,0:T(8,128)(2,1)S(1)} collective-permute-done((bf16[4,4,64,256]{3,2,1,0:T(8,128)(2,1)S(1)}, bf16[4,4,64,256]{3,2,1,0:T(8,128)(2,1)S(1)}, u32[]{:S(2)}, u32[]{:S(2)}) %collective-permute-start.4) | collective-permute-done | bytes 524320 | tf_op jit(solution)/shard_map/ppermute | solution.py:67
  18.5 1.7 %collective-permute-done.1.refs_2_ = bf16[1,4,64,256]{3,2,1,0:T(8,128)(2,1)S(1)} collective-permute-done((bf16[1,4,64,256]{3,2,1,0:T(8,128)(2,1)S(1)}, bf16[1,4,64,256]{3,2,1,0:T(8,128)(2,1)S(1)}, u32[]{:S(2)}, u32[]{:S(2)}) %collective-permute-start.1) | collective-permute-done | bytes 131104 | tf_op jit(solution)/shard_map/ppermute | solution.py:67
  20.2 1.5 %collective-permute-start.7 = (bf16[1,4,64,256]{3,2,1,0:T(8,128)(2,1)S(1)}, bf16[1,4,64,256]{3,2,1,0:T(8,128)(2,1)S(1)}, u32[]{:S(2)}, u32[]{:S(2)}) collective-permute-start(bf16[1,4,64,256]{3,2,1,0:T(8,128)(2,1)S(1)} %get-tuple-element.156), channel_id=1, source_target_pairs={{0,8},{1,9},{2,10},{3,11},{4,12},{5,13},{6,14},{7,15},{8,0},{9,1},... | collective-permute-start | bytes 393224 | tf_op jit(solution)/shard_map/ppermute | solution.py:67
  21.7 1.3 %collective-permute-start.6 = (bf16[1,4,64,256]{3,2,1,0:T(8,128)(2,1)S(1)}, bf16[1,4,64,256]{3,2,1,0:T(8,128)(2,1)S(1)}, u32[]{:S(2)}, u32[]{:S(2)}) collective-permute-start(bf16[1,4,64,256]{3,2,1,0:T(8,128)(2,1)S(1)} %get-tuple-element.155), channel_id=1, source_target_pairs={{0,12},{1,13},{2,14},{3,15},{4,8},{5,9},{6,10},{7,11},{8,4},{9,5},... | collective-permute-start | bytes 393224 | tf_op jit(solution)/shard_map/ppermute | solution.py:67
  24.4 6.4 %collective-permute-done.7.refs_7_ = bf16[1,4,64,256]{3,2,1,0:T(8,128)(2,1)S(1)} collective-permute-done((bf16[1,4,64,256]{3,2,1,0:T(8,128)(2,1)S(1)}, bf16[1,4,64,256]{3,2,1,0:T(8,128)(2,1)S(1)}, u32[]{:S(2)}, u32[]{:S(2)}) %collective-permute-start.7) | collective-permute-done | bytes 131104 | tf_op jit(solution)/shard_map/ppermute | solution.py:67
  33.1 3.0 %collective-permute-start.12 = (bf16[2,4,64,128]{3,2,1,0:T(8,128)(2,1)}, bf16[2,4,64,128]{3,2,1,0:T(8,128)(2,1)S(1)}, u32[]{:S(2)}, u32[]{:S(2)}) collective-permute-start(bf16[2,4,64,128]{3,2,1,0:T(8,128)(2,1)} %get-tuple-element.173), channel_id=1, source_target_pairs={{0,8},{1,9},{2,10},{3,11},{4,12},{5,13},{6,14},{7,15},{8,0},{9,1},... | collective-permute-start | bytes 393224 | tf_op jit(solution)/shard_map/ppermute | solution.py:67
  36.1 1.3 %collective-permute-start.11 = (bf16[2,4,64,128]{3,2,1,0:T(8,128)(2,1)S(1)}, bf16[2,4,64,128]{3,2,1,0:T(8,128)(2,1)S(1)}, u32[]{:S(2)}, u32[]{:S(2)}) collective-permute-start(bf16[2,4,64,128]{3,2,1,0:T(8,128)(2,1)S(1)} %get-tuple-element.172), channel_id=1, source_target_pairs={{0,12},{1,13},{2,14},{3,15},{4,8},{5,9},{6,10},{7,11},{8,4},{9,5},... | collective-permute-start | bytes 393224 | tf_op jit(solution)/shard_map/ppermute | solution.py:67
  37.6 6.8 %attend.4 = (bf16[2,256,256]{2,1,0:T(8,128)(2,1)S(1)}, bf16[2,256,256]{2,1,0:T(8,128)(2,1)S(1)}, f32[2,512,256]{2,1,0:T(8,128)S(1)}, bf16[2,512,256]{2,1,0:T(8,128)(2,1)S(1)}) custom-call(s32[10,8,8]{2,1,0:T(8,128)S(1)} %copy.24.refs_0_, bf16[2,512,256]{2,1,0:T(8,128)(2,1)S(1)} %get-tuple-element.157.refs_1_, ...), custom_call_target="tpu_custom_call" | custom-call | flops 1024 | bytes 1024 | tf_op jit(solution)/shard_map/attend/pallas_call | solution.py:238
  44.4 1.9 %pack_columns.3 = (bf16[4,4,64,128]{3,2,1,0:T(8,128)(2,1)S(1)}, bf16[4,4,64,128]{3,2,1,0:T(8,128)(2,1)S(1)}) custom-call(bf16[64,5120]{1,0:T(8,128)(2,1)} %refs_0_.6, bf16[64,5120]{1,0:T(8,128)(2,1)} %refs_1_.2, bf16[64,5120]{1,0:T(8,128)(2,1)} %refs_2_.2, bf16[64,5120]{1,0:T(8,128)(2,1)} %refs_3_.2), custom_call_target="tpu_custom_call" | custom-call | flops 1024 | bytes 1024 | tf_op jit(solution)/shard_map/pack_columns/pallas_call | solution.py:103
  47.8 2.9 %collective-permute-start.15 = (bf16[2,4,64,128]{3,2,1,0:T(8,128)(2,1)S(1)}, bf16[2,4,64,128]{3,2,1,0:T(8,128)(2,1)S(1)}, u32[]{:S(2)}, u32[]{:S(2)}) collective-permute-start(bf16[2,4,64,128]{3,2,1,0:T(8,128)(2,1)S(1)} %get-tuple-element.187), channel_id=1, source_target_pairs={{0,8},{1,9},{2,10},{3,11},{4,12},{5,13},{6,14},{7,15},{8,0},{9,1},... | collective-permute-start | bytes 393224 | tf_op jit(solution)/shard_map/ppermute | solution.py:67
  50.7 1.8 %collective-permute-start.14 = (bf16[2,4,64,128]{3,2,1,0:T(8,128)(2,1)S(1)}, bf16[2,4,64,128]{3,2,1,0:T(8,128)(2,1)S(1)}, u32[]{:S(2)}, u32[]{:S(2)}) collective-permute-start(bf16[2,4,64,128]{3,2,1,0:T(8,128)(2,1)S(1)} %get-tuple-element.185), channel_id=1, source_target_pairs={{0,12},{1,13},{2,14},{3,15},{4,8},{5,9},{6,10},{7,11},{8,4},{9,5},... | collective-permute-start | bytes 393224 | tf_op jit(solution)/shard_map/ppermute | solution.py:67
  52.5 3.8 %attend.5 = (bf16[2,256,128]{2,1,0:T(8,128)(2,1)S(1)}, bf16[2,256,128]{2,1,0:T(8,128)(2,1)S(1)}, f32[2,512,128]{2,1,0:T(8,128)S(1)}, bf16[2,512,128]{2,1,0:T(8,128)(2,1)S(1)}) custom-call(s32[10,8,8]{2,1,0:T(8,128)S(1)} %copy.24.refs_0_, bf16[2,512,128]{2,1,0:T(8,128)(2,1)S(1)} %get-tuple-element.194.refs_1_, ...), custom_call_target="tpu_custom_call" | custom-call | flops 1024 | bytes 1024 | tf_op jit(solution)/shard_map/attend/pallas_call | solution.py:238
  56.4 4.4 %collective-permute-done.15.refs_3_ = bf16[2,4,64,128]{3,2,1,0:T(8,128)(2,1)S(1)} collective-permute-done((bf16[2,4,64,128]{3,2,1,0:T(8,128)(2,1)S(1)}, bf16[2,4,64,128]{3,2,1,0:T(8,128)(2,1)S(1)}, u32[]{:S(2)}, u32[]{:S(2)}) %collective-permute-start.15) | collective-permute-done | bytes 131104 | tf_op jit(solution)/shard_map/ppermute | solution.py:67
  62.2 1.5 %collective-permute-start.24 = (bf16[4,256,128]{2,1,0:T(8,128)(2,1)S(1)}, bf16[4,256,128]{2,1,0:T(8,128)(2,1)S(1)}, u32[]{:S(2)}, u32[]{:S(2)}) collective-permute-start(bf16[4,256,128]{2,1,0:T(8,128)(2,1)S(1)} %get-tuple-element.217), channel_id=1, source_target_pairs={{0,2},{1,3},{2,0},{3,1},{4,6},{5,7},{6,4},{7,5},{8,10},{9,11},{10,... | collective-permute-start | bytes 786440 | tf_op jit(solution)/shard_map/ppermute | solution.py:67
  63.7 2.4 %collective-permute-start.20 = (bf16[2,4,64,128]{3,2,1,0:T(8,128)(2,1)S(1)}, bf16[2,4,64,128]{3,2,1,0:T(8,128)(2,1)S(1)}, u32[]{:S(2)}, u32[]{:S(2)}) collective-permute-start(bf16[2,4,64,128]{3,2,1,0:T(8,128)(2,1)S(1)} %get-tuple-element.209), channel_id=1, source_target_pairs={{0,8},{1,9},{2,10},{3,11},{4,12},{5,13},{6,14},{7,15},{8,0},{9,1},... | collective-permute-start | bytes 393224 | tf_op jit(solution)/shard_map/ppermute | solution.py:67
  66.2 2.0 %collective-permute-start.19 = (bf16[2,4,64,128]{3,2,1,0:T(8,128)(2,1)S(1)}, bf16[2,4,64,128]{3,2,1,0:T(8,128)(2,1)S(1)}, u32[]{:S(2)}, u32[]{:S(2)}) collective-permute-start(bf16[2,4,64,128]{3,2,1,0:T(8,128)(2,1)S(1)} %get-tuple-element.207), channel_id=1, source_target_pairs={{0,12},{1,13},{2,14},{3,15},{4,8},{5,9},{6,10},{7,11},{8,4},{9,5},... | collective-permute-start | bytes 393224 | tf_op jit(solution)/shard_map/ppermute | solution.py:67
  68.2 3.8 %attend.6 = (bf16[2,256,128]{2,1,0:T(8,128)(2,1)S(1)}, bf16[2,256,128]{2,1,0:T(8,128)(2,1)S(1)}, f32[2,512,128]{2,1,0:T(8,128)S(1)}, bf16[2,512,128]{2,1,0:T(8,128)(2,1)S(1)}) custom-call(s32[10,8,8]{2,1,0:T(8,128)S(1)} %copy.24.refs_0_, bf16[2,512,128]{2,1,0:T(8,128)(2,1)S(1)} %get-tuple-element.218.refs_1_, ...), custom_call_target="tpu_custom_call" | custom-call | flops 1024 | bytes 1024 | tf_op jit(solution)/shard_map/attend/pallas_call | solution.py:238
  73.1 3.5 %collective-permute-done.20.refs_3_ = bf16[2,4,64,128]{3,2,1,0:T(8,128)(2,1)S(1)} collective-permute-done((bf16[2,4,64,128]{3,2,1,0:T(8,128)(2,1)S(1)}, bf16[2,4,64,128]{3,2,1,0:T(8,128)(2,1)S(1)}, u32[]{:S(2)}, u32[]{:S(2)}) %collective-permute-start.20) | collective-permute-done | bytes 131104 | tf_op jit(solution)/shard_map/ppermute | solution.py:67
  78.9 3.8 %attend.7 = (bf16[2,256,128]{2,1,0:T(8,128)(2,1)S(1)}, bf16[2,256,128]{2,1,0:T(8,128)(2,1)S(1)}, f32[2,512,128]{2,1,0:T(8,128)S(1)}, bf16[512,128]{1,0:T(8,128)(2,1)S(1)}, bf16[512,128]{1,0:T(8,128)(2,1)S(1)}) custom-call(s32[10,8,8]{2,1,0:T(8,128)S(1)} %copy.24.refs_0_, bf16[2,512,128]{2,1,0:T(8,128)(2,1)S(1)} %get-tuple-element.234.refs_1_, ...), custom_call_target="tpu_custom_call" | custom-call | flops 1024 | bytes 1024 | tf_op jit(solution)/shard_map/attend/pallas_call | solution.py:238
  87.2 2.4 %collective-permute-done.30.refs_1_ = bf16[2,256,128]{2,1,0:T(8,128)(2,1)S(1)} collective-permute-done((bf16[2,256,128]{2,1,0:T(8,128)(2,1)S(1)}, bf16[2,256,128]{2,1,0:T(8,128)(2,1)S(1)}, u32[]{:S(2)}, u32[]{:S(2)}) %collective-permute-start.30) | collective-permute-done | bytes 131104 | tf_op jit(solution)/shard_map/ppermute | solution.py:67
  89.6 2.2 %collective-permute-done.31.refs_3_ = bf16[2,256,128]{2,1,0:T(8,128)(2,1)S(1)} collective-permute-done((bf16[2,256,128]{2,1,0:T(8,128)(2,1)S(1)}, bf16[2,256,128]{2,1,0:T(8,128)(2,1)S(1)}, u32[]{:S(2)}, u32[]{:S(2)}) %collective-permute-start.31) | collective-permute-done | bytes 131104 | tf_op jit(solution)/shard_map/ppermute | solution.py:67
  (68 shorter events, 16.6 us)
Async XLA Ops:
  2.7 15.8 %collective-permute-start.4 = (bf16[4,4,64,256]{3,2,1,0:T(8,128)(2,1)S(1)}, bf16[4,4,64,256]{3,2,1,0:T(8,128)(2,1)S(1)}, u32[]{:S(2)}, u32[]{:S(2)}) collective-permute-start(bf16[4,4,64,256]{3,2,1,0:T(8,128)(2,1)S(1)} %get-tuple-element.141), channel_id=1, source_target_pairs={{0,2},{1,3},{2,0},{3,1},{4,6},{5,7},{6,4},{7,5},{8,10},{9,11},{10,... | collective-permute-start | bytes 1572872 | tf_op jit(solution)/shard_map/ppermute | solution.py:67
  5.8 12.8 %collective-permute-start = (bf16[1,4,64,256]{3,2,1,0:T(8,128)(2,1)S(1)}, bf16[1,4,64,256]{3,2,1,0:T(8,128)(2,1)S(1)}, u32[]{:S(2)}, u32[]{:S(2)}) collective-permute-start(bf16[1,4,64,256]{3,2,1,0:T(8,128)(2,1)S(1)} %get-tuple-element.137), channel_id=1, source_target_pairs={{0,12},{1,13},{2,14},{3,15},{4,8},{5,9},{6,10},{7,11},{8,4},{9,5},... | collective-permute-start | bytes 393224 | tf_op jit(solution)/shard_map/ppermute | solution.py:67
  9.4 10.8 %collective-permute-start.1 = (bf16[1,4,64,256]{3,2,1,0:T(8,128)(2,1)S(1)}, bf16[1,4,64,256]{3,2,1,0:T(8,128)(2,1)S(1)}, u32[]{:S(2)}, u32[]{:S(2)}) collective-permute-start(bf16[1,4,64,256]{3,2,1,0:T(8,128)(2,1)S(1)} %get-tuple-element.138), channel_id=1, source_target_pairs={{0,8},{1,9},{2,10},{3,11},{4,12},{5,13},{6,14},{7,15},{8,0},{9,1},... | collective-permute-start | bytes 393224 | tf_op jit(solution)/shard_map/ppermute | solution.py:67
  9.4 14.3 %collective-permute-start.3 = (bf16[4,4,64,128]{3,2,1,0:T(8,128)(2,1)S(1)}, bf16[4,4,64,128]{3,2,1,0:T(8,128)(2,1)S(1)}, u32[]{:S(2)}, u32[]{:S(2)}) collective-permute-start(bf16[4,4,64,128]{3,2,1,0:T(8,128)(2,1)S(1)} %get-tuple-element.140), channel_id=1, source_target_pairs={{0,2},{1,3},{2,0},{3,1},{4,6},{5,7},{6,4},{7,5},{8,10},{9,11},{10,... | collective-permute-start | bytes 786440 | tf_op jit(solution)/shard_map/ppermute | solution.py:67
  9.9 10.3 %collective-permute-start.2 = (bf16[1,4,64,256]{3,2,1,0:T(8,128)(2,1)S(1)}, bf16[1,4,64,256]{3,2,1,0:T(8,128)(2,1)S(1)}, u32[]{:S(2)}, u32[]{:S(2)}) collective-permute-start(bf16[1,4,64,256]{3,2,1,0:T(8,128)(2,1)S(1)} %get-tuple-element.139), channel_id=1, source_target_pairs={{0,4},{1,5},{2,6},{3,7},{4,0},{5,1},{6,2},{7,3},{8,12},{9,13},{10,... | collective-permute-start | bytes 393224 | tf_op jit(solution)/shard_map/ppermute | solution.py:67
  20.2 10.6 %collective-permute-start.7 = (bf16[1,4,64,256]{3,2,1,0:T(8,128)(2,1)S(1)}, bf16[1,4,64,256]{3,2,1,0:T(8,128)(2,1)S(1)}, u32[]{:S(2)}, u32[]{:S(2)}) collective-permute-start(bf16[1,4,64,256]{3,2,1,0:T(8,128)(2,1)S(1)} %get-tuple-element.156), channel_id=1, source_target_pairs={{0,8},{1,9},{2,10},{3,11},{4,12},{5,13},{6,14},{7,15},{8,0},{9,1},... | collective-permute-start | bytes 393224 | tf_op jit(solution)/shard_map/ppermute | solution.py:67
  21.7 9.1 %collective-permute-start.6 = (bf16[1,4,64,256]{3,2,1,0:T(8,128)(2,1)S(1)}, bf16[1,4,64,256]{3,2,1,0:T(8,128)(2,1)S(1)}, u32[]{:S(2)}, u32[]{:S(2)}) collective-permute-start(bf16[1,4,64,256]{3,2,1,0:T(8,128)(2,1)S(1)} %get-tuple-element.155), channel_id=1, source_target_pairs={{0,12},{1,13},{2,14},{3,15},{4,8},{5,9},{6,10},{7,11},{8,4},{9,5},... | collective-permute-start | bytes 393224 | tf_op jit(solution)/shard_map/ppermute | solution.py:67
  23.1 8.6 %collective-permute-start.5 = (bf16[1,4,64,256]{3,2,1,0:T(8,128)(2,1)S(1)}, bf16[1,4,64,256]{3,2,1,0:T(8,128)(2,1)S(1)}, u32[]{:S(2)}, u32[]{:S(2)}) collective-permute-start(bf16[1,4,64,256]{3,2,1,0:T(8,128)(2,1)S(1)} %get-tuple-element.153), channel_id=1, source_target_pairs={{0,4},{1,5},{2,6},{3,7},{4,0},{5,1},{6,2},{7,3},{8,12},{9,13},{10,... | collective-permute-start | bytes 393224 | tf_op jit(solution)/shard_map/ppermute | solution.py:67
  31.9 15.0 %collective-permute-start.9 = (bf16[4,4,64,256]{3,2,1,0:T(8,128)(2,1)S(1)}, bf16[4,4,64,256]{3,2,1,0:T(8,128)(2,1)S(1)}, u32[]{:S(2)}, u32[]{:S(2)}) collective-permute-start(bf16[4,4,64,256]{3,2,1,0:T(8,128)(2,1)S(1)} %get-tuple-element.166), channel_id=1, source_target_pairs={{0,2},{1,3},{2,0},{3,1},{4,6},{5,7},{6,4},{7,5},{8,10},{9,11},{10,... | collective-permute-start | bytes 1572872 | tf_op jit(solution)/shard_map/ppermute | solution.py:67
  33.1 13.2 %collective-permute-start.12 = (bf16[2,4,64,128]{3,2,1,0:T(8,128)(2,1)}, bf16[2,4,64,128]{3,2,1,0:T(8,128)(2,1)S(1)}, u32[]{:S(2)}, u32[]{:S(2)}) collective-permute-start(bf16[2,4,64,128]{3,2,1,0:T(8,128)(2,1)} %get-tuple-element.173), channel_id=1, source_target_pairs={{0,8},{1,9},{2,10},{3,11},{4,12},{5,13},{6,14},{7,15},{8,0},{9,1},... | collective-permute-start | bytes 393224 | tf_op jit(solution)/shard_map/ppermute | solution.py:67
  36.1 10.2 %collective-permute-start.11 = (bf16[2,4,64,128]{3,2,1,0:T(8,128)(2,1)S(1)}, bf16[2,4,64,128]{3,2,1,0:T(8,128)(2,1)S(1)}, u32[]{:S(2)}, u32[]{:S(2)}) collective-permute-start(bf16[2,4,64,128]{3,2,1,0:T(8,128)(2,1)S(1)} %get-tuple-element.172), channel_id=1, source_target_pairs={{0,12},{1,13},{2,14},{3,15},{4,8},{5,9},{6,10},{7,11},{8,4},{9,5},... | collective-permute-start | bytes 393224 | tf_op jit(solution)/shard_map/ppermute | solution.py:67
  37.4 9.5 %collective-permute-start.10 = (bf16[2,4,64,128]{3,2,1,0:T(8,128)(2,1)S(1)}, bf16[2,4,64,128]{3,2,1,0:T(8,128)(2,1)S(1)}, u32[]{:S(2)}, u32[]{:S(2)}) collective-permute-start(bf16[2,4,64,128]{3,2,1,0:T(8,128)(2,1)S(1)} %get-tuple-element.170), channel_id=1, source_target_pairs={{0,4},{1,5},{2,6},{3,7},{4,0},{5,1},{6,2},{7,3},{8,12},{9,13},{10,... | collective-permute-start | bytes 393224 | tf_op jit(solution)/shard_map/ppermute | solution.py:67
  47.2 14.9 %collective-permute-start.21 = (bf16[4,256,256]{2,1,0:T(8,128)(2,1)S(1)}, bf16[4,256,256]{2,1,0:T(8,128)(2,1)S(1)}, u32[]{:S(2)}, u32[]{:S(2)}) collective-permute-start(bf16[4,256,256]{2,1,0:T(8,128)(2,1)S(1)} %get-tuple-element.193), channel_id=1, source_target_pairs={{0,2},{1,3},{2,0},{3,1},{4,6},{5,7},{6,4},{7,5},{8,10},{9,11},{10,... | collective-permute-start | bytes 1572872 | tf_op jit(solution)/shard_map/ppermute | solution.py:67
  47.8 12.9 %collective-permute-start.15 = (bf16[2,4,64,128]{3,2,1,0:T(8,128)(2,1)S(1)}, bf16[2,4,64,128]{3,2,1,0:T(8,128)(2,1)S(1)}, u32[]{:S(2)}, u32[]{:S(2)}) collective-permute-start(bf16[2,4,64,128]{3,2,1,0:T(8,128)(2,1)S(1)} %get-tuple-element.187), channel_id=1, source_target_pairs={{0,8},{1,9},{2,10},{3,11},{4,12},{5,13},{6,14},{7,15},{8,0},{9,1},... | collective-permute-start | bytes 393224 | tf_op jit(solution)/shard_map/ppermute | solution.py:67
  50.7 10.1 %collective-permute-start.14 = (bf16[2,4,64,128]{3,2,1,0:T(8,128)(2,1)S(1)}, bf16[2,4,64,128]{3,2,1,0:T(8,128)(2,1)S(1)}, u32[]{:S(2)}, u32[]{:S(2)}) collective-permute-start(bf16[2,4,64,128]{3,2,1,0:T(8,128)(2,1)S(1)} %get-tuple-element.185), channel_id=1, source_target_pairs={{0,12},{1,13},{2,14},{3,15},{4,8},{5,9},{6,10},{7,11},{8,4},{9,5},... | collective-permute-start | bytes 393224 | tf_op jit(solution)/shard_map/ppermute | solution.py:67
  52.5 9.4 %collective-permute-start.13 = (bf16[2,4,64,128]{3,2,1,0:T(8,128)(2,1)S(1)}, bf16[2,4,64,128]{3,2,1,0:T(8,128)(2,1)S(1)}, u32[]{:S(2)}, u32[]{:S(2)}) collective-permute-start(bf16[2,4,64,128]{3,2,1,0:T(8,128)(2,1)S(1)} %get-tuple-element.183), channel_id=1, source_target_pairs={{0,4},{1,5},{2,6},{3,7},{4,0},{5,1},{6,2},{7,3},{8,12},{9,13},{10,... | collective-permute-start | bytes 393224 | tf_op jit(solution)/shard_map/ppermute | solution.py:67
  61.9 6.2 %collective-permute-start.23 = (bf16[2,512,128]{2,1,0:T(8,128)(2,1)S(1)}, bf16[2,512,128]{2,1,0:T(8,128)(2,1)S(1)}, u32[]{:S(2)}, u32[]{:S(2)}) collective-permute-start(bf16[2,512,128]{2,1,0:T(8,128)(2,1)S(1)} %get-tuple-element.200.refs_2_), channel_id=1, source_target_pairs={{0,1},{1,0},{2,3},{3,2},{4,5},{5,4},{6,7},{7,6},{8,9},{9,8},{10,11... | collective-permute-start | bytes 786440 | tf_op jit(solution)/shard_map/ppermute | solution.py:67
  62.2 15.1 %collective-permute-start.24 = (bf16[4,256,128]{2,1,0:T(8,128)(2,1)S(1)}, bf16[4,256,128]{2,1,0:T(8,128)(2,1)S(1)}, u32[]{:S(2)}, u32[]{:S(2)}) collective-permute-start(bf16[4,256,128]{2,1,0:T(8,128)(2,1)S(1)} %get-tuple-element.217), channel_id=1, source_target_pairs={{0,2},{1,3},{2,0},{3,1},{4,6},{5,7},{6,4},{7,5},{8,10},{9,11},{10,... | collective-permute-start | bytes 786440 | tf_op jit(solution)/shard_map/ppermute | solution.py:67
  63.7 12.9 %collective-permute-start.20 = (bf16[2,4,64,128]{3,2,1,0:T(8,128)(2,1)S(1)}, bf16[2,4,64,128]{3,2,1,0:T(8,128)(2,1)S(1)}, u32[]{:S(2)}, u32[]{:S(2)}) collective-permute-start(bf16[2,4,64,128]{3,2,1,0:T(8,128)(2,1)S(1)} %get-tuple-element.209), channel_id=1, source_target_pairs={{0,8},{1,9},{2,10},{3,11},{4,12},{5,13},{6,14},{7,15},{8,0},{9,1},... | collective-permute-start | bytes 393224 | tf_op jit(solution)/shard_map/ppermute | solution.py:67
  66.2 10.5 %collective-permute-start.19 = (bf16[2,4,64,128]{3,2,1,0:T(8,128)(2,1)S(1)}, bf16[2,4,64,128]{3,2,1,0:T(8,128)(2,1)S(1)}, u32[]{:S(2)}, u32[]{:S(2)}) collective-permute-start(bf16[2,4,64,128]{3,2,1,0:T(8,128)(2,1)S(1)} %get-tuple-element.207), channel_id=1, source_target_pairs={{0,12},{1,13},{2,14},{3,15},{4,8},{5,9},{6,10},{7,11},{8,4},{9,5},... | collective-permute-start | bytes 393224 | tf_op jit(solution)/shard_map/ppermute | solution.py:67
  68.2 9.1 %collective-permute-start.18 = (bf16[2,4,64,128]{3,2,1,0:T(8,128)(2,1)S(1)}, bf16[2,4,64,128]{3,2,1,0:T(8,128)(2,1)S(1)}, u32[]{:S(2)}, u32[]{:S(2)}) collective-permute-start(bf16[2,4,64,128]{3,2,1,0:T(8,128)(2,1)S(1)} %get-tuple-element.205), channel_id=1, source_target_pairs={{0,4},{1,5},{2,6},{3,7},{4,0},{5,1},{6,2},{7,3},{8,12},{9,13},{10,... | collective-permute-start | bytes 393224 | tf_op jit(solution)/shard_map/ppermute | solution.py:67
  77.5 8.9 %collective-permute-start.29 = (bf16[4,256,128]{2,1,0:T(8,128)(2,1)S(1)}, bf16[4,256,128]{2,1,0:T(8,128)(2,1)S(1)}, u32[]{:S(2)}, u32[]{:S(2)}) collective-permute-start(bf16[4,256,128]{2,1,0:T(8,128)(2,1)S(1)} %get-tuple-element.233), channel_id=1, source_target_pairs={{0,2},{1,3},{2,0},{3,1},{4,6},{5,7},{6,4},{7,5},{8,10},{9,11},{10,... | collective-permute-start | bytes 786440 | tf_op jit(solution)/shard_map/ppermute | solution.py:67
  83.3 6.3 %collective-permute-start.30 = (bf16[2,256,128]{2,1,0:T(8,128)(2,1)S(1)}, bf16[2,256,128]{2,1,0:T(8,128)(2,1)S(1)}, u32[]{:S(2)}, u32[]{:S(2)}) collective-permute-start(bf16[2,256,128]{2,1,0:T(8,128)(2,1)S(1)} %get-tuple-element.255), channel_id=1, source_target_pairs={{0,2},{1,3},{2,0},{3,1},{4,6},{5,7},{6,4},{7,5},{8,10},{9,11},{10,... | collective-permute-start | bytes 393224 | tf_op jit(solution)/shard_map/ppermute | solution.py:67
  84.4 7.5 %collective-permute-start.31 = (bf16[2,256,128]{2,1,0:T(8,128)(2,1)S(1)}, bf16[2,256,128]{2,1,0:T(8,128)(2,1)S(1)}, u32[]{:S(2)}, u32[]{:S(2)}) collective-permute-start(bf16[2,256,128]{2,1,0:T(8,128)(2,1)S(1)} %get-tuple-element.257), channel_id=1, source_target_pairs={{0,2},{1,3},{2,0},{3,1},{4,6},{5,7},{6,4},{7,5},{8,10},{9,11},{10,... | collective-permute-start | bytes 393224 | tf_op jit(solution)/shard_map/ppermute | solution.py:67
  (9 other events, 34.4 us)

commit v5 on v4

--- a/solution.py
+++ b/solution.py
@@ -36,8 +36,9 @@
     def __init__(self, rows, width, head_axis, frame_axis):
         self.rows = rows
         self.zn = head_axis
-        self.steps = [0, 1, 3, 2] if head_axis == 4 else list(range(head_axis))
-        self.first_steps = [0, 3, 2, 1] if head_axis == 4 else list(range(head_axis))
+        far = [head_axis - 1, head_axis - 2] if head_axis > 2 else range(1, head_axis)
+        self.steps = [0, *range(1, head_axis - 2), *far]
+        self.first_steps = [0, *range(head_axis - 1, 0, -1)]
         self.groups = width // HD // head_axis
         self.on = math.gcd(self.groups, frame_axis)
         self.inn = frame_axis // self.on
@@ -88,15 +89,22 @@
     def body(*refs):
         ins, outs, held, sem = refs[:4], refs[4:-2], refs[-2], refs[-1]
         z, o, _ = plan.place()
-        copies = [pltpu.make_async_copy(ref, held.at[a], sem.at[a]) for a, ref in enumerate(ins)]
+        group = plan.groups * HD
+        copies = []
+        for k in range(plan.zn):
+            at = pl.ds(pl.multiple_of(there(z, k, plan.zn) * group, HD), group)
+            for a, ref in enumerate(ins):
+                copies.append(
+                    pltpu.make_async_copy(ref.at[:, at], held.at[k, a], sem.at[len(copies)])
+                )
         for copy in copies:
             copy.start()
-        for copy in copies:
-            copy.wait()
-        for out, (step, first, heads) in zip(outs, blocks, strict=True):
-            for k in range(plan.zn):
-                at = plan.column(there(z, k, plan.zn), there(o, step, plan.on), first)
-                out[k] = held[:, :, pl.ds(at, heads * HD)]
+        for k in range(plan.zn):
+            for copy in copies[4 * k : 4 * k + 4]:
+                copy.wait()
+            for out, (step, first, heads) in zip(outs, blocks, strict=True):
+                at = pl.multiple_of((there(o, step, plan.on) * plan.mine + first) * HD, HD)
+                out[k] = held[k, :, :, pl.ds(at, heads * HD)]
 
     out = [shape(plan.zn, 4, plan.rows, heads * HD) for _, _, heads in blocks]
     arrays = [pltpu.with_memory_space_constraint(a, pltpu.HBM) for a in arrays]
@@ -106,8 +114,8 @@
         in_specs=[HBM] * 4,
         out_specs=[VMEM] * len(out),
         scratch_shapes=[
-            pltpu.VMEM((4, *arrays[0].shape), BF16),
-            pltpu.SemaphoreType.DMA((4,)),
+            pltpu.VMEM((plan.zn, 4, plan.rows, plan.groups * HD), BF16),
+            pltpu.SemaphoreType.DMA((4 * plan.zn,)),
         ],
         compiler_params=pltpu.CompilerParams(vmem_limit_bytes=VMEM_LIMIT),
         cost_estimate=SMALL,
@@ -325,7 +333,7 @@
 
 
 def chunk_list(plan):
-    sizes = [2, 1, 1, 1] if plan.mine == 5 else [1] * plan.mine
+    sizes = [2] + [1] * (plan.mine - 2) if plan.mine > 2 else [1] * plan.mine
     return [(sum(sizes[:n]), size) for n, size in enumerate(sizes)]
 
 
@@ -464,7 +472,10 @@
     final = sums(last, row_parts, key_parts, parts, False)
     for n in range(max(0, last - 2), last):
         outs = put(n, pieces[n], outs)
-    outs = put(last, final, outs)
+    late = [piece for piece in final if piece[0] and piece[1]]
+    outs = put(last, [piece for piece in final if not (piece[0] and piece[1])], outs)
+    if late:
+        outs = put(last, late, outs)
     return tuple(outs)
 
 

time: 93 us -> 92.9 us (level)
  waiting for transfers between devices: 32.9 us -> 31.9 us
    ppermute x32, waiting for transfers between devices: 32.9 us -> 31.9 us  [send(): return lax.ppermute(array, ('head', 'frame'), pairs)]
    pallas_call x4 -> x5, Pallas kernels: 3.58 us -> 4.26 us  [place(): pl.pallas_call(body, out_shape=out, in_specs=[VMEM] * len(pieces) + [HBM]...]
  transfers between devices with their start and end apart: 32 -> 32, of which waited for: 15 -> 15; matrix products, arithmetic and copies ran while one was open for 0% -> 0% of each run, Pallas kernels for 26% -> 27%
where the time goes in v5:
time: 92.9 us; the launch traced here: 92.7 us
  waiting for transfers between devices  31.9 us (34%)
  starting transfers between devices  31.5 us (34%)
  Pallas kernels  28.1 us (30%)
  between operations  1.08 us (1%)
    ppermute x32, waiting for transfers between devices, send(): return lax.ppermute(array, ('head', 'frame'), pairs)  31.9 us
    ppermute x32, starting transfers between devices, send(): return lax.ppermute(array, ('head', 'frame'), pairs)  31.5 us
    pallas_call x4, Pallas kernels, attend(): pl.pallas_call(functools.partial(attend_body, plan, first, heads, split),...  18.3 us
    pallas_call x5, Pallas kernels, place(): pl.pallas_call(body, out_shape=out, in_specs=[VMEM] * len(pieces) + [HBM]...  4.26 us
    pallas_call x2, Pallas kernels, pack_columns(): pl.pallas_call(body, out_shape=out, in_specs=[HBM] * 4, out_specs=[VMEM]...  3.96 us
  transfers between devices with their start and end apart: 32, of which 15 were waited for; matrix products, arithmetic and copies ran while one was open for 0% of the time, Pallas kernels for 27%

profile of v5, /device:TPU:0, one launch (start us, length us, event | category | flops | bytes accessed | tf_op | source)
XLA Modules:
  0.0 92.7 jit_solution(6756452364568004619)
XLA Ops:
  0.6 2.0 %pack_columns.2 = (bf16[4,4,64,256]{3,2,1,0:T(8,128)(2,1)S(1)}, bf16[4,4,64,128]{3,2,1,0:T(8,128)(2,1)S(1)}, bf16[4,4,64,256]{3,2,1,0:T(8,128)(2,1)S(1)}, bf16[4...) custom-call(bf16[64,5120]{1,0:T(8,128)(2,1)} %refs_0_.6, bf16[64,5120]{1,0:T(8,128)(2,1)} %refs_1_.2, ...), custom_call_target="tpu_custom_call" | custom-call | flops 1024 | bytes 1024 | tf_op jit(solution)/shard_map/pack_columns/pallas_call | solution.py:111
  2.6 3.0 %collective-permute-start.4 = (bf16[4,4,64,256]{3,2,1,0:T(8,128)(2,1)S(1)}, bf16[4,4,64,256]{3,2,1,0:T(8,128)(2,1)S(1)}, u32[]{:S(2)}, u32[]{:S(2)}) collective-permute-start(bf16[4,4,64,256]{3,2,1,0:T(8,128)(2,1)S(1)} %get-tuple-element.146), channel_id=1, source_target_pairs={{0,2},{1,3},{2,0},{3,1},{4,6},{5,7},{6,4},{7,5},{8,10},{9,11},{10,... | collective-permute-start | bytes 1572872 | tf_op jit(solution)/shard_map/ppermute | solution.py:68
  5.7 3.7 %collective-permute-start = (bf16[1,4,64,256]{3,2,1,0:T(8,128)(2,1)S(1)}, bf16[1,4,64,256]{3,2,1,0:T(8,128)(2,1)S(1)}, u32[]{:S(2)}, u32[]{:S(2)}) collective-permute-start(bf16[1,4,64,256]{3,2,1,0:T(8,128)(2,1)S(1)} %get-tuple-element.142), channel_id=1, source_target_pairs={{0,12},{1,13},{2,14},{3,15},{4,8},{5,9},{6,10},{7,11},{8,4},{9,5},... | collective-permute-start | bytes 393224 | tf_op jit(solution)/shard_map/ppermute | solution.py:68
  10.5 7.9 %collective-permute-done.4.refs_0_ = bf16[4,4,64,256]{3,2,1,0:T(8,128)(2,1)S(1)} collective-permute-done((bf16[4,4,64,256]{3,2,1,0:T(8,128)(2,1)S(1)}, bf16[4,4,64,256]{3,2,1,0:T(8,128)(2,1)S(1)}, u32[]{:S(2)}, u32[]{:S(2)}) %collective-permute-start.4) | collective-permute-done | bytes 524320 | tf_op jit(solution)/shard_map/ppermute | solution.py:68
  18.5 1.7 %collective-permute-done.1.refs_2_ = bf16[1,4,64,256]{3,2,1,0:T(8,128)(2,1)S(1)} collective-permute-done((bf16[1,4,64,256]{3,2,1,0:T(8,128)(2,1)S(1)}, bf16[1,4,64,256]{3,2,1,0:T(8,128)(2,1)S(1)}, u32[]{:S(2)}, u32[]{:S(2)}) %collective-permute-start.1) | collective-permute-done | bytes 131104 | tf_op jit(solution)/shard_map/ppermute | solution.py:68
  20.2 1.5 %collective-permute-start.7 = (bf16[1,4,64,256]{3,2,1,0:T(8,128)(2,1)S(1)}, bf16[1,4,64,256]{3,2,1,0:T(8,128)(2,1)S(1)}, u32[]{:S(2)}, u32[]{:S(2)}) collective-permute-start(bf16[1,4,64,256]{3,2,1,0:T(8,128)(2,1)S(1)} %get-tuple-element.161), channel_id=1, source_target_pairs={{0,8},{1,9},{2,10},{3,11},{4,12},{5,13},{6,14},{7,15},{8,0},{9,1},... | collective-permute-start | bytes 393224 | tf_op jit(solution)/shard_map/ppermute | solution.py:68
  21.7 1.3 %collective-permute-start.6 = (bf16[1,4,64,256]{3,2,1,0:T(8,128)(2,1)S(1)}, bf16[1,4,64,256]{3,2,1,0:T(8,128)(2,1)S(1)}, u32[]{:S(2)}, u32[]{:S(2)}) collective-permute-start(bf16[1,4,64,256]{3,2,1,0:T(8,128)(2,1)S(1)} %get-tuple-element.160), channel_id=1, source_target_pairs={{0,12},{1,13},{2,14},{3,15},{4,8},{5,9},{6,10},{7,11},{8,4},{9,5},... | collective-permute-start | bytes 393224 | tf_op jit(solution)/shard_map/ppermute | solution.py:68
  24.4 6.4 %collective-permute-done.7.refs_7_ = bf16[1,4,64,256]{3,2,1,0:T(8,128)(2,1)S(1)} collective-permute-done((bf16[1,4,64,256]{3,2,1,0:T(8,128)(2,1)S(1)}, bf16[1,4,64,256]{3,2,1,0:T(8,128)(2,1)S(1)}, u32[]{:S(2)}, u32[]{:S(2)}) %collective-permute-start.7) | collective-permute-done | bytes 131104 | tf_op jit(solution)/shard_map/ppermute | solution.py:68
  33.0 3.0 %collective-permute-start.12 = (bf16[2,4,64,128]{3,2,1,0:T(8,128)(2,1)}, bf16[2,4,64,128]{3,2,1,0:T(8,128)(2,1)S(1)}, u32[]{:S(2)}, u32[]{:S(2)}) collective-permute-start(bf16[2,4,64,128]{3,2,1,0:T(8,128)(2,1)} %get-tuple-element.178), channel_id=1, source_target_pairs={{0,8},{1,9},{2,10},{3,11},{4,12},{5,13},{6,14},{7,15},{8,0},{9,1},... | collective-permute-start | bytes 393224 | tf_op jit(solution)/shard_map/ppermute | solution.py:68
  36.0 1.3 %collective-permute-start.11 = (bf16[2,4,64,128]{3,2,1,0:T(8,128)(2,1)S(1)}, bf16[2,4,64,128]{3,2,1,0:T(8,128)(2,1)S(1)}, u32[]{:S(2)}, u32[]{:S(2)}) collective-permute-start(bf16[2,4,64,128]{3,2,1,0:T(8,128)(2,1)S(1)} %get-tuple-element.177), channel_id=1, source_target_pairs={{0,12},{1,13},{2,14},{3,15},{4,8},{5,9},{6,10},{7,11},{8,4},{9,5},... | collective-permute-start | bytes 393224 | tf_op jit(solution)/shard_map/ppermute | solution.py:68
  37.5 6.8 %attend.4 = (bf16[2,256,256]{2,1,0:T(8,128)(2,1)S(1)}, bf16[2,256,256]{2,1,0:T(8,128)(2,1)S(1)}, f32[2,512,256]{2,1,0:T(8,128)S(1)}, bf16[2,512,256]{2,1,0:T(8,128)(2,1)S(1)}) custom-call(s32[10,8,8]{2,1,0:T(8,128)S(1)} %copy.28.refs_0_, bf16[2,512,256]{2,1,0:T(8,128)(2,1)S(1)} %get-tuple-element.162.refs_1_, ...), custom_call_target="tpu_custom_call" | custom-call | flops 1024 | bytes 1024 | tf_op jit(solution)/shard_map/attend/pallas_call | solution.py:246
  44.4 2.0 %pack_columns.3 = (bf16[4,4,64,128]{3,2,1,0:T(8,128)(2,1)S(1)}, bf16[4,4,64,128]{3,2,1,0:T(8,128)(2,1)S(1)}) custom-call(bf16[64,5120]{1,0:T(8,128)(2,1)} %refs_0_.6, bf16[64,5120]{1,0:T(8,128)(2,1)} %refs_1_.2, bf16[64,5120]{1,0:T(8,128)(2,1)} %refs_2_.2, bf16[64,5120]{1,0:T(8,128)(2,1)} %refs_3_.2), custom_call_target="tpu_custom_call" | custom-call | flops 1024 | bytes 1024 | tf_op jit(solution)/shard_map/pack_columns/pallas_call | solution.py:111
  47.8 2.8 %collective-permute-start.15 = (bf16[2,4,64,128]{3,2,1,0:T(8,128)(2,1)S(1)}, bf16[2,4,64,128]{3,2,1,0:T(8,128)(2,1)S(1)}, u32[]{:S(2)}, u32[]{:S(2)}) collective-permute-start(bf16[2,4,64,128]{3,2,1,0:T(8,128)(2,1)S(1)} %get-tuple-element.192), channel_id=1, source_target_pairs={{0,8},{1,9},{2,10},{3,11},{4,12},{5,13},{6,14},{7,15},{8,0},{9,1},... | collective-permute-start | bytes 393224 | tf_op jit(solution)/shard_map/ppermute | solution.py:68
  50.7 1.8 %collective-permute-start.14 = (bf16[2,4,64,128]{3,2,1,0:T(8,128)(2,1)S(1)}, bf16[2,4,64,128]{3,2,1,0:T(8,128)(2,1)S(1)}, u32[]{:S(2)}, u32[]{:S(2)}) collective-permute-start(bf16[2,4,64,128]{3,2,1,0:T(8,128)(2,1)S(1)} %get-tuple-element.190), channel_id=1, source_target_pairs={{0,12},{1,13},{2,14},{3,15},{4,8},{5,9},{6,10},{7,11},{8,4},{9,5},... | collective-permute-start | bytes 393224 | tf_op jit(solution)/shard_map/ppermute | solution.py:68
  52.4 3.9 %attend.5 = (bf16[2,256,128]{2,1,0:T(8,128)(2,1)S(1)}, bf16[2,256,128]{2,1,0:T(8,128)(2,1)S(1)}, f32[2,512,128]{2,1,0:T(8,128)S(1)}, bf16[2,512,128]{2,1,0:T(8,128)(2,1)S(1)}) custom-call(s32[10,8,8]{2,1,0:T(8,128)S(1)} %copy.28.refs_0_, bf16[2,512,128]{2,1,0:T(8,128)(2,1)S(1)} %get-tuple-element.199.refs_1_, ...), custom_call_target="tpu_custom_call" | custom-call | flops 1024 | bytes 1024 | tf_op jit(solution)/shard_map/attend/pallas_call | solution.py:246
  56.4 4.4 %collective-permute-done.15.refs_3_ = bf16[2,4,64,128]{3,2,1,0:T(8,128)(2,1)S(1)} collective-permute-done((bf16[2,4,64,128]{3,2,1,0:T(8,128)(2,1)S(1)}, bf16[2,4,64,128]{3,2,1,0:T(8,128)(2,1)S(1)}, u32[]{:S(2)}, u32[]{:S(2)}) %collective-permute-start.15) | collective-permute-done | bytes 131104 | tf_op jit(solution)/shard_map/ppermute | solution.py:68
  62.2 1.5 %collective-permute-start.24 = (bf16[4,256,128]{2,1,0:T(8,128)(2,1)S(1)}, bf16[4,256,128]{2,1,0:T(8,128)(2,1)S(1)}, u32[]{:S(2)}, u32[]{:S(2)}) collective-permute-start(bf16[4,256,128]{2,1,0:T(8,128)(2,1)S(1)} %get-tuple-element.222), channel_id=1, source_target_pairs={{0,2},{1,3},{2,0},{3,1},{4,6},{5,7},{6,4},{7,5},{8,10},{9,11},{10,... | collective-permute-start | bytes 786440 | tf_op jit(solution)/shard_map/ppermute | solution.py:68
  63.7 2.4 %collective-permute-start.20 = (bf16[2,4,64,128]{3,2,1,0:T(8,128)(2,1)S(1)}, bf16[2,4,64,128]{3,2,1,0:T(8,128)(2,1)S(1)}, u32[]{:S(2)}, u32[]{:S(2)}) collective-permute-start(bf16[2,4,64,128]{3,2,1,0:T(8,128)(2,1)S(1)} %get-tuple-element.214), channel_id=1, source_target_pairs={{0,8},{1,9},{2,10},{3,11},{4,12},{5,13},{6,14},{7,15},{8,0},{9,1},... | collective-permute-start | bytes 393224 | tf_op jit(solution)/shard_map/ppermute | solution.py:68
  66.1 2.0 %collective-permute-start.19 = (bf16[2,4,64,128]{3,2,1,0:T(8,128)(2,1)S(1)}, bf16[2,4,64,128]{3,2,1,0:T(8,128)(2,1)S(1)}, u32[]{:S(2)}, u32[]{:S(2)}) collective-permute-start(bf16[2,4,64,128]{3,2,1,0:T(8,128)(2,1)S(1)} %get-tuple-element.212), channel_id=1, source_target_pairs={{0,12},{1,13},{2,14},{3,15},{4,8},{5,9},{6,10},{7,11},{8,4},{9,5},... | collective-permute-start | bytes 393224 | tf_op jit(solution)/shard_map/ppermute | solution.py:68
  68.1 3.8 %attend.6 = (bf16[2,256,128]{2,1,0:T(8,128)(2,1)S(1)}, bf16[2,256,128]{2,1,0:T(8,128)(2,1)S(1)}, f32[2,512,128]{2,1,0:T(8,128)S(1)}, bf16[2,512,128]{2,1,0:T(8,128)(2,1)S(1)}) custom-call(s32[10,8,8]{2,1,0:T(8,128)S(1)} %copy.28.refs_0_, bf16[2,512,128]{2,1,0:T(8,128)(2,1)S(1)} %get-tuple-element.223.refs_1_, ...), custom_call_target="tpu_custom_call" | custom-call | flops 1024 | bytes 1024 | tf_op jit(solution)/shard_map/attend/pallas_call | solution.py:246
  73.1 3.5 %collective-permute-done.20.refs_3_ = bf16[2,4,64,128]{3,2,1,0:T(8,128)(2,1)S(1)} collective-permute-done((bf16[2,4,64,128]{3,2,1,0:T(8,128)(2,1)S(1)}, bf16[2,4,64,128]{3,2,1,0:T(8,128)(2,1)S(1)}, u32[]{:S(2)}, u32[]{:S(2)}) %collective-permute-start.20) | collective-permute-done | bytes 131104 | tf_op jit(solution)/shard_map/ppermute | solution.py:68
  78.8 3.8 %attend.7 = (bf16[2,256,128]{2,1,0:T(8,128)(2,1)S(1)}, bf16[2,256,128]{2,1,0:T(8,128)(2,1)S(1)}, f32[2,512,128]{2,1,0:T(8,128)S(1)}, bf16[512,128]{1,0:T(8,128)(2,1)S(1)}, bf16[512,128]{1,0:T(8,128)(2,1)S(1)}) custom-call(s32[10,8,8]{2,1,0:T(8,128)S(1)} %copy.28.refs_0_, bf16[2,512,128]{2,1,0:T(8,128)(2,1)S(1)} %get-tuple-element.239.refs_1_, ...), custom_call_target="tpu_custom_call" | custom-call | flops 1024 | bytes 1024 | tf_op jit(solution)/shard_map/attend/pallas_call | solution.py:246
  87.2 2.4 %collective-permute-done.31.refs_1_ = bf16[2,256,128]{2,1,0:T(8,128)(2,1)S(1)} collective-permute-done((bf16[2,256,128]{2,1,0:T(8,128)(2,1)S(1)}, bf16[2,256,128]{2,1,0:T(8,128)(2,1)S(1)}, u32[]{:S(2)}, u32[]{:S(2)}) %collective-permute-start.31) | collective-permute-done | bytes 131104 | tf_op jit(solution)/shard_map/ppermute | solution.py:68
  90.4 1.4 %collective-permute-done.29.refs_0_ = bf16[2,256,128]{2,1,0:T(8,128)(2,1)S(1)} collective-permute-done((bf16[2,256,128]{2,1,0:T(8,128)(2,1)S(1)}, bf16[2,256,128]{2,1,0:T(8,128)(2,1)S(1)}, u32[]{:S(2)}, u32[]{:S(2)}) %collective-permute-start.29) | collective-permute-done | bytes 131104 | tf_op jit(solution)/shard_map/ppermute | solution.py:68
  (69 shorter events, 17.2 us)
Async XLA Ops:
  2.6 15.8 %collective-permute-start.4 = (bf16[4,4,64,256]{3,2,1,0:T(8,128)(2,1)S(1)}, bf16[4,4,64,256]{3,2,1,0:T(8,128)(2,1)S(1)}, u32[]{:S(2)}, u32[]{:S(2)}) collective-permute-start(bf16[4,4,64,256]{3,2,1,0:T(8,128)(2,1)S(1)} %get-tuple-element.146), channel_id=1, source_target_pairs={{0,2},{1,3},{2,0},{3,1},{4,6},{5,7},{6,4},{7,5},{8,10},{9,11},{10,... | collective-permute-start | bytes 1572872 | tf_op jit(solution)/shard_map/ppermute | solution.py:68
  5.7 12.8 %collective-permute-start = (bf16[1,4,64,256]{3,2,1,0:T(8,128)(2,1)S(1)}, bf16[1,4,64,256]{3,2,1,0:T(8,128)(2,1)S(1)}, u32[]{:S(2)}, u32[]{:S(2)}) collective-permute-start(bf16[1,4,64,256]{3,2,1,0:T(8,128)(2,1)S(1)} %get-tuple-element.142), channel_id=1, source_target_pairs={{0,12},{1,13},{2,14},{3,15},{4,8},{5,9},{6,10},{7,11},{8,4},{9,5},... | collective-permute-start | bytes 393224 | tf_op jit(solution)/shard_map/ppermute | solution.py:68
  9.4 10.8 %collective-permute-start.1 = (bf16[1,4,64,256]{3,2,1,0:T(8,128)(2,1)S(1)}, bf16[1,4,64,256]{3,2,1,0:T(8,128)(2,1)S(1)}, u32[]{:S(2)}, u32[]{:S(2)}) collective-permute-start(bf16[1,4,64,256]{3,2,1,0:T(8,128)(2,1)S(1)} %get-tuple-element.143), channel_id=1, source_target_pairs={{0,8},{1,9},{2,10},{3,11},{4,12},{5,13},{6,14},{7,15},{8,0},{9,1},... | collective-permute-start | bytes 393224 | tf_op jit(solution)/shard_map/ppermute | solution.py:68
  9.4 14.3 %collective-permute-start.3 = (bf16[4,4,64,128]{3,2,1,0:T(8,128)(2,1)S(1)}, bf16[4,4,64,128]{3,2,1,0:T(8,128)(2,1)S(1)}, u32[]{:S(2)}, u32[]{:S(2)}) collective-permute-start(bf16[4,4,64,128]{3,2,1,0:T(8,128)(2,1)S(1)} %get-tuple-element.145), channel_id=1, source_target_pairs={{0,2},{1,3},{2,0},{3,1},{4,6},{5,7},{6,4},{7,5},{8,10},{9,11},{10,... | collective-permute-start | bytes 786440 | tf_op jit(solution)/shard_map/ppermute | solution.py:68
  9.9 10.3 %collective-permute-start.2 = (bf16[1,4,64,256]{3,2,1,0:T(8,128)(2,1)S(1)}, bf16[1,4,64,256]{3,2,1,0:T(8,128)(2,1)S(1)}, u32[]{:S(2)}, u32[]{:S(2)}) collective-permute-start(bf16[1,4,64,256]{3,2,1,0:T(8,128)(2,1)S(1)} %get-tuple-element.144), channel_id=1, source_target_pairs={{0,4},{1,5},{2,6},{3,7},{4,0},{5,1},{6,2},{7,3},{8,12},{9,13},{10,... | collective-permute-start | bytes 393224 | tf_op jit(solution)/shard_map/ppermute | solution.py:68
  20.2 10.6 %collective-permute-start.7 = (bf16[1,4,64,256]{3,2,1,0:T(8,128)(2,1)S(1)}, bf16[1,4,64,256]{3,2,1,0:T(8,128)(2,1)S(1)}, u32[]{:S(2)}, u32[]{:S(2)}) collective-permute-start(bf16[1,4,64,256]{3,2,1,0:T(8,128)(2,1)S(1)} %get-tuple-element.161), channel_id=1, source_target_pairs={{0,8},{1,9},{2,10},{3,11},{4,12},{5,13},{6,14},{7,15},{8,0},{9,1},... | collective-permute-start | bytes 393224 | tf_op jit(solution)/shard_map/ppermute | solution.py:68
  21.7 9.1 %collective-permute-start.6 = (bf16[1,4,64,256]{3,2,1,0:T(8,128)(2,1)S(1)}, bf16[1,4,64,256]{3,2,1,0:T(8,128)(2,1)S(1)}, u32[]{:S(2)}, u32[]{:S(2)}) collective-permute-start(bf16[1,4,64,256]{3,2,1,0:T(8,128)(2,1)S(1)} %get-tuple-element.160), channel_id=1, source_target_pairs={{0,12},{1,13},{2,14},{3,15},{4,8},{5,9},{6,10},{7,11},{8,4},{9,5},... | collective-permute-start | bytes 393224 | tf_op jit(solution)/shard_map/ppermute | solution.py:68
  23.0 8.6 %collective-permute-start.5 = (bf16[1,4,64,256]{3,2,1,0:T(8,128)(2,1)S(1)}, bf16[1,4,64,256]{3,2,1,0:T(8,128)(2,1)S(1)}, u32[]{:S(2)}, u32[]{:S(2)}) collective-permute-start(bf16[1,4,64,256]{3,2,1,0:T(8,128)(2,1)S(1)} %get-tuple-element.158), channel_id=1, source_target_pairs={{0,4},{1,5},{2,6},{3,7},{4,0},{5,1},{6,2},{7,3},{8,12},{9,13},{10,... | collective-permute-start | bytes 393224 | tf_op jit(solution)/shard_map/ppermute | solution.py:68
  31.8 15.0 %collective-permute-start.9 = (bf16[4,4,64,256]{3,2,1,0:T(8,128)(2,1)S(1)}, bf16[4,4,64,256]{3,2,1,0:T(8,128)(2,1)S(1)}, u32[]{:S(2)}, u32[]{:S(2)}) collective-permute-start(bf16[4,4,64,256]{3,2,1,0:T(8,128)(2,1)S(1)} %get-tuple-element.171), channel_id=1, source_target_pairs={{0,2},{1,3},{2,0},{3,1},{4,6},{5,7},{6,4},{7,5},{8,10},{9,11},{10,... | collective-permute-start | bytes 1572872 | tf_op jit(solution)/shard_map/ppermute | solution.py:68
  33.0 13.4 %collective-permute-start.12 = (bf16[2,4,64,128]{3,2,1,0:T(8,128)(2,1)}, bf16[2,4,64,128]{3,2,1,0:T(8,128)(2,1)S(1)}, u32[]{:S(2)}, u32[]{:S(2)}) collective-permute-start(bf16[2,4,64,128]{3,2,1,0:T(8,128)(2,1)} %get-tuple-element.178), channel_id=1, source_target_pairs={{0,8},{1,9},{2,10},{3,11},{4,12},{5,13},{6,14},{7,15},{8,0},{9,1},... | collective-permute-start | bytes 393224 | tf_op jit(solution)/shard_map/ppermute | solution.py:68
  36.0 10.3 %collective-permute-start.11 = (bf16[2,4,64,128]{3,2,1,0:T(8,128)(2,1)S(1)}, bf16[2,4,64,128]{3,2,1,0:T(8,128)(2,1)S(1)}, u32[]{:S(2)}, u32[]{:S(2)}) collective-permute-start(bf16[2,4,64,128]{3,2,1,0:T(8,128)(2,1)S(1)} %get-tuple-element.177), channel_id=1, source_target_pairs={{0,12},{1,13},{2,14},{3,15},{4,8},{5,9},{6,10},{7,11},{8,4},{9,5},... | collective-permute-start | bytes 393224 | tf_op jit(solution)/shard_map/ppermute | solution.py:68
  37.4 9.5 %collective-permute-start.10 = (bf16[2,4,64,128]{3,2,1,0:T(8,128)(2,1)S(1)}, bf16[2,4,64,128]{3,2,1,0:T(8,128)(2,1)S(1)}, u32[]{:S(2)}, u32[]{:S(2)}) collective-permute-start(bf16[2,4,64,128]{3,2,1,0:T(8,128)(2,1)S(1)} %get-tuple-element.175), channel_id=1, source_target_pairs={{0,4},{1,5},{2,6},{3,7},{4,0},{5,1},{6,2},{7,3},{8,12},{9,13},{10,... | collective-permute-start | bytes 393224 | tf_op jit(solution)/shard_map/ppermute | solution.py:68
  47.1 14.9 %collective-permute-start.21 = (bf16[4,256,256]{2,1,0:T(8,128)(2,1)S(1)}, bf16[4,256,256]{2,1,0:T(8,128)(2,1)S(1)}, u32[]{:S(2)}, u32[]{:S(2)}) collective-permute-start(bf16[4,256,256]{2,1,0:T(8,128)(2,1)S(1)} %get-tuple-element.198), channel_id=1, source_target_pairs={{0,2},{1,3},{2,0},{3,1},{4,6},{5,7},{6,4},{7,5},{8,10},{9,11},{10,... | collective-permute-start | bytes 1572872 | tf_op jit(solution)/shard_map/ppermute | solution.py:68
  47.8 12.9 %collective-permute-start.15 = (bf16[2,4,64,128]{3,2,1,0:T(8,128)(2,1)S(1)}, bf16[2,4,64,128]{3,2,1,0:T(8,128)(2,1)S(1)}, u32[]{:S(2)}, u32[]{:S(2)}) collective-permute-start(bf16[2,4,64,128]{3,2,1,0:T(8,128)(2,1)S(1)} %get-tuple-element.192), channel_id=1, source_target_pairs={{0,8},{1,9},{2,10},{3,11},{4,12},{5,13},{6,14},{7,15},{8,0},{9,1},... | collective-permute-start | bytes 393224 | tf_op jit(solution)/shard_map/ppermute | solution.py:68
  50.7 10.1 %collective-permute-start.14 = (bf16[2,4,64,128]{3,2,1,0:T(8,128)(2,1)S(1)}, bf16[2,4,64,128]{3,2,1,0:T(8,128)(2,1)S(1)}, u32[]{:S(2)}, u32[]{:S(2)}) collective-permute-start(bf16[2,4,64,128]{3,2,1,0:T(8,128)(2,1)S(1)} %get-tuple-element.190), channel_id=1, source_target_pairs={{0,12},{1,13},{2,14},{3,15},{4,8},{5,9},{6,10},{7,11},{8,4},{9,5},... | collective-permute-start | bytes 393224 | tf_op jit(solution)/shard_map/ppermute | solution.py:68
  52.4 9.4 %collective-permute-start.13 = (bf16[2,4,64,128]{3,2,1,0:T(8,128)(2,1)S(1)}, bf16[2,4,64,128]{3,2,1,0:T(8,128)(2,1)S(1)}, u32[]{:S(2)}, u32[]{:S(2)}) collective-permute-start(bf16[2,4,64,128]{3,2,1,0:T(8,128)(2,1)S(1)} %get-tuple-element.188), channel_id=1, source_target_pairs={{0,4},{1,5},{2,6},{3,7},{4,0},{5,1},{6,2},{7,3},{8,12},{9,13},{10,... | collective-permute-start | bytes 393224 | tf_op jit(solution)/shard_map/ppermute | solution.py:68
  61.9 6.2 %collective-permute-start.23 = (bf16[2,512,128]{2,1,0:T(8,128)(2,1)S(1)}, bf16[2,512,128]{2,1,0:T(8,128)(2,1)S(1)}, u32[]{:S(2)}, u32[]{:S(2)}) collective-permute-start(bf16[2,512,128]{2,1,0:T(8,128)(2,1)S(1)} %get-tuple-element.205.refs_2_), channel_id=1, source_target_pairs={{0,1},{1,0},{2,3},{3,2},{4,5},{5,4},{6,7},{7,6},{8,9},{9,8},{10,11... | collective-permute-start | bytes 786440 | tf_op jit(solution)/shard_map/ppermute | solution.py:68
  62.2 15.1 %collective-permute-start.24 = (bf16[4,256,128]{2,1,0:T(8,128)(2,1)S(1)}, bf16[4,256,128]{2,1,0:T(8,128)(2,1)S(1)}, u32[]{:S(2)}, u32[]{:S(2)}) collective-permute-start(bf16[4,256,128]{2,1,0:T(8,128)(2,1)S(1)} %get-tuple-element.222), channel_id=1, source_target_pairs={{0,2},{1,3},{2,0},{3,1},{4,6},{5,7},{6,4},{7,5},{8,10},{9,11},{10,... | collective-permute-start | bytes 786440 | tf_op jit(solution)/shard_map/ppermute | solution.py:68
  63.7 12.9 %collective-permute-start.20 = (bf16[2,4,64,128]{3,2,1,0:T(8,128)(2,1)S(1)}, bf16[2,4,64,128]{3,2,1,0:T(8,128)(2,1)S(1)}, u32[]{:S(2)}, u32[]{:S(2)}) collective-permute-start(bf16[2,4,64,128]{3,2,1,0:T(8,128)(2,1)S(1)} %get-tuple-element.214), channel_id=1, source_target_pairs={{0,8},{1,9},{2,10},{3,11},{4,12},{5,13},{6,14},{7,15},{8,0},{9,1},... | collective-permute-start | bytes 393224 | tf_op jit(solution)/shard_map/ppermute | solution.py:68
  66.1 10.5 %collective-permute-start.19 = (bf16[2,4,64,128]{3,2,1,0:T(8,128)(2,1)S(1)}, bf16[2,4,64,128]{3,2,1,0:T(8,128)(2,1)S(1)}, u32[]{:S(2)}, u32[]{:S(2)}) collective-permute-start(bf16[2,4,64,128]{3,2,1,0:T(8,128)(2,1)S(1)} %get-tuple-element.212), channel_id=1, source_target_pairs={{0,12},{1,13},{2,14},{3,15},{4,8},{5,9},{6,10},{7,11},{8,4},{9,5},... | collective-permute-start | bytes 393224 | tf_op jit(solution)/shard_map/ppermute | solution.py:68
  68.1 9.1 %collective-permute-start.18 = (bf16[2,4,64,128]{3,2,1,0:T(8,128)(2,1)S(1)}, bf16[2,4,64,128]{3,2,1,0:T(8,128)(2,1)S(1)}, u32[]{:S(2)}, u32[]{:S(2)}) collective-permute-start(bf16[2,4,64,128]{3,2,1,0:T(8,128)(2,1)S(1)} %get-tuple-element.210), channel_id=1, source_target_pairs={{0,4},{1,5},{2,6},{3,7},{4,0},{5,1},{6,2},{7,3},{8,12},{9,13},{10,... | collective-permute-start | bytes 393224 | tf_op jit(solution)/shard_map/ppermute | solution.py:68
  77.4 8.9 %collective-permute-start.30 = (bf16[4,256,128]{2,1,0:T(8,128)(2,1)S(1)}, bf16[4,256,128]{2,1,0:T(8,128)(2,1)S(1)}, u32[]{:S(2)}, u32[]{:S(2)}) collective-permute-start(bf16[4,256,128]{2,1,0:T(8,128)(2,1)S(1)} %get-tuple-element.238), channel_id=1, source_target_pairs={{0,2},{1,3},{2,0},{3,1},{4,6},{5,7},{6,4},{7,5},{8,10},{9,11},{10,... | collective-permute-start | bytes 786440 | tf_op jit(solution)/shard_map/ppermute | solution.py:68
  83.2 6.4 %collective-permute-start.31 = (bf16[2,256,128]{2,1,0:T(8,128)(2,1)S(1)}, bf16[2,256,128]{2,1,0:T(8,128)(2,1)S(1)}, u32[]{:S(2)}, u32[]{:S(2)}) collective-permute-start(bf16[2,256,128]{2,1,0:T(8,128)(2,1)S(1)} %get-tuple-element.261), channel_id=1, source_target_pairs={{0,2},{1,3},{2,0},{3,1},{4,6},{5,7},{6,4},{7,5},{8,10},{9,11},{10,... | collective-permute-start | bytes 393224 | tf_op jit(solution)/shard_map/ppermute | solution.py:68
  84.3 7.5 %collective-permute-start.29 = (bf16[2,256,128]{2,1,0:T(8,128)(2,1)S(1)}, bf16[2,256,128]{2,1,0:T(8,128)(2,1)S(1)}, u32[]{:S(2)}, u32[]{:S(2)}) collective-permute-start(bf16[2,256,128]{2,1,0:T(8,128)(2,1)S(1)} %get-tuple-element.245), channel_id=1, source_target_pairs={{0,2},{1,3},{2,0},{3,1},{4,6},{5,7},{6,4},{7,5},{8,10},{9,11},{10,... | collective-permute-start | bytes 393224 | tf_op jit(solution)/shard_map/ppermute | solution.py:68
  (9 other events, 34.4 us)

commit v6 on v5

--- a/solution.py
+++ b/solution.py
@@ -317,7 +317,7 @@
         in_specs=[VMEM] * len(pieces) + [HBM] * len(outs),
         out_specs=[HBM] * 4,
         input_output_aliases={len(pieces) + n: n for n in range(len(outs))},
-        scratch_shapes=[pltpu.SemaphoreType.DMA((4 * plan.on,))],
+        scratch_shapes=[pltpu.SemaphoreType.DMA((8 * plan.on,))],
         compiler_params=pltpu.CompilerParams(vmem_limit_bytes=VMEM_LIMIT),
         cost_estimate=SMALL,
         name="place",
@@ -466,7 +466,11 @@
             copies = line.ran(take_in(line.tie([a for _, _, a in came])))
             kept = [piece for piece in pieces[n - 1] if not piece[0]]
             pieces[n - 1] = kept + [(s, w, a) for (s, w, _), a in zip(came, copies, strict=True)]
-        pieces.append(sums(n, *results, True))
+        if n == last - 2:
+            row_parts, key_parts, parts = results
+            pieces.append(sums(n, give_back(row_parts), key_parts, parts, False))
+        else:
+            pieces.append(sums(n, *results, True))
     row_parts, key_parts, parts = work(last)
     row_parts = give_back(row_parts)
     final = sums(last, row_parts, key_parts, parts, False)

time: 92.9 us -> 91.9 us (0.989)
  waiting for transfers between devices: 31.9 us -> 28.9 us
  starting transfers between devices: 31.5 us -> 33.2 us
    ppermute x32 -> x33, waiting for transfers between devices: 31.9 us -> 28.9 us  [send(): return lax.ppermute(array, ('head', 'frame'), pairs)]
    ppermute x32 -> x33, starting transfers between devices: 31.5 us -> 33.2 us  [send(): return lax.ppermute(array, ('head', 'frame'), pairs)]
  transfers between devices with their start and end apart: 32 -> 33, of which waited for: 15 -> 13; matrix products, arithmetic and copies ran while one was open for 0% -> 0% of each run, Pallas kernels for 27% -> 28%
where the time goes in v6:
time: 91.9 us; the launch traced here: 91.7 us
  starting transfers between devices  33.2 us (36%)
  waiting for transfers between devices  28.9 us (31%)
  Pallas kernels  28.4 us (31%)
  between operations  1.08 us (1%)
    ppermute x33, starting transfers between devices, send(): return lax.ppermute(array, ('head', 'frame'), pairs)  33.2 us
    ppermute x33, waiting for transfers between devices, send(): return lax.ppermute(array, ('head', 'frame'), pairs)  28.9 us
    pallas_call x4, Pallas kernels, attend(): pl.pallas_call(functools.partial(attend_body, plan, first, heads, split),...  18.3 us
    pallas_call x5, Pallas kernels, place(): pl.pallas_call(body, out_shape=out, in_specs=[VMEM] * len(pieces) + [HBM]...  4.64 us
    pallas_call x2, Pallas kernels, pack_columns(): pl.pallas_call(body, out_shape=out, in_specs=[HBM] * 4, out_specs=[VMEM]...  3.96 us
  transfers between devices with their start and end apart: 33, of which 13 were waited for; matrix products, arithmetic and copies ran while one was open for 0% of the time, Pallas kernels for 28%

profile of v6, /device:TPU:0, one launch (start us, length us, event | category | flops | bytes accessed | tf_op | source)
XLA Modules:
  0.0 91.7 jit_solution(483688144042087846)
XLA Ops:
  0.6 2.0 %pack_columns.2 = (bf16[4,4,64,256]{3,2,1,0:T(8,128)(2,1)S(1)}, bf16[4,4,64,128]{3,2,1,0:T(8,128)(2,1)S(1)}, bf16[4,4,64,256]{3,2,1,0:T(8,128)(2,1)S(1)}, bf16[4...) custom-call(bf16[64,5120]{1,0:T(8,128)(2,1)} %refs_0_.6, bf16[64,5120]{1,0:T(8,128)(2,1)} %refs_1_.2, ...), custom_call_target="tpu_custom_call" | custom-call | flops 1024 | bytes 1024 | tf_op jit(solution)/shard_map/pack_columns/pallas_call | solution.py:111
  2.6 3.0 %collective-permute-start.4 = (bf16[4,4,64,256]{3,2,1,0:T(8,128)(2,1)S(1)}, bf16[4,4,64,256]{3,2,1,0:T(8,128)(2,1)S(1)}, u32[]{:S(2)}, u32[]{:S(2)}) collective-permute-start(bf16[4,4,64,256]{3,2,1,0:T(8,128)(2,1)S(1)} %get-tuple-element.150), channel_id=1, source_target_pairs={{0,2},{1,3},{2,0},{3,1},{4,6},{5,7},{6,4},{7,5},{8,10},{9,11},{10,... | collective-permute-start | bytes 1572872 | tf_op jit(solution)/shard_map/ppermute | solution.py:68
  5.7 3.7 %collective-permute-start = (bf16[1,4,64,256]{3,2,1,0:T(8,128)(2,1)S(1)}, bf16[1,4,64,256]{3,2,1,0:T(8,128)(2,1)S(1)}, u32[]{:S(2)}, u32[]{:S(2)}) collective-permute-start(bf16[1,4,64,256]{3,2,1,0:T(8,128)(2,1)S(1)} %get-tuple-element.146), channel_id=1, source_target_pairs={{0,12},{1,13},{2,14},{3,15},{4,8},{5,9},{6,10},{7,11},{8,4},{9,5},... | collective-permute-start | bytes 393224 | tf_op jit(solution)/shard_map/ppermute | solution.py:68
  10.5 7.9 %collective-permute-done.4.refs_0_ = bf16[4,4,64,256]{3,2,1,0:T(8,128)(2,1)S(1)} collective-permute-done((bf16[4,4,64,256]{3,2,1,0:T(8,128)(2,1)S(1)}, bf16[4,4,64,256]{3,2,1,0:T(8,128)(2,1)S(1)}, u32[]{:S(2)}, u32[]{:S(2)}) %collective-permute-start.4) | collective-permute-done | bytes 524320 | tf_op jit(solution)/shard_map/ppermute | solution.py:68
  18.5 1.7 %collective-permute-done.1.refs_2_ = bf16[1,4,64,256]{3,2,1,0:T(8,128)(2,1)S(1)} collective-permute-done((bf16[1,4,64,256]{3,2,1,0:T(8,128)(2,1)S(1)}, bf16[1,4,64,256]{3,2,1,0:T(8,128)(2,1)S(1)}, u32[]{:S(2)}, u32[]{:S(2)}) %collective-permute-start.1) | collective-permute-done | bytes 131104 | tf_op jit(solution)/shard_map/ppermute | solution.py:68
  20.2 1.5 %collective-permute-start.7 = (bf16[1,4,64,256]{3,2,1,0:T(8,128)(2,1)S(1)}, bf16[1,4,64,256]{3,2,1,0:T(8,128)(2,1)S(1)}, u32[]{:S(2)}, u32[]{:S(2)}) collective-permute-start(bf16[1,4,64,256]{3,2,1,0:T(8,128)(2,1)S(1)} %get-tuple-element.165), channel_id=1, source_target_pairs={{0,8},{1,9},{2,10},{3,11},{4,12},{5,13},{6,14},{7,15},{8,0},{9,1},... | collective-permute-start | bytes 393224 | tf_op jit(solution)/shard_map/ppermute | solution.py:68
  21.7 1.3 %collective-permute-start.6 = (bf16[1,4,64,256]{3,2,1,0:T(8,128)(2,1)S(1)}, bf16[1,4,64,256]{3,2,1,0:T(8,128)(2,1)S(1)}, u32[]{:S(2)}, u32[]{:S(2)}) collective-permute-start(bf16[1,4,64,256]{3,2,1,0:T(8,128)(2,1)S(1)} %get-tuple-element.164), channel_id=1, source_target_pairs={{0,12},{1,13},{2,14},{3,15},{4,8},{5,9},{6,10},{7,11},{8,4},{9,5},... | collective-permute-start | bytes 393224 | tf_op jit(solution)/shard_map/ppermute | solution.py:68
  24.4 6.4 %collective-permute-done.7.refs_7_ = bf16[1,4,64,256]{3,2,1,0:T(8,128)(2,1)S(1)} collective-permute-done((bf16[1,4,64,256]{3,2,1,0:T(8,128)(2,1)S(1)}, bf16[1,4,64,256]{3,2,1,0:T(8,128)(2,1)S(1)}, u32[]{:S(2)}, u32[]{:S(2)}) %collective-permute-start.7) | collective-permute-done | bytes 131104 | tf_op jit(solution)/shard_map/ppermute | solution.py:68
  33.0 3.0 %collective-permute-start.12 = (bf16[2,4,64,128]{3,2,1,0:T(8,128)(2,1)}, bf16[2,4,64,128]{3,2,1,0:T(8,128)(2,1)S(1)}, u32[]{:S(2)}, u32[]{:S(2)}) collective-permute-start(bf16[2,4,64,128]{3,2,1,0:T(8,128)(2,1)} %get-tuple-element.182), channel_id=1, source_target_pairs={{0,8},{1,9},{2,10},{3,11},{4,12},{5,13},{6,14},{7,15},{8,0},{9,1},... | collective-permute-start | bytes 393224 | tf_op jit(solution)/shard_map/ppermute | solution.py:68
  36.0 1.3 %collective-permute-start.11 = (bf16[2,4,64,128]{3,2,1,0:T(8,128)(2,1)S(1)}, bf16[2,4,64,128]{3,2,1,0:T(8,128)(2,1)S(1)}, u32[]{:S(2)}, u32[]{:S(2)}) collective-permute-start(bf16[2,4,64,128]{3,2,1,0:T(8,128)(2,1)S(1)} %get-tuple-element.181), channel_id=1, source_target_pairs={{0,12},{1,13},{2,14},{3,15},{4,8},{5,9},{6,10},{7,11},{8,4},{9,5},... | collective-permute-start | bytes 393224 | tf_op jit(solution)/shard_map/ppermute | solution.py:68
  37.5 6.8 %attend.4 = (bf16[2,256,256]{2,1,0:T(8,128)(2,1)S(1)}, bf16[2,256,256]{2,1,0:T(8,128)(2,1)S(1)}, f32[2,512,256]{2,1,0:T(8,128)S(1)}, bf16[2,512,256]{2,1,0:T(8,128)(2,1)S(1)}) custom-call(s32[10,8,8]{2,1,0:T(8,128)S(1)} %copy.28.refs_0_, bf16[2,512,256]{2,1,0:T(8,128)(2,1)S(1)} %get-tuple-element.166.refs_1_, ...), custom_call_target="tpu_custom_call" | custom-call | flops 1024 | bytes 1024 | tf_op jit(solution)/shard_map/attend/pallas_call | solution.py:246
  44.4 2.0 %pack_columns.3 = (bf16[4,4,64,128]{3,2,1,0:T(8,128)(2,1)S(1)}, bf16[4,4,64,128]{3,2,1,0:T(8,128)(2,1)S(1)}) custom-call(bf16[64,5120]{1,0:T(8,128)(2,1)} %refs_0_.6, bf16[64,5120]{1,0:T(8,128)(2,1)} %refs_1_.2, bf16[64,5120]{1,0:T(8,128)(2,1)} %refs_2_.2, bf16[64,5120]{1,0:T(8,128)(2,1)} %refs_3_.2), custom_call_target="tpu_custom_call" | custom-call | flops 1024 | bytes 1024 | tf_op jit(solution)/shard_map/pack_columns/pallas_call | solution.py:111
  47.8 2.8 %collective-permute-start.15 = (bf16[2,4,64,128]{3,2,1,0:T(8,128)(2,1)S(1)}, bf16[2,4,64,128]{3,2,1,0:T(8,128)(2,1)S(1)}, u32[]{:S(2)}, u32[]{:S(2)}) collective-permute-start(bf16[2,4,64,128]{3,2,1,0:T(8,128)(2,1)S(1)} %get-tuple-element.196), channel_id=1, source_target_pairs={{0,8},{1,9},{2,10},{3,11},{4,12},{5,13},{6,14},{7,15},{8,0},{9,1},... | collective-permute-start | bytes 393224 | tf_op jit(solution)/shard_map/ppermute | solution.py:68
  50.7 1.8 %collective-permute-start.14 = (bf16[2,4,64,128]{3,2,1,0:T(8,128)(2,1)S(1)}, bf16[2,4,64,128]{3,2,1,0:T(8,128)(2,1)S(1)}, u32[]{:S(2)}, u32[]{:S(2)}) collective-permute-start(bf16[2,4,64,128]{3,2,1,0:T(8,128)(2,1)S(1)} %get-tuple-element.194), channel_id=1, source_target_pairs={{0,12},{1,13},{2,14},{3,15},{4,8},{5,9},{6,10},{7,11},{8,4},{9,5},... | collective-permute-start | bytes 393224 | tf_op jit(solution)/shard_map/ppermute | solution.py:68
  52.4 3.9 %attend.5 = (bf16[2,256,128]{2,1,0:T(8,128)(2,1)S(1)}, bf16[2,256,128]{2,1,0:T(8,128)(2,1)S(1)}, f32[2,512,128]{2,1,0:T(8,128)S(1)}, bf16[2,512,128]{2,1,0:T(8,128)(2,1)S(1)}) custom-call(s32[10,8,8]{2,1,0:T(8,128)S(1)} %copy.28.refs_0_, bf16[2,512,128]{2,1,0:T(8,128)(2,1)S(1)} %get-tuple-element.203.refs_1_, ...), custom_call_target="tpu_custom_call" | custom-call | flops 1024 | bytes 1024 | tf_op jit(solution)/shard_map/attend/pallas_call | solution.py:246
  56.4 4.4 %collective-permute-done.15.refs_3_ = bf16[2,4,64,128]{3,2,1,0:T(8,128)(2,1)S(1)} collective-permute-done((bf16[2,4,64,128]{3,2,1,0:T(8,128)(2,1)S(1)}, bf16[2,4,64,128]{3,2,1,0:T(8,128)(2,1)S(1)}, u32[]{:S(2)}, u32[]{:S(2)}) %collective-permute-start.15) | collective-permute-done | bytes 131104 | tf_op jit(solution)/shard_map/ppermute | solution.py:68
  62.0 2.7 %collective-permute-start.20 = (bf16[2,4,64,128]{3,2,1,0:T(8,128)(2,1)S(1)}, bf16[2,4,64,128]{3,2,1,0:T(8,128)(2,1)S(1)}, u32[]{:S(2)}, u32[]{:S(2)}) collective-permute-start(bf16[2,4,64,128]{3,2,1,0:T(8,128)(2,1)S(1)} %get-tuple-element.218), channel_id=1, source_target_pairs={{0,8},{1,9},{2,10},{3,11},{4,12},{5,13},{6,14},{7,15},{8,0},{9,1},... | collective-permute-start | bytes 393224 | tf_op jit(solution)/shard_map/ppermute | solution.py:68
  64.7 1.8 %collective-permute-start.19 = (bf16[2,4,64,128]{3,2,1,0:T(8,128)(2,1)S(1)}, bf16[2,4,64,128]{3,2,1,0:T(8,128)(2,1)S(1)}, u32[]{:S(2)}, u32[]{:S(2)}) collective-permute-start(bf16[2,4,64,128]{3,2,1,0:T(8,128)(2,1)S(1)} %get-tuple-element.216), channel_id=1, source_target_pairs={{0,12},{1,13},{2,14},{3,15},{4,8},{5,9},{6,10},{7,11},{8,4},{9,5},... | collective-permute-start | bytes 393224 | tf_op jit(solution)/shard_map/ppermute | solution.py:68
  66.5 1.5 %collective-permute-start.24 = (bf16[2,256,128]{2,1,0:T(8,128)(2,1)S(1)}, bf16[2,256,128]{2,1,0:T(8,128)(2,1)S(1)}, u32[]{:S(2)}, u32[]{:S(2)}) collective-permute-start(bf16[2,256,128]{2,1,0:T(8,128)(2,1)S(1)} %get-tuple-element.235), channel_id=1, source_target_pairs={{0,2},{1,3},{2,0},{3,1},{4,6},{5,7},{6,4},{7,5},{8,10},{9,11},{10,... | collective-permute-start | bytes 393224 | tf_op jit(solution)/shard_map/ppermute | solution.py:68
  68.8 3.8 %attend.6 = (bf16[2,256,128]{2,1,0:T(8,128)(2,1)S(1)}, bf16[2,256,128]{2,1,0:T(8,128)(2,1)S(1)}, f32[2,512,128]{2,1,0:T(8,128)S(1)}, bf16[2,512,128]{2,1,0:T(8,128)(2,1)S(1)}) custom-call(s32[10,8,8]{2,1,0:T(8,128)S(1)} %copy.28.refs_0_, bf16[2,512,128]{2,1,0:T(8,128)(2,1)S(1)} %get-tuple-element.225.refs_1_, ...), custom_call_target="tpu_custom_call" | custom-call | flops 1024 | bytes 1024 | tf_op jit(solution)/shard_map/attend/pallas_call | solution.py:246
  73.7 1.2 %collective-permute-done.20.refs_3_ = bf16[2,4,64,128]{3,2,1,0:T(8,128)(2,1)S(1)} collective-permute-done((bf16[2,4,64,128]{3,2,1,0:T(8,128)(2,1)S(1)}, bf16[2,4,64,128]{3,2,1,0:T(8,128)(2,1)S(1)}, u32[]{:S(2)}, u32[]{:S(2)}) %collective-permute-start.20) | collective-permute-done | bytes 131104 | tf_op jit(solution)/shard_map/ppermute | solution.py:68
  76.5 1.5 %collective-permute-start.31 = (bf16[4,256,128]{2,1,0:T(8,128)(2,1)S(1)}, bf16[4,256,128]{2,1,0:T(8,128)(2,1)S(1)}, u32[]{:S(2)}, u32[]{:S(2)}) collective-permute-start(bf16[4,256,128]{2,1,0:T(8,128)(2,1)S(1)} %get-tuple-element.262), channel_id=1, source_target_pairs={{0,2},{1,3},{2,0},{3,1},{4,6},{5,7},{6,4},{7,5},{8,10},{9,11},{10,... | collective-permute-start | bytes 786440 | tf_op jit(solution)/shard_map/ppermute | solution.py:68
  78.0 3.8 %attend.7 = (bf16[2,256,128]{2,1,0:T(8,128)(2,1)S(1)}, bf16[2,256,128]{2,1,0:T(8,128)(2,1)S(1)}, f32[2,512,128]{2,1,0:T(8,128)S(1)}, bf16[512,128]{1,0:T(8,128)(2,1)S(1)}, bf16[512,128]{1,0:T(8,128)(2,1)S(1)}) custom-call(s32[10,8,8]{2,1,0:T(8,128)S(1)} %copy.28.refs_0_, bf16[2,512,128]{2,1,0:T(8,128)(2,1)S(1)} %get-tuple-element.244.refs_1_, ...), custom_call_target="tpu_custom_call" | custom-call | flops 1024 | bytes 1024 | tf_op jit(solution)/shard_map/attend/pallas_call | solution.py:246
  86.5 2.3 %collective-permute-done.32.refs_1_ = bf16[2,256,128]{2,1,0:T(8,128)(2,1)S(1)} collective-permute-done((bf16[2,256,128]{2,1,0:T(8,128)(2,1)S(1)}, bf16[2,256,128]{2,1,0:T(8,128)(2,1)S(1)}, u32[]{:S(2)}, u32[]{:S(2)}) %collective-permute-start.32) | collective-permute-done | bytes 131104 | tf_op jit(solution)/shard_map/ppermute | solution.py:68
  (71 shorter events, 18.4 us)
Async XLA Ops:
  2.6 15.8 %collective-permute-start.4 = (bf16[4,4,64,256]{3,2,1,0:T(8,128)(2,1)S(1)}, bf16[4,4,64,256]{3,2,1,0:T(8,128)(2,1)S(1)}, u32[]{:S(2)}, u32[]{:S(2)}) collective-permute-start(bf16[4,4,64,256]{3,2,1,0:T(8,128)(2,1)S(1)} %get-tuple-element.150), channel_id=1, source_target_pairs={{0,2},{1,3},{2,0},{3,1},{4,6},{5,7},{6,4},{7,5},{8,10},{9,11},{10,... | collective-permute-start | bytes 1572872 | tf_op jit(solution)/shard_map/ppermute | solution.py:68
  5.7 12.8 %collective-permute-start = (bf16[1,4,64,256]{3,2,1,0:T(8,128)(2,1)S(1)}, bf16[1,4,64,256]{3,2,1,0:T(8,128)(2,1)S(1)}, u32[]{:S(2)}, u32[]{:S(2)}) collective-permute-start(bf16[1,4,64,256]{3,2,1,0:T(8,128)(2,1)S(1)} %get-tuple-element.146), channel_id=1, source_target_pairs={{0,12},{1,13},{2,14},{3,15},{4,8},{5,9},{6,10},{7,11},{8,4},{9,5},... | collective-permute-start | bytes 393224 | tf_op jit(solution)/shard_map/ppermute | solution.py:68
  9.4 10.8 %collective-permute-start.1 = (bf16[1,4,64,256]{3,2,1,0:T(8,128)(2,1)S(1)}, bf16[1,4,64,256]{3,2,1,0:T(8,128)(2,1)S(1)}, u32[]{:S(2)}, u32[]{:S(2)}) collective-permute-start(bf16[1,4,64,256]{3,2,1,0:T(8,128)(2,1)S(1)} %get-tuple-element.147), channel_id=1, source_target_pairs={{0,8},{1,9},{2,10},{3,11},{4,12},{5,13},{6,14},{7,15},{8,0},{9,1},... | collective-permute-start | bytes 393224 | tf_op jit(solution)/shard_map/ppermute | solution.py:68
  9.4 14.3 %collective-permute-start.3 = (bf16[4,4,64,128]{3,2,1,0:T(8,128)(2,1)S(1)}, bf16[4,4,64,128]{3,2,1,0:T(8,128)(2,1)S(1)}, u32[]{:S(2)}, u32[]{:S(2)}) collective-permute-start(bf16[4,4,64,128]{3,2,1,0:T(8,128)(2,1)S(1)} %get-tuple-element.149), channel_id=1, source_target_pairs={{0,2},{1,3},{2,0},{3,1},{4,6},{5,7},{6,4},{7,5},{8,10},{9,11},{10,... | collective-permute-start | bytes 786440 | tf_op jit(solution)/shard_map/ppermute | solution.py:68
  9.9 10.3 %collective-permute-start.2 = (bf16[1,4,64,256]{3,2,1,0:T(8,128)(2,1)S(1)}, bf16[1,4,64,256]{3,2,1,0:T(8,128)(2,1)S(1)}, u32[]{:S(2)}, u32[]{:S(2)}) collective-permute-start(bf16[1,4,64,256]{3,2,1,0:T(8,128)(2,1)S(1)} %get-tuple-element.148), channel_id=1, source_target_pairs={{0,4},{1,5},{2,6},{3,7},{4,0},{5,1},{6,2},{7,3},{8,12},{9,13},{10,... | collective-permute-start | bytes 393224 | tf_op jit(solution)/shard_map/ppermute | solution.py:68
  20.2 10.6 %collective-permute-start.7 = (bf16[1,4,64,256]{3,2,1,0:T(8,128)(2,1)S(1)}, bf16[1,4,64,256]{3,2,1,0:T(8,128)(2,1)S(1)}, u32[]{:S(2)}, u32[]{:S(2)}) collective-permute-start(bf16[1,4,64,256]{3,2,1,0:T(8,128)(2,1)S(1)} %get-tuple-element.165), channel_id=1, source_target_pairs={{0,8},{1,9},{2,10},{3,11},{4,12},{5,13},{6,14},{7,15},{8,0},{9,1},... | collective-permute-start | bytes 393224 | tf_op jit(solution)/shard_map/ppermute | solution.py:68
  21.7 9.1 %collective-permute-start.6 = (bf16[1,4,64,256]{3,2,1,0:T(8,128)(2,1)S(1)}, bf16[1,4,64,256]{3,2,1,0:T(8,128)(2,1)S(1)}, u32[]{:S(2)}, u32[]{:S(2)}) collective-permute-start(bf16[1,4,64,256]{3,2,1,0:T(8,128)(2,1)S(1)} %get-tuple-element.164), channel_id=1, source_target_pairs={{0,12},{1,13},{2,14},{3,15},{4,8},{5,9},{6,10},{7,11},{8,4},{9,5},... | collective-permute-start | bytes 393224 | tf_op jit(solution)/shard_map/ppermute | solution.py:68
  23.0 8.6 %collective-permute-start.5 = (bf16[1,4,64,256]{3,2,1,0:T(8,128)(2,1)S(1)}, bf16[1,4,64,256]{3,2,1,0:T(8,128)(2,1)S(1)}, u32[]{:S(2)}, u32[]{:S(2)}) collective-permute-start(bf16[1,4,64,256]{3,2,1,0:T(8,128)(2,1)S(1)} %get-tuple-element.162), channel_id=1, source_target_pairs={{0,4},{1,5},{2,6},{3,7},{4,0},{5,1},{6,2},{7,3},{8,12},{9,13},{10,... | collective-permute-start | bytes 393224 | tf_op jit(solution)/shard_map/ppermute | solution.py:68
  31.8 15.0 %collective-permute-start.9 = (bf16[4,4,64,256]{3,2,1,0:T(8,128)(2,1)S(1)}, bf16[4,4,64,256]{3,2,1,0:T(8,128)(2,1)S(1)}, u32[]{:S(2)}, u32[]{:S(2)}) collective-permute-start(bf16[4,4,64,256]{3,2,1,0:T(8,128)(2,1)S(1)} %get-tuple-element.175), channel_id=1, source_target_pairs={{0,2},{1,3},{2,0},{3,1},{4,6},{5,7},{6,4},{7,5},{8,10},{9,11},{10,... | collective-permute-start | bytes 1572872 | tf_op jit(solution)/shard_map/ppermute | solution.py:68
  33.0 13.4 %collective-permute-start.12 = (bf16[2,4,64,128]{3,2,1,0:T(8,128)(2,1)}, bf16[2,4,64,128]{3,2,1,0:T(8,128)(2,1)S(1)}, u32[]{:S(2)}, u32[]{:S(2)}) collective-permute-start(bf16[2,4,64,128]{3,2,1,0:T(8,128)(2,1)} %get-tuple-element.182), channel_id=1, source_target_pairs={{0,8},{1,9},{2,10},{3,11},{4,12},{5,13},{6,14},{7,15},{8,0},{9,1},... | collective-permute-start | bytes 393224 | tf_op jit(solution)/shard_map/ppermute | solution.py:68
  36.0 10.3 %collective-permute-start.11 = (bf16[2,4,64,128]{3,2,1,0:T(8,128)(2,1)S(1)}, bf16[2,4,64,128]{3,2,1,0:T(8,128)(2,1)S(1)}, u32[]{:S(2)}, u32[]{:S(2)}) collective-permute-start(bf16[2,4,64,128]{3,2,1,0:T(8,128)(2,1)S(1)} %get-tuple-element.181), channel_id=1, source_target_pairs={{0,12},{1,13},{2,14},{3,15},{4,8},{5,9},{6,10},{7,11},{8,4},{9,5},... | collective-permute-start | bytes 393224 | tf_op jit(solution)/shard_map/ppermute | solution.py:68
  37.4 9.5 %collective-permute-start.10 = (bf16[2,4,64,128]{3,2,1,0:T(8,128)(2,1)S(1)}, bf16[2,4,64,128]{3,2,1,0:T(8,128)(2,1)S(1)}, u32[]{:S(2)}, u32[]{:S(2)}) collective-permute-start(bf16[2,4,64,128]{3,2,1,0:T(8,128)(2,1)S(1)} %get-tuple-element.179), channel_id=1, source_target_pairs={{0,4},{1,5},{2,6},{3,7},{4,0},{5,1},{6,2},{7,3},{8,12},{9,13},{10,... | collective-permute-start | bytes 393224 | tf_op jit(solution)/shard_map/ppermute | solution.py:68
  47.1 19.4 %collective-permute-start.21 = (bf16[4,256,256]{2,1,0:T(8,128)(2,1)S(1)}, bf16[4,256,256]{2,1,0:T(8,128)(2,1)S(1)}, u32[]{:S(2)}, u32[]{:S(2)}) collective-permute-start(bf16[4,256,256]{2,1,0:T(8,128)(2,1)S(1)} %get-tuple-element.202), channel_id=1, source_target_pairs={{0,2},{1,3},{2,0},{3,1},{4,6},{5,7},{6,4},{7,5},{8,10},{9,11},{10,... | collective-permute-start | bytes 1572872 | tf_op jit(solution)/shard_map/ppermute | solution.py:68
  47.8 12.9 %collective-permute-start.15 = (bf16[2,4,64,128]{3,2,1,0:T(8,128)(2,1)S(1)}, bf16[2,4,64,128]{3,2,1,0:T(8,128)(2,1)S(1)}, u32[]{:S(2)}, u32[]{:S(2)}) collective-permute-start(bf16[2,4,64,128]{3,2,1,0:T(8,128)(2,1)S(1)} %get-tuple-element.196), channel_id=1, source_target_pairs={{0,8},{1,9},{2,10},{3,11},{4,12},{5,13},{6,14},{7,15},{8,0},{9,1},... | collective-permute-start | bytes 393224 | tf_op jit(solution)/shard_map/ppermute | solution.py:68
  50.7 10.1 %collective-permute-start.14 = (bf16[2,4,64,128]{3,2,1,0:T(8,128)(2,1)S(1)}, bf16[2,4,64,128]{3,2,1,0:T(8,128)(2,1)S(1)}, u32[]{:S(2)}, u32[]{:S(2)}) collective-permute-start(bf16[2,4,64,128]{3,2,1,0:T(8,128)(2,1)S(1)} %get-tuple-element.194), channel_id=1, source_target_pairs={{0,12},{1,13},{2,14},{3,15},{4,8},{5,9},{6,10},{7,11},{8,4},{9,5},... | collective-permute-start | bytes 393224 | tf_op jit(solution)/shard_map/ppermute | solution.py:68
  52.4 9.4 %collective-permute-start.13 = (bf16[2,4,64,128]{3,2,1,0:T(8,128)(2,1)S(1)}, bf16[2,4,64,128]{3,2,1,0:T(8,128)(2,1)S(1)}, u32[]{:S(2)}, u32[]{:S(2)}) collective-permute-start(bf16[2,4,64,128]{3,2,1,0:T(8,128)(2,1)S(1)} %get-tuple-element.192), channel_id=1, source_target_pairs={{0,4},{1,5},{2,6},{3,7},{4,0},{5,1},{6,2},{7,3},{8,12},{9,13},{10,... | collective-permute-start | bytes 393224 | tf_op jit(solution)/shard_map/ppermute | solution.py:68
  56.3 10.3 %collective-permute-start.22 = (bf16[2,512,128]{2,1,0:T(8,128)(2,1)S(1)}, bf16[2,512,128]{2,1,0:T(8,128)(2,1)S(1)}, u32[]{:S(2)}, u32[]{:S(2)}) collective-permute-start(bf16[2,512,128]{2,1,0:T(8,128)(2,1)S(1)} %get-tuple-element.204), channel_id=1, source_target_pairs={{0,1},{1,0},{2,3},{3,2},{4,5},{5,4},{6,7},{7,6},{8,9},{9,8},{10,11... | collective-permute-start | bytes 786440 | tf_op jit(solution)/shard_map/ppermute | solution.py:68
  62.0 12.9 %collective-permute-start.20 = (bf16[2,4,64,128]{3,2,1,0:T(8,128)(2,1)S(1)}, bf16[2,4,64,128]{3,2,1,0:T(8,128)(2,1)S(1)}, u32[]{:S(2)}, u32[]{:S(2)}) collective-permute-start(bf16[2,4,64,128]{3,2,1,0:T(8,128)(2,1)S(1)} %get-tuple-element.218), channel_id=1, source_target_pairs={{0,8},{1,9},{2,10},{3,11},{4,12},{5,13},{6,14},{7,15},{8,0},{9,1},... | collective-permute-start | bytes 393224 | tf_op jit(solution)/shard_map/ppermute | solution.py:68
  64.7 10.3 %collective-permute-start.19 = (bf16[2,4,64,128]{3,2,1,0:T(8,128)(2,1)S(1)}, bf16[2,4,64,128]{3,2,1,0:T(8,128)(2,1)S(1)}, u32[]{:S(2)}, u32[]{:S(2)}) collective-permute-start(bf16[2,4,64,128]{3,2,1,0:T(8,128)(2,1)S(1)} %get-tuple-element.216), channel_id=1, source_target_pairs={{0,12},{1,13},{2,14},{3,15},{4,8},{5,9},{6,10},{7,11},{8,4},{9,5},... | collective-permute-start | bytes 393224 | tf_op jit(solution)/shard_map/ppermute | solution.py:68
  66.5 9.4 %collective-permute-start.18 = (bf16[2,4,64,128]{3,2,1,0:T(8,128)(2,1)S(1)}, bf16[2,4,64,128]{3,2,1,0:T(8,128)(2,1)S(1)}, u32[]{:S(2)}, u32[]{:S(2)}) collective-permute-start(bf16[2,4,64,128]{3,2,1,0:T(8,128)(2,1)S(1)} %get-tuple-element.214), channel_id=1, source_target_pairs={{0,4},{1,5},{2,6},{3,7},{4,0},{5,1},{6,2},{7,3},{8,12},{9,13},{10,... | collective-permute-start | bytes 393224 | tf_op jit(solution)/shard_map/ppermute | solution.py:68
  66.5 9.4 %collective-permute-start.24 = (bf16[2,256,128]{2,1,0:T(8,128)(2,1)S(1)}, bf16[2,256,128]{2,1,0:T(8,128)(2,1)S(1)}, u32[]{:S(2)}, u32[]{:S(2)}) collective-permute-start(bf16[2,256,128]{2,1,0:T(8,128)(2,1)S(1)} %get-tuple-element.235), channel_id=1, source_target_pairs={{0,2},{1,3},{2,0},{3,1},{4,6},{5,7},{6,4},{7,5},{8,10},{9,11},{10,... | collective-permute-start | bytes 393224 | tf_op jit(solution)/shard_map/ppermute | solution.py:68
  68.1 7.9 %collective-permute-start.25 = (bf16[2,256,128]{2,1,0:T(8,128)(2,1)S(1)}, bf16[2,256,128]{2,1,0:T(8,128)(2,1)S(1)}, u32[]{:S(2)}, u32[]{:S(2)}) collective-permute-start(bf16[2,256,128]{2,1,0:T(8,128)(2,1)S(1)} %get-tuple-element.224), channel_id=1, source_target_pairs={{0,2},{1,3},{2,0},{3,1},{4,6},{5,7},{6,4},{7,5},{8,10},{9,11},{10,... | collective-permute-start | bytes 393224 | tf_op jit(solution)/shard_map/ppermute | solution.py:68
  76.5 9.0 %collective-permute-start.31 = (bf16[4,256,128]{2,1,0:T(8,128)(2,1)S(1)}, bf16[4,256,128]{2,1,0:T(8,128)(2,1)S(1)}, u32[]{:S(2)}, u32[]{:S(2)}) collective-permute-start(bf16[4,256,128]{2,1,0:T(8,128)(2,1)S(1)} %get-tuple-element.262), channel_id=1, source_target_pairs={{0,2},{1,3},{2,0},{3,1},{4,6},{5,7},{6,4},{7,5},{8,10},{9,11},{10,... | collective-permute-start | bytes 786440 | tf_op jit(solution)/shard_map/ppermute | solution.py:68
  83.5 7.2 %collective-permute-start.30 = (bf16[2,256,128]{2,1,0:T(8,128)(2,1)S(1)}, bf16[2,256,128]{2,1,0:T(8,128)(2,1)S(1)}, u32[]{:S(2)}, u32[]{:S(2)}) collective-permute-start(bf16[2,256,128]{2,1,0:T(8,128)(2,1)S(1)} %get-tuple-element.250), channel_id=1, source_target_pairs={{0,2},{1,3},{2,0},{3,1},{4,6},{5,7},{6,4},{7,5},{8,10},{9,11},{10,... | collective-permute-start | bytes 393224 | tf_op jit(solution)/shard_map/ppermute | solution.py:68
  (10 other events, 38.1 us)
